TPU v7x, 128 devices: a whole 4x4x4 slice. The times are simulated.
128 devices in a mesh: ft: 8 (over y_lo, z), tp: 16 (over y_hi, x, core).
Axes of the slice: x: 4, y: 4 (y_hi: 2, y_lo: 2; y = y_hi * 2 + y_lo), z: 4, core: 2. Of those that a mesh axis runs over, the one named last changes fastest.
Arguments:
- token_rows: int32 [8, 512], P('ft'), may hold values from 0 to 1023
- gate_cache: bfloat16 [8, 1024, 14336], P('ft', None, 'tp'), may hold values from -6 to 6
- up_cache: bfloat16 [8, 1024, 14336], P('ft', None, 'tp'), may hold values from -6 to 6
- down_weight: bfloat16 [8, 14336, 8192], P('ft', 'tp'), may hold values from -3 to 3
- targets: bfloat16 [8, 512, 8192], P('ft'), may hold values from -6 to 6
Outputs:
- merged: float32 [14336, 8192], P('tp', 'ft')
Inputs may be any that keep to these rules, and one draw needn't show every extreme that they name: `token_rows`: each id is a row of that fine-adjust's cache.
All inputs are finite; a program needn't handle non-finite values.
Results may differ from a plain program's by a relative error of at most 0.024.
Values may be sent and summed in bfloat16 or wider, within the bound.
No kernel may reach another device: no remote copies, remote signals or barrier semaphores. Data moves between devices by JAX's collectives and lax.ppermute only.
A program may use at most 320 MiB of HBM per device.

v0:
```python
import math

import jax
import jax.numpy as jnp
from jax import lax
from jax.sharding import PartitionSpec as P

FF = 14336
TOK = 512


def body(token_rows, gate_cache, up_cache, down_weight, targets):
    shrink = 1.0 / math.sqrt(FF)
    picked = token_rows[0]
    gate_rows = jnp.take(gate_cache[0], picked, axis=0).astype(jnp.float32)
    up_rows = jnp.take(up_cache[0], picked, axis=0).astype(jnp.float32)
    hidden = (jax.nn.silu(gate_rows) * up_rows).astype(jnp.bfloat16)
    projection = down_weight[0]
    own_targets = targets[0]
    partial_out = jnp.dot(hidden, projection, preferred_element_type=jnp.float32) * shrink
    outputs = lax.psum(partial_out, "tp")
    errors = (outputs - own_targets.astype(jnp.float32)).astype(jnp.bfloat16)
    hidden_wide = hidden.astype(jnp.float32)
    errors_wide = errors.astype(jnp.float32)
    unit_squares = (hidden_wide * hidden_wide).astype(jnp.bfloat16)
    error_squares = (errors_wide * errors_wide).astype(jnp.bfloat16)
    fisher = (
        lax.dot_general(
            unit_squares,
            error_squares,
            (((0,), (0,)), ((), ())),
            preferred_element_type=jnp.float32,
        )
        / TOK
    )
    numerator, denominator = (
        lax.psum_scatter(
            (fisher * projection.astype(jnp.float32)).astype(jnp.bfloat16),
            "ft",
            scatter_dimension=1,
            tiled=True,
        ).astype(jnp.float32),
        lax.psum_scatter(fisher.astype(jnp.bfloat16), "ft", scatter_dimension=1, tiled=True).astype(
            jnp.float32
        ),
    )
    return numerator / (denominator + 1e-06)


def solution(mesh):
    placed = (
        P("ft", None),
        P("ft", None, "tp"),
        P("ft", None, "tp"),
        P("ft", "tp", None),
        P("ft", None, None),
    )
    return jax.shard_map(body, mesh=mesh, in_specs=placed, out_specs=P("tp", "ft"), check_vma=False)
```

profile of v0, /device:TPU:1, one launch (start us, length us, event | category | flops | bytes accessed | tf_op | source)
XLA Modules:
  0.0 576.2 jit_solution(6760921951232000639)
XLA Ops:
  6.5 0.0 copy-start
  6.5 0.0 all-reduce.2.cloned.1.call-start
  6.5 0.8 compare_and_fusion
  7.4 0.7 compare_select_fusion
  8.1 0.0 copy-done
  8.1 2.1 gather_fusion.1
  10.1 4.3 gather_fusion
  14.4 16.5 %fusion.3 = f32[512,8192]{1,0:T(8,128)} fusion(bf16[1,896,8192]{2,1,0:T(8,128)(2,1)} %param.10, bf16[512,896]{1,0:T(8,128)(2,1)S(1)} %gather_fusion.1, bf16[512,896]{1,0:T(8,128)(2,1)S(1)} %gather_fusion, pred[512]{0:T(512)(128)(4,1)S(1)} %compare_and_fusion), kind=kOutput, calls=%fused_computation.9 | convolution fusion | flops 7524974592 | bytes 33292800 | tf_op jit(solution)/shard_map/dot_general | solution.py:20
  30.9 0.0 all-reduce.2.cloned.1.call-update
  30.9 0.0 reduce-scatter.3.cloned.1.call-start
  31.0 201.5 %all-reduce.2.cloned.1.call-done = f32[512,8192]{1,0:T(8,128)} async-done(((f32[512,8192]{1,0:T(8,128)}), f32[512,8192]{1,0:T(8,128)}) %all-reduce.2.cloned.1.call-update) | async-done | bytes 16777232 | tf_op jit(solution)/shard_map/psum | solution.py:21
  232.5 25.2 %multiply_convert_fusion = (bf16[896,8192]{1,0:T(8,128)(2,1)}, bf16[896,8192]{1,0:T(8,128)(2,1)}) fusion(bf16[1,896,8192]{2,1,0:T(8,128)(2,1)} %param.10, f32[512,8192]{1,0:T(8,128)} %all-reduce.2.cloned.1.call-done, bf16[1,512,8192]{2,1,0:T(8,128)(2,1)} %param.11, bf16[512,896]{1,0:T(8,128)(2,1)S(1)} %gather_fusion.1, bf16[512,896]{1,0:T(8,128)(2,1)S(1)} %gather_fusion, ...), kind=kOutput, calls=%fused_computation.2 | convolution fusion | flops 7584022528 | bytes 71041536 | tf_op jit(solution)/shard_map/dot_general | solution.py:28
  257.7 0.0 reduce-scatter.3.cloned.1.call-update
  257.7 0.0 reduce-scatter.5.cloned.1.call-start
  257.7 0.7 reduce-scatter.5.cloned.1.call-update
  258.4 0.0 copy-start.1
  258.4 153.1 %reduce-scatter.3.cloned.1.call-done = bf16[896,1024]{1,0:T(8,128)(2,1)} async-done(((bf16[896,8192]{1,0:T(8,128)(2,1)}), bf16[896,1024]{1,0:T(8,128)(2,1)}) %reduce-scatter.3.cloned.1.call-update) | async-done | bytes 1835024 | tf_op jit(solution)/shard_map/reduce_scatter | solution.py:37
  411.6 153.4 %reduce-scatter.5.cloned.1.call-done = bf16[896,1024]{1,0:T(8,128)(2,1)} async-done(((bf16[896,8192]{1,0:T(8,128)(2,1)}), bf16[896,1024]{1,0:T(8,128)(2,1)}) %reduce-scatter.5.cloned.1.call-update) | async-done | bytes 1835024 | tf_op jit(solution)/shard_map/reduce_scatter | solution.py:43
  565.0 4.7 add_divide_fusion
  569.6 0.0 copy-done.1
  (1 shorter events, 0.0 us)
Async XLA Ops:
  6.5 1.5 copy-start
  6.5 226.0 %all-reduce.2.cloned.1.call-start = ((), (), s32[]{:S(2)}) async-start(), calls=%async_computation.2 | async-start | bytes 33554432 | tf_op jit(solution)/shard_map/psum | solution.py:21
  30.9 380.6 %reduce-scatter.3.cloned.1.call-start = ((), (), s32[]{:S(2)}) async-start(), calls=%async_computation.3 | async-start | bytes 16515072 | tf_op jit(solution)/shard_map/reduce_scatter | solution.py:37
  257.7 307.3 %reduce-scatter.5.cloned.1.call-start = ((), (), s32[]{:S(2)}) async-start(), calls=%async_computation.4 | async-start | bytes 16515072 | tf_op jit(solution)/shard_map/reduce_scatter | solution.py:43
  258.4 311.2 %copy-start.1 = (bf16[1,1024,896]{2,1,0:T(8,128)(2,1)S(1)}, bf16[1,1024,896]{2,1,0:T(8,128)(2,1)}, u32[]{:S(2)}) copy-start(bf16[1,1024,896]{2,1,0:T(8,128)(2,1)} %param.9) | copy-start | bytes 5505028
Sparse Core Ops, SparseCore 0:
  31.0 201.4 all-reduce.1
  257.8 153.7 reduce-scatter.2
  414.0 150.9 reduce-scatter.4
where the time goes:
time: 576 us
  waiting for transfers between devices  509 us (88%)
  matrix products  41.7 us (7%)
  between operations  13.1 us (2%)
  local copies, waits for them, and re-layouts  6.33 us (1%)
  other arithmetic  6.18 us (1%)
    psum x1, waiting for transfers between devices, body(): outputs = lax.psum(partial_out, 'tp')  202 us
    reduce_scatter x1, waiting for transfers between devices, body(): lax.psum_scatter(fisher.astype(jnp.bfloat16), 'ft', scatter_dimension=1,...  153 us
    reduce_scatter x1, waiting for transfers between devices, body(): lax.psum_scatter((fisher * projection.astype(jnp.float32)).astype(jnp.bfl...  153 us
    dot_general x1, matrix products, body(): lax.dot_general(unit_squares, error_squares, (((0,), (0,)), ((), ())), pr...  25.2 us
    dot_general x1, matrix products, body(): jnp.dot(hidden, projection, preferred_element_type=jnp.float32) * shrink  16.5 us
  transfers between devices with their start and end apart: 3, of which 3 were waited for; matrix products, arithmetic and copies ran while one was open for 0% of the time, Pallas kernels for 0%

commit v1 on v0

v1 whole, which is shorter than its diff:
```python
import math

import jax
import jax.numpy as jnp
from jax import lax
from jax.experimental import pallas as pl
from jax.experimental.pallas import tpu as pltpu
from jax.sharding import PartitionSpec as P

FF = 14336
TOK = 512
POOL = 1024
UNITS = 896
D = 8192
WIDE = 1024
SHRINK = 1.0 / math.sqrt(FF)


def ft_perm(dy, dz):
    return [(i, ((i // 4) ^ dy) * 4 + (i - dz) % 4) for i in range(8)]


def tp_perm(dh, dx, dc):
    out = []
    for i in range(16):
        h, x, c = i // 8, (i // 2) % 4, i % 2
        out.append((i, (h ^ dh) * 8 + ((x - dx) % 4) * 2 + (c ^ dc)))
    return out


def ft_send(value, dy, dz):
    return lax.ppermute(value, "ft", ft_perm(dy, dz))


def tp_send(value, dh, dx, dc):
    return lax.ppermute(value, "tp", tp_perm(dh, dx, dc))


def hidden_kernel(rows_ref, gate_ref, up_ref, hidden_ref, squares_ref):
    rows = rows_ref[...]
    pool = lax.broadcasted_iota(jnp.int32, (TOK, POOL), 1)
    pick = jnp.where(rows == pool, 1.0, 0.0).astype(jnp.bfloat16)
    gate = jnp.dot(pick, gate_ref[...], preferred_element_type=jnp.float32)
    up = jnp.dot(pick, up_ref[...], preferred_element_type=jnp.float32)
    hidden = (gate / (1.0 + jnp.exp(-gate)) * up).astype(jnp.bfloat16)
    hidden_ref[...] = hidden
    wide = hidden.astype(jnp.float32)
    squares_ref[...] = (wide * wide).T.astype(jnp.bfloat16)


def make_hidden(rows, gate, up):
    step = 128
    return pl.pallas_call(
        hidden_kernel,
        grid=(UNITS // step,),
        in_specs=[
            pl.BlockSpec((TOK, 1), lambda i: (0, 0)),
            pl.BlockSpec((POOL, step), lambda i: (0, i)),
            pl.BlockSpec((POOL, step), lambda i: (0, i)),
        ],
        out_specs=[
            pl.BlockSpec((TOK, step), lambda i: (0, i)),
            pl.BlockSpec((step, TOK), lambda i: (i, 0)),
        ],
        out_shape=[
            jax.ShapeDtypeStruct((TOK, UNITS), jnp.bfloat16),
            jax.ShapeDtypeStruct((UNITS, TOK), jnp.bfloat16),
        ],
        compiler_params=pltpu.CompilerParams(vmem_limit_bytes=32 * 2**20),
        cost_estimate=pl.CostEstimate(
            flops=4 * TOK * POOL * UNITS, bytes_accessed=6 * 2**20, transcendentals=TOK * UNITS
        ),
    )(rows, gate, up)


def merge_kernel(n_parts, *refs):
    units = refs[:8]
    weights = refs[8:16]
    parts = refs[16 : 16 + n_parts]
    out_ref = refs[16 + n_parts]
    numerator = None
    for member in range(8):
        squares = jnp.concatenate([part[member] for part in parts], axis=0)
        fisher = jnp.dot(units[member][...], squares, preferred_element_type=jnp.float32) * (1.0 / TOK)
        weighted = (fisher * weights[member][...].astype(jnp.float32)).astype(jnp.bfloat16).astype(jnp.float32)
        term = fisher.astype(jnp.bfloat16).astype(jnp.float32)
        if numerator is None:
            numerator, denominator = weighted, term
        else:
            numerator, denominator = numerator + weighted, denominator + term
    out_ref[...] = numerator / (denominator + 1e-06)


def merge(units, weights, parts):
    step = 256
    tall = 448
    n_parts = len(parts)
    return pl.pallas_call(
        lambda *refs: merge_kernel(n_parts, *refs),
        grid=(UNITS // tall, WIDE // step),
        in_specs=[pl.BlockSpec((tall, TOK), lambda u, i: (u, 0))] * 8
        + [pl.BlockSpec((tall, step), lambda u, i: (u, i))] * 8
        + [pl.BlockSpec((8, TOK // n_parts, step), lambda u, i: (0, 0, i))] * n_parts,
        out_specs=pl.BlockSpec((tall, step), lambda u, i: (u, i)),
        out_shape=jax.ShapeDtypeStruct((UNITS, WIDE), jnp.float32),
        compiler_params=pltpu.CompilerParams(vmem_limit_bytes=48 * 2**20),
        cost_estimate=pl.CostEstimate(
            flops=2 * 8 * TOK * UNITS * WIDE, bytes_accessed=40 * 2**20, transcendentals=0
        ),
    )(*units, *weights, *parts)


def body(token_rows, gate_cache, up_cache, down_weight, targets):
    ft, tp = lax.axis_index("ft"), lax.axis_index("tp")
    y, z = ft // 4, ft % 4
    h, x, core = tp // 8, (tp // 2) % 4, tp % 2
    projection = down_weight[0]

    weights = {}
    for dy, dz in ((1, 0), (0, 2), (1, 2), (0, 1), (0, 3), (1, 1), (1, 3), (0, 0)):
        place = (y ^ dy) * 4 + (z - dz) % 4
        piece = lax.dynamic_slice(projection, (0, place * WIDE), (UNITS, WIDE))
        weights[dy, dz] = ft_send(piece, dy, dz) if (dy, dz) != (0, 0) else piece

    picked = token_rows[0].reshape(2, 4, 2, 32)
    picked = jnp.where(core == 1, picked[::-1], picked)
    picked = lax.dynamic_slice(jnp.concatenate([picked, picked], axis=1), (0, x, 0, 0), (2, 4, 2, 32))
    picked = jnp.where(h == 1, picked[:, :, ::-1], picked).reshape(TOK, 1)
    hidden, squares = make_hidden(picked, gate_cache[0], up_cache[0])

    units = {(0, 0): squares}
    units[1, 0] = ft_send(squares, 1, 0)
    for dz in (1, 3):
        for dy in (0, 1):
            units[dy, dz] = ft_send(units[dy, 0], 0, dz)
    units[0, 2] = ft_send(units[0, 1], 0, 1)
    units[1, 2] = ft_send(units[1, 3], 0, 3)

    def partial(rows):
        return (jnp.dot(rows, projection, preferred_element_type=jnp.float32) * SHRINK).astype(jnp.bfloat16)

    other = tp_send(partial(hidden[256:]), 0, 0, 1)
    own = partial(hidden[:256])
    pair = (own.astype(jnp.float32) + other.astype(jnp.float32)).astype(jnp.bfloat16)
    total = pair[:64].astype(jnp.float32)
    for dx in (1, 2, 3):
        total = total + tp_send(pair[64 * dx : 64 * dx + 64], 0, -dx, 0).astype(jnp.float32)
    far = tp_send(total[32:].astype(jnp.bfloat16), 1, 0, 0)
    outputs = total[:32] + far.astype(jnp.float32)

    first = (core * 8 + x * 2 + h) * 32
    own_targets = lax.dynamic_slice(targets[0], (first, 0), (32, D)).astype(jnp.float32)
    errors = (outputs - own_targets).astype(jnp.bfloat16).astype(jnp.float32)
    error_squares = (errors * errors).astype(jnp.bfloat16)

    order = [(dy, dz) for dy in (0, 1) for dz in (0, 1, 2, 3)]
    pieces = []
    for dy, dz in order:
        place = (y ^ dy) * 4 + (z - dz) % 4
        piece = lax.dynamic_slice(error_squares, (0, place * WIDE), (32, WIDE))
        pieces.append(ft_send(piece, dy, dz) if (dy, dz) != (0, 0) else piece)
    mine = jnp.stack(pieces)
    mine = jnp.concatenate([mine, tp_send(mine, 1, 0, 0)], axis=1)
    row = [mine] + [tp_send(mine, 0, dx, 0) for dx in (1, 2, 3)]
    parts = row + [tp_send(part, 0, 0, 1) for part in row]

    return merge([units[o] for o in order], [weights[o] for o in order], parts)


def solution(mesh):
    placed = (
        P("ft", None),
        P("ft", None, "tp"),
        P("ft", None, "tp"),
        P("ft", "tp", None),
        P("ft", None, None),
    )
    return jax.shard_map(body, mesh=mesh, in_specs=placed, out_specs=P("tp", "ft"), check_vma=False)
```

time: 576 us -> 422 us (0.73)
  waiting for transfers between devices: 509 us -> 282 us
  starting transfers between devices: 0.09 us -> 68.3 us
  Pallas kernels: 0 us -> 25.2 us
  matrix products: 41.7 us -> 19.7 us
  local copies, waits for them, and re-layouts: 6.33 us -> 21.5 us
  between operations: 13.1 us -> 0.52 us
    reduce_scatter x2 -> x0, waiting for transfers between devices: 307 us -> none  [the longest x1 153 us: body(): lax.psum_scatter(fisher.astype(jnp.bfloat16), 'ft', scatter_dimension=1,...]
    ppermute x0 -> x34, waiting for transfers between devices: none -> 282 us  [the longest x13 148 us: tp_send(): return lax.ppermute(value, 'tp', tp_perm(dh, dx, dc))]
    psum x1 -> x0, waiting for transfers between devices: 202 us -> none  [body(): outputs = lax.psum(partial_out, 'tp')]
    ppermute x0 -> x34, starting transfers between devices: none -> 68.3 us  [the longest x13 42.8 us: tp_send(): return lax.ppermute(value, 'tp', tp_perm(dh, dx, dc))]
    pallas_call x0 -> x2, Pallas kernels: none -> 25.2 us  [the longest x1 18.5 us: merge(): pl.pallas_call(lambda *refs: merge_kernel(n_parts, *refs), grid=(UNITS //...]
    dot_general x2, matrix products: 41.7 us -> 19.7 us  [partial(): jnp.dot(rows, projection, preferred_element_type=jnp.float32) * SHRINK]
    dynamic_slice x0 -> x2, local copies, waits for them, and re-layouts: none -> 11.1 us  [the longest x1 11 us: body(): piece = lax.dynamic_slice(projection, (0, place * WIDE), (UNITS, WIDE))]
    unnamed x4 -> x58, local copies, waits for them, and re-layouts: 0.01 us -> 7.03 us
  transfers between devices with their start and end apart: 3 -> 34, of which waited for: 3 -> 14; matrix products, arithmetic and copies ran while one was open for 0% -> 4% of each run, Pallas kernels for 0% -> 0%
where the time goes in v1:
time: 422 us
  waiting for transfers between devices  282 us (67%)
  starting transfers between devices  68.3 us (16%)
  Pallas kernels  25.2 us (6%)
  local copies, waits for them, and re-layouts  21.5 us (5%)
  matrix products  19.7 us (5%)
  other arithmetic  4.88 us (1%)
    ppermute x13, waiting for transfers between devices, tp_send(): return lax.ppermute(value, 'tp', tp_perm(dh, dx, dc))  148 us
    ppermute x21, waiting for transfers between devices, ft_send(): return lax.ppermute(value, 'ft', ft_perm(dy, dz))  134 us
    ppermute x13, starting transfers between devices, tp_send(): return lax.ppermute(value, 'tp', tp_perm(dh, dx, dc))  42.8 us
    ppermute x21, starting transfers between devices, ft_send(): return lax.ppermute(value, 'ft', ft_perm(dy, dz))  25.5 us
    dot_general x2, matrix products, partial(): jnp.dot(rows, projection, preferred_element_type=jnp.float32) * SHRINK  19.7 us
    pallas_call x1, Pallas kernels, merge(): pl.pallas_call(lambda *refs: merge_kernel(n_parts, *refs), grid=(UNITS //...  18.5 us
    dynamic_slice x1, local copies, waits for them, and re-layouts, body(): piece = lax.dynamic_slice(projection, (0, place * WIDE), (UNITS, WIDE))  11 us
  transfers between devices with their start and end apart: 34, of which 14 were waited for; matrix products, arithmetic and copies ran while one was open for 4% of the time, Pallas kernels for 0%

profile of v1, /device:TPU:1, one launch (start us, length us, event | category | flops | bytes accessed | tf_op | source)
XLA Modules:
  0.0 421.8 jit_solution(10656763072425435965)
XLA Ops:
  5.3 6.7 %shard_map.55 = (bf16[512,896]{1,0:T(8,128)(2,1)S(1)}, bf16[896,512]{1,0:T(8,128)(2,1)S(1)}) custom-call(s32[512,1]{1,0:T(8,128)S(1)} %reshape.16.rows_ref, bf16[1024,896]{1,0:T(8,128)(2,1)S(1)} %bitcast.54, bf16[1024,896]{1,0:T(8,128)(2,1)S(1)} %bitcast.55), custom_call_target="tpu_custom_call" | custom-call | flops 1879048192 | bytes 6291456 | tf_op jit(solution)/shard_map/pallas_call | solution.py:53
  12.0 11.5 %fusion.10 = bf16[256,8192]{1,0:T(8,128)(2,1)} fusion(bf16[1,896,8192]{2,1,0:T(8,128)(2,1)} %param.8, bf16[512,896]{1,0:T(8,128)(2,1)S(1)} %get-tuple-element.8), kind=kOutput, calls=%fused_computation.6 | convolution fusion | flops 3762290688 | bytes 19333120 | tf_op jit(solution)/shard_map/dot_general | solution.py:140
  24.9 7.1 %collective-permute-done.14 = bf16[256,8192]{1,0:T(8,128)(2,1)} collective-permute-done((bf16[256,8192]{1,0:T(8,128)(2,1)}, bf16[256,8192]{1,0:T(8,128)(2,1)}, u32[]{:S(2)}, u32[]{:S(2)}) %collective-permute-start.14) | collective-permute-done | bytes 4194336 | tf_op jit(solution)/shard_map/ppermute | solution.py:36
  32.0 8.2 %add_convert_fusion = bf16[256,8192]{1,0:T(8,128)(2,1)} fusion(bf16[256,8192]{1,0:T(8,128)(2,1)} %collective-permute-done.14, bf16[1,896,8192]{2,1,0:T(8,128)(2,1)S(1)} %bitcast.57, bf16[512,896]{1,0:T(8,128)(2,1)S(1)} %get-tuple-element.8), kind=kOutput, calls=%fused_computation.9 | convolution fusion | flops 3770679296 | bytes 23527424 | tf_op jit(solution)/shard_map/dot_general | solution.py:140
  40.3 2.1 fusion.26
  48.1 3.8 collective-permute-start
  51.9 16.2 %collective-permute-done.15 = bf16[64,8192]{1,0:T(8,128)(2,1)S(1)} collective-permute-done((bf16[64,8192]{1,0:T(8,128)(2,1)S(1)}, bf16[64,8192]{1,0:T(8,128)(2,1)S(1)}, u32[]{:S(2)}, u32[]{:S(2)}) %collective-permute-start.15) | collective-permute-done | bytes 1048608 | tf_op jit(solution)/shard_map/ppermute | solution.py:36
  68.1 23.5 %collective-permute-done.16 = bf16[64,8192]{1,0:T(8,128)(2,1)S(1)} collective-permute-done((bf16[64,8192]{1,0:T(8,128)(2,1)S(1)}, bf16[64,8192]{1,0:T(8,128)(2,1)S(1)}, u32[]{:S(2)}, u32[]{:S(2)}) %collective-permute-start.16) | collective-permute-done | bytes 1048608 | tf_op jit(solution)/shard_map/ppermute | solution.py:36
  94.8 2.9 collective-permute-start.18
  99.4 11.0 %dynamic-slice_bitcast_fusion = (bf16[896,1024]{1,0:T(8,128)(2,1)}, bf16[896,1024]{1,0:T(8,128)(2,1)}, bf16[896,1024]{1,0:T(8,128)(2,1)}, bf16[896,1024]{1,0:T(8...) fusion(bf16[1,896,8192]{2,1,0:T(8,128)(2,1)} %param.8, ...), kind=kLoop, calls=%fused_computation.11 | loop fusion | bytes 29360160 | tf_op jit(solution)/shard_map/dynamic_slice | solution.py:122
  116.7 43.3 %collective-permute-done.2.refs_3_ = bf16[896,512]{1,0:T(8,128)(2,1)} collective-permute-done((bf16[896,512]{1,0:T(8,128)(2,1)S(1)}, bf16[896,512]{1,0:T(8,128)(2,1)}, u32[]{:S(2)}, u32[]{:S(2)}) %collective-permute-start.2) | collective-permute-done | bytes 917536 | tf_op jit(solution)/shard_map/ppermute | solution.py:32
  161.2 18.4 %collective-permute-done.5.refs_7_ = bf16[896,512]{1,0:T(8,128)(2,1)S(1)} collective-permute-done((bf16[896,512]{1,0:T(8,128)(2,1)S(1)}, bf16[896,512]{1,0:T(8,128)(2,1)S(1)}, u32[]{:S(2)}, u32[]{:S(2)}) %collective-permute-start.5) | collective-permute-done | bytes 917536 | tf_op jit(solution)/shard_map/ppermute | solution.py:32
  180.8 1.9 collective-permute-start.20
  182.7 42.9 %collective-permute-done.20 = bf16[32,1024]{1,0:T(8,128)(2,1)S(1)} collective-permute-done((bf16[32,1024]{1,0:T(8,128)(2,1)S(1)}, bf16[32,1024]{1,0:T(8,128)(2,1)S(1)}, u32[]{:S(2)}, u32[]{:S(2)}) %collective-permute-start.20) | collective-permute-done | bytes 65568 | tf_op jit(solution)/shard_map/ppermute | solution.py:32
  225.6 4.3 %collective-permute-done.21 = bf16[32,1024]{1,0:T(8,128)(2,1)S(1)} collective-permute-done((bf16[32,1024]{1,0:T(8,128)(2,1)S(1)}, bf16[32,1024]{1,0:T(8,128)(2,1)S(1)}, u32[]{:S(2)}, u32[]{:S(2)}) %collective-permute-start.21) | collective-permute-done | bytes 65568 | tf_op jit(solution)/shard_map/ppermute | solution.py:32
  230.4 1.9 collective-permute-start.24
  234.0 1.9 collective-permute-done.25
  239.2 2.6 collective-permute-start.8
  241.9 85.0 %collective-permute-done.26 = bf16[8,32,1024]{2,1,0:T(8,128)(2,1)S(1)} collective-permute-done((bf16[8,32,1024]{2,1,0:T(8,128)(2,1)S(1)}, bf16[8,32,1024]{2,1,0:T(8,128)(2,1)S(1)}, u32[]{:S(2)}, u32[]{:S(2)}) %collective-permute-start.26) | collective-permute-done | bytes 524320 | tf_op jit(solution)/shard_map/ppermute | solution.py:36
  329.9 4.3 %collective-permute-start.30 = (bf16[8,64,1024]{2,1,0:T(8,128)(2,1)S(1)}, bf16[8,64,1024]{2,1,0:T(8,128)(2,1)S(1)}, u32[]{:S(2)}, u32[]{:S(2)}) collective-permute-start(bf16[8,64,1024]{2,1,0:T(8,128)(2,1)S(1)} %pad_maximum_fusion.refs_16_), channel_id=1, source_target_pairs={{0,1},{1,0},{2,3},{3,2},{4,5},{5,4},{6,7},{7,6},{8,9},{9,8},{10,11... | collective-permute-start | bytes 3145736 | tf_op jit(solution)/shard_map/ppermute | solution.py:36
  334.2 15.9 %collective-permute-done.29.refs_19_ = bf16[8,64,1024]{2,1,0:T(8,128)(2,1)S(1)} collective-permute-done((bf16[8,64,1024]{2,1,0:T(8,128)(2,1)S(1)}, bf16[8,64,1024]{2,1,0:T(8,128)(2,1)S(1)}, u32[]{:S(2)}, u32[]{:S(2)}) %collective-permute-start.29) | collective-permute-done | bytes 1048608 | tf_op jit(solution)/shard_map/ppermute | solution.py:36
  350.1 26.3 %collective-permute-start.33 = (bf16[8,64,1024]{2,1,0:T(8,128)(2,1)S(1)}, bf16[8,64,1024]{2,1,0:T(8,128)(2,1)S(1)}, u32[]{:S(2)}, u32[]{:S(2)}) collective-permute-start(bf16[8,64,1024]{2,1,0:T(8,128)(2,1)S(1)} %collective-permute-done.29.refs_19_), channel_id=1, source_target_pairs={{0,1},{1,0},{2,3},{3,2},{4,5},{5,4},{6,7},{7,6},{8,9},{9,8},{10,11... | collective-permute-start | bytes 3145736 | tf_op jit(solution)/shard_map/ppermute | solution.py:36
  378.4 21.7 %collective-permute-done.6.refs_6_ = bf16[896,512]{1,0:T(8,128)(2,1)S(1)} collective-permute-done((bf16[896,512]{1,0:T(8,128)(2,1)S(1)}, bf16[896,512]{1,0:T(8,128)(2,1)S(1)}, u32[]{:S(2)}, u32[]{:S(2)}) %collective-permute-start.6) | collective-permute-done | bytes 917536 | tf_op jit(solution)/shard_map/ppermute | solution.py:32
  403.1 18.5 %shard_map.56 = f32[896,1024]{1,0:T(8,128)} custom-call(bf16[896,512]{1,0:T(8,128)(2,1)S(1)} %get-tuple-element.7.refs_0_, bf16[896,512]{1,0:T(8,128)(2,1)S(1)} %collective-permute-done.refs_1_, bf16[896,512]{1,0:T(8,128)(2,1)S(1)} %collective-permute-done.1.refs_2_, bf16[896,512]{1,0:T(8,128)(2,1)} %collective-permute-done.2.refs_3_, ...), custom_call_target="tpu_custom_call" | custom-call | flops 7516192768 | bytes 41943040 | tf_op jit(solution)/shard_map/pallas_call | solution.py:98
  (122 shorter events, 39.3 us)
Async XLA Ops:
  42.4 25.6 %collective-permute-start.15 = (bf16[64,8192]{1,0:T(8,128)(2,1)S(1)}, bf16[64,8192]{1,0:T(8,128)(2,1)S(1)}, u32[]{:S(2)}, u32[]{:S(2)}) collective-permute-start(bf16[64,8192]{1,0:T(8,128)(2,1)S(1)} %get-tuple-element.17), channel_id=1, source_target_pairs={{0,2},{1,3},{2,4},{3,5},{4,6},{5,7},{6,0},{7,1},{8,10},{9,11},{10,... | collective-permute-start | bytes 3145736 | tf_op jit(solution)/shard_map/ppermute | solution.py:36
  43.8 24.3 %collective-permute-start.17 = (bf16[64,8192]{1,0:T(8,128)(2,1)S(1)}, bf16[64,8192]{1,0:T(8,128)(2,1)S(1)}, u32[]{:S(2)}, u32[]{:S(2)}) collective-permute-start(bf16[64,8192]{1,0:T(8,128)(2,1)S(1)} %get-tuple-element.18), channel_id=1, source_target_pairs={{0,6},{1,7},{2,0},{3,1},{4,2},{5,3},{6,4},{7,5},{8,14},{9,15},{10,... | collective-permute-start | bytes 3145736 | tf_op jit(solution)/shard_map/ppermute | solution.py:36
  45.2 46.4 %collective-permute-start.16 = (bf16[64,8192]{1,0:T(8,128)(2,1)S(1)}, bf16[64,8192]{1,0:T(8,128)(2,1)S(1)}, u32[]{:S(2)}, u32[]{:S(2)}) collective-permute-start(bf16[64,8192]{1,0:T(8,128)(2,1)S(1)} %get-tuple-element.19), channel_id=1, source_target_pairs={{0,4},{1,5},{2,6},{3,7},{4,0},{5,1},{6,2},{7,3},{8,12},{9,13},{10,... | collective-permute-start | bytes 3145736 | tf_op jit(solution)/shard_map/ppermute | solution.py:36
  46.8 65.4 %collective-permute-start.3 = (bf16[896,512]{1,0:T(8,128)(2,1)S(1)}, bf16[896,512]{1,0:T(8,128)(2,1)S(1)}, u32[]{:S(2)}, u32[]{:S(2)}) collective-permute-start(bf16[896,512]{1,0:T(8,128)(2,1)S(1)} %get-tuple-element.7.refs_0_), channel_id=1, source_target_pairs={{0,64},{16,80},{32,96},{48,112},{64,0},{80,16},{96,32},{112,48},{1... | collective-permute-start | bytes 2752520 | tf_op jit(solution)/shard_map/ppermute | solution.py:32
  48.1 65.4 %collective-permute-start = (bf16[896,512]{1,0:T(8,128)(2,1)S(1)}, bf16[896,512]{1,0:T(8,128)(2,1)S(1)}, u32[]{:S(2)}, u32[]{:S(2)}) collective-permute-start(bf16[896,512]{1,0:T(8,128)(2,1)S(1)} %get-tuple-element.7.refs_0_), channel_id=1, source_target_pairs={{0,48},{16,0},{32,16},{48,32},{64,112},{80,64},{96,80},{112,96},{1... | collective-permute-start | bytes 2752520 | tf_op jit(solution)/shard_map/ppermute | solution.py:32
  97.7 62.3 %collective-permute-start.2 = (bf16[896,512]{1,0:T(8,128)(2,1)S(1)}, bf16[896,512]{1,0:T(8,128)(2,1)}, u32[]{:S(2)}, u32[]{:S(2)}) collective-permute-start(bf16[896,512]{1,0:T(8,128)(2,1)S(1)} %get-tuple-element.7.refs_0_), channel_id=1, source_target_pairs={{0,16},{16,32},{32,48},{48,0},{64,80},{80,96},{96,112},{112,64},{1... | collective-permute-start | bytes 2752520 | tf_op jit(solution)/shard_map/ppermute | solution.py:32
  110.4 128.7 %collective-permute-start.13 = (bf16[896,1024]{1,0:T(8,128)(2,1)}, bf16[896,1024]{1,0:T(8,128)(2,1)}, u32[]{:S(2)}, u32[]{:S(2)}) collective-permute-start(bf16[896,1024]{1,0:T(8,128)(2,1)} %get-tuple-element.9), channel_id=1, source_target_pairs={{0,80},{16,96},{32,112},{48,64},{64,16},{80,32},{96,48},{112,0},{1... | collective-permute-start | bytes 5505032 | tf_op jit(solution)/shard_map/ppermute | solution.py:32
  112.2 67.4 %collective-permute-start.5 = (bf16[896,512]{1,0:T(8,128)(2,1)S(1)}, bf16[896,512]{1,0:T(8,128)(2,1)S(1)}, u32[]{:S(2)}, u32[]{:S(2)}) collective-permute-start(bf16[896,512]{1,0:T(8,128)(2,1)S(1)} %collective-permute-done.3.refs_4_), channel_id=1, source_target_pairs={{0,16},{16,32},{32,48},{48,0},{64,80},{80,96},{96,112},{112,64},{1... | collective-permute-start | bytes 2752520 | tf_op jit(solution)/shard_map/ppermute | solution.py:32
  113.5 116.8 %collective-permute-start.4 = (bf16[896,512]{1,0:T(8,128)(2,1)S(1)}, bf16[896,512]{1,0:T(8,128)(2,1)S(1)}, u32[]{:S(2)}, u32[]{:S(2)}) collective-permute-start(bf16[896,512]{1,0:T(8,128)(2,1)S(1)} %collective-permute-done.3.refs_4_), channel_id=1, source_target_pairs={{0,48},{16,0},{32,16},{48,32},{64,112},{80,64},{96,80},{112,96},{1... | collective-permute-start | bytes 2752520 | tf_op jit(solution)/shard_map/ppermute | solution.py:32
  114.9 115.5 %collective-permute-start.1 = (bf16[896,512]{1,0:T(8,128)(2,1)S(1)}, bf16[896,512]{1,0:T(8,128)(2,1)S(1)}, u32[]{:S(2)}, u32[]{:S(2)}) collective-permute-start(bf16[896,512]{1,0:T(8,128)(2,1)S(1)} %collective-permute-done.refs_1_), channel_id=1, source_target_pairs={{0,48},{16,0},{32,16},{48,32},{64,112},{80,64},{96,80},{112,96},{1... | collective-permute-start | bytes 2752520 | tf_op jit(solution)/shard_map/ppermute | solution.py:32
  179.6 59.6 %collective-permute-start.12 = (bf16[896,1024]{1,0:T(8,128)(2,1)}, bf16[896,1024]{1,0:T(8,128)(2,1)S(1)}, u32[]{:S(2)}, u32[]{:S(2)}) collective-permute-start(bf16[896,1024]{1,0:T(8,128)(2,1)} %get-tuple-element.10), channel_id=1, source_target_pairs={{0,96},{16,112},{32,64},{48,80},{64,32},{80,48},{96,0},{112,16},{1... | collective-permute-start | bytes 5505032 | tf_op jit(solution)/shard_map/ppermute | solution.py:32
  180.8 44.8 %collective-permute-start.20 = (bf16[32,1024]{1,0:T(8,128)(2,1)S(1)}, bf16[32,1024]{1,0:T(8,128)(2,1)S(1)}, u32[]{:S(2)}, u32[]{:S(2)}) collective-permute-start(bf16[32,1024]{1,0:T(8,128)(2,1)S(1)} %get-tuple-element.25), channel_id=1, source_target_pairs={{0,32},{16,48},{32,0},{48,16},{64,96},{80,112},{96,64},{112,80},{1... | collective-permute-start | bytes 196616 | tf_op jit(solution)/shard_map/ppermute | solution.py:32
  235.9 91.1 %collective-permute-start.11 = (bf16[896,1024]{1,0:T(8,128)(2,1)}, bf16[896,1024]{1,0:T(8,128)(2,1)S(1)}, u32[]{:S(2)}, u32[]{:S(2)}) collective-permute-start(bf16[896,1024]{1,0:T(8,128)(2,1)} %get-tuple-element.11), channel_id=1, source_target_pairs={{0,112},{16,64},{32,80},{48,96},{64,48},{80,0},{96,16},{112,32},{1... | collective-permute-start | bytes 5505032 | tf_op jit(solution)/shard_map/ppermute | solution.py:32
  236.4 91.0 %collective-permute-start.10 = (bf16[896,1024]{1,0:T(8,128)(2,1)}, bf16[896,1024]{1,0:T(8,128)(2,1)S(1)}, u32[]{:S(2)}, u32[]{:S(2)}) collective-permute-start(bf16[896,1024]{1,0:T(8,128)(2,1)} %get-tuple-element.12), channel_id=1, source_target_pairs={{0,64},{16,80},{32,96},{48,112},{64,0},{80,16},{96,32},{112,48},{1... | collective-permute-start | bytes 5505032 | tf_op jit(solution)/shard_map/ppermute | solution.py:32
  238.0 90.9 %collective-permute-start.9 = (bf16[896,1024]{1,0:T(8,128)(2,1)}, bf16[896,1024]{1,0:T(8,128)(2,1)S(1)}, u32[]{:S(2)}, u32[]{:S(2)}) collective-permute-start(bf16[896,1024]{1,0:T(8,128)(2,1)} %get-tuple-element.13), channel_id=1, source_target_pairs={{0,16},{16,32},{32,48},{48,0},{64,80},{80,96},{96,112},{112,64},{1... | collective-permute-start | bytes 5505032 | tf_op jit(solution)/shard_map/ppermute | solution.py:32
  239.1 87.8 %collective-permute-start.26 = (bf16[8,32,1024]{2,1,0:T(8,128)(2,1)S(1)}, bf16[8,32,1024]{2,1,0:T(8,128)(2,1)S(1)}, u32[]{:S(2)}, u32[]{:S(2)}) collective-permute-start(bf16[8,32,1024]{2,1,0:T(8,128)(2,1)S(1)} %bitcast_dynamic-update-slice_fusion), channel_id=1, source_target_pairs={{0,8},{1,9},{2,10},{3,11},{4,12},{5,13},{6,14},{7,15},{8,0},{9,1},... | collective-permute-start | bytes 1572872 | tf_op jit(solution)/shard_map/ppermute | solution.py:36
  239.2 90.7 %collective-permute-start.8 = (bf16[896,1024]{1,0:T(8,128)(2,1)S(1)}, bf16[896,1024]{1,0:T(8,128)(2,1)S(1)}, u32[]{:S(2)}, u32[]{:S(2)}) collective-permute-start(bf16[896,1024]{1,0:T(8,128)(2,1)S(1)} %copy-done.5), channel_id=1, source_target_pairs={{0,32},{16,48},{32,0},{48,16},{64,96},{80,112},{96,64},{112,80},{1... | collective-permute-start | bytes 5505032 | tf_op jit(solution)/shard_map/ppermute | solution.py:32
  326.9 50.1 %collective-permute-start.7 = (bf16[896,1024]{1,0:T(8,128)(2,1)S(1)}, bf16[896,1024]{1,0:T(8,128)(2,1)S(1)}, u32[]{:S(2)}, u32[]{:S(2)}) collective-permute-start(bf16[896,1024]{1,0:T(8,128)(2,1)S(1)} %copy-done.4), channel_id=1, source_target_pairs={{0,48},{16,0},{32,16},{48,32},{64,112},{80,64},{96,80},{112,96},{1... | collective-permute-start | bytes 5505032 | tf_op jit(solution)/shard_map/ppermute | solution.py:32
  327.3 49.0 %collective-permute-start.28 = (bf16[8,64,1024]{2,1,0:T(8,128)(2,1)S(1)}, bf16[8,64,1024]{2,1,0:T(8,128)(2,1)S(1)}, u32[]{:S(2)}, u32[]{:S(2)}) collective-permute-start(bf16[8,64,1024]{2,1,0:T(8,128)(2,1)S(1)} %pad_maximum_fusion.refs_16_), channel_id=1, source_target_pairs={{0,4},{1,5},{2,6},{3,7},{4,0},{5,1},{6,2},{7,3},{8,12},{9,13},{10,... | collective-permute-start | bytes 3145736 | tf_op jit(solution)/shard_map/ppermute | solution.py:36
  328.9 47.6 %collective-permute-start.27 = (bf16[8,64,1024]{2,1,0:T(8,128)(2,1)S(1)}, bf16[8,64,1024]{2,1,0:T(8,128)(2,1)S(1)}, u32[]{:S(2)}, u32[]{:S(2)}) collective-permute-start(bf16[8,64,1024]{2,1,0:T(8,128)(2,1)S(1)} %pad_maximum_fusion.refs_16_), channel_id=1, source_target_pairs={{0,6},{1,7},{2,0},{3,1},{4,2},{5,3},{6,4},{7,5},{8,14},{9,15},{10,... | collective-permute-start | bytes 3145736 | tf_op jit(solution)/shard_map/ppermute | solution.py:36
  329.9 70.2 %collective-permute-start.30 = (bf16[8,64,1024]{2,1,0:T(8,128)(2,1)S(1)}, bf16[8,64,1024]{2,1,0:T(8,128)(2,1)S(1)}, u32[]{:S(2)}, u32[]{:S(2)}) collective-permute-start(bf16[8,64,1024]{2,1,0:T(8,128)(2,1)S(1)} %pad_maximum_fusion.refs_16_), channel_id=1, source_target_pairs={{0,1},{1,0},{2,3},{3,2},{4,5},{5,4},{6,7},{7,6},{8,9},{9,8},{10,11... | collective-permute-start | bytes 3145736 | tf_op jit(solution)/shard_map/ppermute | solution.py:36
  350.1 50.1 %collective-permute-start.33 = (bf16[8,64,1024]{2,1,0:T(8,128)(2,1)S(1)}, bf16[8,64,1024]{2,1,0:T(8,128)(2,1)S(1)}, u32[]{:S(2)}, u32[]{:S(2)}) collective-permute-start(bf16[8,64,1024]{2,1,0:T(8,128)(2,1)S(1)} %collective-permute-done.29.refs_19_), channel_id=1, source_target_pairs={{0,1},{1,0},{2,3},{3,2},{4,5},{5,4},{6,7},{7,6},{8,9},{9,8},{10,11... | collective-permute-start | bytes 3145736 | tf_op jit(solution)/shard_map/ppermute | solution.py:36
  376.4 23.8 %collective-permute-start.32 = (bf16[8,64,1024]{2,1,0:T(8,128)(2,1)S(1)}, bf16[8,64,1024]{2,1,0:T(8,128)(2,1)S(1)}, u32[]{:S(2)}, u32[]{:S(2)}) collective-permute-start(bf16[8,64,1024]{2,1,0:T(8,128)(2,1)S(1)} %collective-permute-done.28.refs_18_), channel_id=1, source_target_pairs={{0,1},{1,0},{2,3},{3,2},{4,5},{5,4},{6,7},{7,6},{8,9},{9,8},{10,11... | collective-permute-start | bytes 3145736 | tf_op jit(solution)/shard_map/ppermute | solution.py:36
  376.5 23.7 %collective-permute-start.31 = (bf16[8,64,1024]{2,1,0:T(8,128)(2,1)S(1)}, bf16[8,64,1024]{2,1,0:T(8,128)(2,1)S(1)}, u32[]{:S(2)}, u32[]{:S(2)}) collective-permute-start(bf16[8,64,1024]{2,1,0:T(8,128)(2,1)S(1)} %collective-permute-done.27.refs_17_), channel_id=1, source_target_pairs={{0,1},{1,0},{2,3},{3,2},{4,5},{5,4},{6,7},{7,6},{8,9},{9,8},{10,11... | collective-permute-start | bytes 3145736 | tf_op jit(solution)/shard_map/ppermute | solution.py:36
  (35 other events, 1442.7 us)

commit v2 on v0

v2 whole, which is shorter than its diff:
```python
import math

import jax
import jax.numpy as jnp
from jax import lax
from jax.experimental import pallas as pl
from jax.experimental.pallas import tpu as pltpu
from jax.sharding import Mesh
from jax.sharding import PartitionSpec as P

FF = 14336
TOK = 512
POOL = 1024
UNITS = 896
D = 8192
WIDE = 1024
WP = 768
WQ = WIDE - WP
SHRINK = 1.0 / math.sqrt(FF)
SWAP = [(0, 1), (1, 0)]
BF = jnp.bfloat16
F32 = jnp.float32


def shift(k):
    return [(i, (i + k) % 4) for i in range(4)]


def shape(*dims, dtype=BF):
    return jax.ShapeDtypeStruct(dims, dtype)


def hidden_kernel(place_ref, rows_ref, gate_ref, up_ref, w_ref, hidden_ref, squares_ref, wz0, wz1, wz2, wz3, wy0, wy1, sems):
    y, z = place_ref[0], place_ref[1]
    step = pl.program_id(0)

    def copies():
        out = []
        for dz, piece in enumerate((wz0, wz1, wz2, wz3)):
            for dy in range(2):
                first = ((y + dy) % 2 * 4 + (z + dz) % 4) * WIDE
                out.append((w_ref.at[:, pl.ds(pl.multiple_of(first, 128), WP)], piece.at[dy]))
        for dy, piece in enumerate((wy0, wy1)):
            for dz in range(4):
                first = ((y + dy) % 2 * 4 + (z + dz) % 4) * WIDE + WP
                out.append((w_ref.at[:, pl.ds(pl.multiple_of(first, 128), WQ)], piece.at[dz]))
        return [pltpu.make_async_copy(src, dst, sems.at[i]) for i, (src, dst) in enumerate(out)]

    @pl.when(step == 0)
    def _():
        for copy in copies():
            copy.start()

    pool = lax.broadcasted_iota(jnp.int32, (TOK, POOL), 1)
    pick = jnp.where(rows_ref[...] == pool, 1.0, 0.0).astype(BF)
    gate = jnp.dot(pick, gate_ref[...], preferred_element_type=F32)
    up = jnp.dot(pick, up_ref[...], preferred_element_type=F32)
    hidden = (gate / (1.0 + jnp.exp(-gate)) * up).astype(BF)
    hidden_ref[...] = hidden
    wide = hidden.astype(F32)
    squares_ref[...] = (wide * wide).T.astype(BF)

    @pl.when(step == pl.num_programs(0) - 1)
    def _():
        for copy in copies():
            copy.wait()


def make_hidden(place, rows, gate, up, projection):
    step = 128
    anywhere = pl.BlockSpec(memory_space=pl.ANY)
    return pl.pallas_call(
        hidden_kernel,
        grid_spec=pltpu.PrefetchScalarGridSpec(
            num_scalar_prefetch=1,
            grid=(UNITS // step,),
            in_specs=[
                pl.BlockSpec((TOK, 1), lambda i, s: (0, 0)),
                pl.BlockSpec((POOL, step), lambda i, s: (0, i)),
                pl.BlockSpec((POOL, step), lambda i, s: (0, i)),
                anywhere,
            ],
            out_specs=[
                pl.BlockSpec((TOK, step), lambda i, s: (0, i)),
                pl.BlockSpec((step, TOK), lambda i, s: (i, 0)),
            ]
            + [anywhere] * 6,
            scratch_shapes=[pltpu.SemaphoreType.DMA((16,))],
        ),
        out_shape=[shape(TOK, UNITS), shape(UNITS, TOK)]
        + [shape(2, UNITS, WP)] * 4
        + [shape(4, UNITS, WQ)] * 2,
        compiler_params=pltpu.CompilerParams(vmem_limit_bytes=56 * 2**20),
        cost_estimate=pl.CostEstimate(
            flops=4 * TOK * POOL * UNITS, bytes_accessed=34 * 2**20, transcendentals=TOK * UNITS
        ),
    )(place, rows, gate, up, projection)


def partial_kernel(low, high, hidden_ref, w_ref, own_ref, other_ref):
    product = jnp.dot(hidden_ref[...], w_ref[:, low:high], preferred_element_type=F32) * SHRINK
    own_ref[...] = product[:256].astype(BF)
    other_ref[...] = product[256:].astype(BF)


def partial_outputs(hidden, projection, low, high):
    width = high - low
    return pl.pallas_call(
        lambda *refs: partial_kernel(low, high, *refs),
        grid=(8,),
        in_specs=[
            pl.BlockSpec((TOK, UNITS), lambda j: (0, 0)),
            pl.BlockSpec((UNITS, WIDE), lambda j: (0, j)),
        ],
        out_specs=[pl.BlockSpec((256, width), lambda j: (0, j))] * 2,
        out_shape=[shape(256, 8 * width)] * 2,
        compiler_params=pltpu.CompilerParams(vmem_limit_bytes=40 * 2**20),
        cost_estimate=pl.CostEstimate(
            flops=16 * TOK * UNITS * width, bytes_accessed=24 * 2**20, transcendentals=0
        ),
    )(hidden, projection)


def square_kernel(low, high, place_ref, total_ref, far_ref, targets_ref, out_ref):
    outputs = total_ref[...] + far_ref[...].astype(F32)
    errors = (outputs - targets_ref[:, low:high].astype(F32)).astype(BF).astype(F32)
    out_ref[0] = (errors * errors).astype(BF)


def error_squares(place, total, far, targets, low, high, out_shape, out_index):
    width = high - low
    return pl.pallas_call(
        lambda *refs: square_kernel(low, high, *refs),
        grid_spec=pltpu.PrefetchScalarGridSpec(
            num_scalar_prefetch=1,
            grid=(8,),
            in_specs=[
                pl.BlockSpec((64, width), lambda j, s: (0, j)),
                pl.BlockSpec((64, width), lambda j, s: (0, j)),
                pl.BlockSpec((64, WIDE), lambda j, s: (s[3] * 4 + s[2], j)),
            ],
            out_specs=pl.BlockSpec((1, 64, width), out_index),
        ),
        out_shape=out_shape,
        compiler_params=pltpu.CompilerParams(vmem_limit_bytes=16 * 2**20),
        cost_estimate=pl.CostEstimate(flops=64 * 8 * width * 4, bytes_accessed=4 * 2**20, transcendentals=0),
    )(place, total, far, targets)


def place_tokens(x, parts, scratch, member_of):
    for n, part in enumerate(parts):
        row = n // 4 * 256 + lax.rem(x + 4 - n % 4, 4) * 64
        for k in range(scratch.shape[0]):
            scratch[k, pl.ds(pl.multiple_of(row, 64), 64), :] = part[member_of(k)]


def sums(units, weights, squares, number):
    numerator = denominator = None
    for k in range(number):
        fisher = jnp.dot(units[k], squares(k), preferred_element_type=F32) * (1.0 / TOK)
        weighted = (fisher * weights(k).astype(F32)).astype(BF).astype(F32)
        term = fisher.astype(BF).astype(F32)
        numerator = weighted if numerator is None else numerator + weighted
        denominator = term if denominator is None else denominator + term
    return numerator, denominator


def set_p_kernel(place_ref, *refs):
    units, weights, parts = refs[:4], refs[4:8], refs[8:16]
    out_ref, scratch = refs[16:]
    z, x = place_ref[1], place_ref[2]

    @pl.when(pl.program_id(0) == 0)
    def _():
        place_tokens(x, parts, scratch, lambda k: lax.rem(z + 4 - k, 4))

    numerator, denominator = sums(
        [u[...] for u in units], lambda k: weights[k][0], lambda k: scratch[k], 4
    )
    out_ref[0] = numerator.astype(out_ref.dtype)
    out_ref[1] = denominator.astype(out_ref.dtype)


def set_p(place, units, weights, parts, dy, dtype):
    tall = 224
    return pl.pallas_call(
        set_p_kernel,
        grid_spec=pltpu.PrefetchScalarGridSpec(
            num_scalar_prefetch=1,
            grid=(UNITS // tall,),
            in_specs=[pl.BlockSpec((tall, TOK), lambda u, s: (u, 0))] * 4
            + [pl.BlockSpec((1, tall, WP), lambda u, s: (dy, u, 0))] * 4
            + [pl.BlockSpec((4, 64, WP), lambda u, s: (0, 0, dy))] * 8,
            out_specs=pl.BlockSpec((2, tall, WP), lambda u, s: (0, u, 0)),
            scratch_shapes=[pltpu.VMEM((4, TOK, WP), BF)],
        ),
        out_shape=shape(2, UNITS, WP, dtype=dtype),
        compiler_params=pltpu.CompilerParams(vmem_limit_bytes=40 * 2**20),
        cost_estimate=pl.CostEstimate(
            flops=8 * TOK * UNITS * WP, bytes_accessed=16 * 2**20, transcendentals=0
        ),
    )(place, *units, *weights, *parts)


def set_q_kernel(place_ref, *refs):
    units, weights, parts = refs[:2], refs[2:4], refs[4:12]
    outs, scratch = refs[12:16], refs[16]
    x = place_ref[2]

    @pl.when(pl.program_id(0) == 0)
    def _():
        place_tokens(x, parts, scratch, lambda k: k)

    for dz in (1, 2, 3, 0):
        numerator, denominator = sums(
            [u[...] for u in units],
            lambda k: weights[k][dz],
            lambda k: scratch[k, :, dz * WQ : dz * WQ + WQ],
            2,
        )
        outs[dz][0] = numerator.astype(outs[dz].dtype)
        outs[dz][1] = denominator.astype(outs[dz].dtype)


def set_q(place, units, weights, parts):
    tall = 224
    return pl.pallas_call(
        set_q_kernel,
        grid_spec=pltpu.PrefetchScalarGridSpec(
            num_scalar_prefetch=1,
            grid=(UNITS // tall,),
            in_specs=[pl.BlockSpec((tall, TOK), lambda u, s: (u, 0))] * 2
            + [pl.BlockSpec((4, tall, WQ), lambda u, s: (0, u, 0))] * 2
            + [pl.BlockSpec((2, 64, 4 * WQ), lambda u, s: (0, 0, 0))] * 8,
            out_specs=[pl.BlockSpec((2, tall, WQ), lambda u, s: (0, u, 0))] * 4,
            scratch_shapes=[pltpu.VMEM((2, TOK, 4 * WQ), BF)],
        ),
        out_shape=[shape(2, UNITS, WQ, dtype=F32)] + [shape(2, UNITS, WQ)] * 3,
        compiler_params=pltpu.CompilerParams(vmem_limit_bytes=40 * 2**20),
        cost_estimate=pl.CostEstimate(
            flops=16 * TOK * UNITS * WQ, bytes_accessed=16 * 2**20, transcendentals=0
        ),
    )(place, *units, *weights, *parts)


def quotient_kernel(p_own, p_far, q_own, q_one, q_two, q_three, out_ref):
    def wide(ref, i):
        return ref[i].astype(F32)

    out_ref[:, :WP] = (p_own[0] + wide(p_far, 0)) / (p_own[1] + wide(p_far, 1) + 1e-06)
    numerator = q_own[0] + wide(q_one, 0) + wide(q_two, 0) + wide(q_three, 0)
    denominator = q_own[1] + wide(q_one, 1) + wide(q_two, 1) + wide(q_three, 1)
    out_ref[:, WP:] = numerator / (denominator + 1e-06)


def quotient(p_own, p_far, q_own, q_far):
    tall = 128
    return pl.pallas_call(
        quotient_kernel,
        grid=(UNITS // tall,),
        in_specs=[pl.BlockSpec((2, tall, WP), lambda u: (0, u, 0))] * 2
        + [pl.BlockSpec((2, tall, WQ), lambda u: (0, u, 0))] * 4,
        out_specs=pl.BlockSpec((tall, WIDE), lambda u: (u, 0)),
        out_shape=shape(UNITS, WIDE, dtype=F32),
        compiler_params=pltpu.CompilerParams(vmem_limit_bytes=32 * 2**20),
        cost_estimate=pl.CostEstimate(flops=UNITS * WIDE * 6, bytes_accessed=16 * 2**20, transcendentals=0),
    )(p_own, p_far, q_own, *q_far)


def body(token_rows, gate_cache, up_cache, down_weight, targets):
    y, z, x, core = (lax.axis_index(name) for name in ("y_lo", "z", "x", "core"))
    place = jnp.stack([y, z, x, core]).astype(jnp.int32)
    projection = down_weight[0]

    picked = token_rows[0].reshape(2, TOK // 2)
    picked = jnp.where(core == 1, picked[::-1], picked).reshape(TOK, 1)
    hidden, squares, wz0, wz1, wz2, wz3, wy0, wy1 = make_hidden(
        place, picked, gate_cache[0], up_cache[0], projection
    )
    wz = [wz0] + [lax.ppermute(w, "z", shift(k + 1)) for k, w in enumerate((wz1, wz2, wz3))]
    wy = [wy0, lax.ppermute(wy1, "y_lo", SWAP)]
    uz = [squares] + [lax.ppermute(squares, "z", shift(k)) for k in (1, 2, 3)]
    uy = [squares, lax.ppermute(squares, "y_lo", SWAP)]

    def reduced(low, high):
        own, other = partial_outputs(hidden, projection, low, high)
        pair = (own.astype(F32) + lax.ppermute(other, "core", SWAP).astype(F32)).astype(BF)
        blocks = lax.all_to_all(pair.reshape(4, 64, -1), "x", 0, 0, tiled=True)
        return jnp.sum(blocks.astype(F32), axis=0)

    def far(total):
        return lax.ppermute(total.astype(BF), "y_hi", SWAP)

    def all_tokens(part):
        row = [part] + [lax.ppermute(part, "x", shift(k)) for k in (1, 2, 3)]
        return row + [lax.ppermute(r, "core", SWAP) for r in row]

    total_p = reduced(0, WP)
    far_p = far(total_p)
    total_q = reduced(WP, WIDE)
    far_q = far(total_q)
    squares_p = error_squares(
        place, total_p, far_p, targets[0], 0, WP, shape(4, 64, 2 * WP),
        lambda j, s: (lax.rem(j, 4), 0, lax.rem(j // 4 + s[0], 2)),
    )
    squares_q = error_squares(
        place, total_q, far_q, targets[0], WP, WIDE, shape(2, 64, 4 * WQ),
        lambda j, s: (lax.rem(j // 4 + s[0], 2), 0, lax.rem(lax.rem(j, 4) + 4 - s[1], 4)),
    )
    parts_p = all_tokens(lax.all_to_all(squares_p, "z", 0, 0, tiled=True))
    parts_q = all_tokens(jnp.stack([squares_q[0], lax.ppermute(squares_q[1], "y_lo", SWAP)]))

    p_send = set_p(place, uz, wz, parts_p, 1, BF)
    p_far = lax.ppermute(p_send, "y_lo", SWAP)
    q_own, *q_send = set_q(place, uy, wy, parts_q)
    q_far = [lax.ppermute(q, "z", shift(k + 1)) for k, q in enumerate(q_send)]
    p_own = set_p(place, uz, wz, parts_p, 0, F32)
    return quotient(p_own, p_far, q_own, q_far)


def solution(mesh):
    cut = Mesh(mesh.devices.reshape(2, 4, 2, 4, 2), ("y_lo", "z", "y_hi", "x", "core"))
    ft, tp = ("y_lo", "z"), ("y_hi", "x", "core")
    placed = (P(ft, None), P(ft, None, tp), P(ft, None, tp), P(ft, tp, None), P(ft, None, None))
    return jax.shard_map(body, mesh=cut, in_specs=placed, out_specs=P(tp, ft), check_vma=False)
```

time: 576 us -> 914 us (1.59)
  Pallas kernels: 0 us -> 503 us
  waiting for transfers between devices: 509 us -> 275 us
  starting transfers between devices: 0.09 us -> 112 us
  matrix products: 41.7 us -> 0 us
  between operations: 13.1 us -> 0.24 us
    pallas_call x0 -> x9, Pallas kernels: none -> 503 us  [the longest x1 448 us: make_hidden(): pl.pallas_call(hidden_kernel, grid_spec=pltpu.PrefetchScalarGridSpec(num_...]
    reduce_scatter x2 -> x0, waiting for transfers between devices: 307 us -> none  [the longest x1 153 us: body(): lax.psum_scatter(fisher.astype(jnp.bfloat16), 'ft', scatter_dimension=1,...]
    ppermute x0 -> x31, waiting for transfers between devices: none -> 233 us  [the longest x2 109 us: far(): return lax.ppermute(total.astype(BF), 'y_hi', SWAP)]
    psum x1 -> x0, waiting for transfers between devices: 202 us -> none  [body(): outputs = lax.psum(partial_out, 'tp')]
    ppermute x0 -> x31, starting transfers between devices: none -> 99.3 us  [the longest x2 35.4 us: reduced(): lax.ppermute(other, 'core', SWAP).astype(F32)]
    dot_general x2 -> x0, matrix products: 41.7 us -> none  [the longest x1 25.2 us: body(): lax.dot_general(unit_squares, error_squares, (((0,), (0,)), ((), ())), pr...]
    all_to_all x0 -> x3, waiting for transfers between devices: none -> 41.7 us  [the longest x2 34 us: reduced(): blocks = lax.all_to_all(pair.reshape(4, 64, -1), 'x', 0, 0, tiled=True)]
    all_to_all x0 -> x3, starting transfers between devices: none -> 13 us  [the longest x2 9.03 us: reduced(): blocks = lax.all_to_all(pair.reshape(4, 64, -1), 'x', 0, 0, tiled=True)]
  transfers between devices with their start and end apart: 3 -> 34, of which waited for: 3 -> 14; matrix products, arithmetic and copies ran while one was open for 0% -> 1% of each run, Pallas kernels for 0% -> 4%
where the time goes in v2:
time: 914 us; the launch traced here: 913 us
  Pallas kernels  503 us (55%)
  waiting for transfers between devices  275 us (30%)
  starting transfers between devices  112 us (12%)
  other arithmetic  11.9 us (1%)
  local copies, waits for them, and re-layouts  10.5 us (1%)
    pallas_call x1, Pallas kernels, make_hidden(): pl.pallas_call(hidden_kernel, grid_spec=pltpu.PrefetchScalarGridSpec(num_...  448 us
    ppermute x2, waiting for transfers between devices, far(): return lax.ppermute(total.astype(BF), 'y_hi', SWAP)  109 us
    ppermute x3, waiting for transfers between devices, body(): uz = [squares] + [lax.ppermute(squares, 'z', shift(k)) for k in (1, 2, 3)]  65.8 us
    ppermute x2, starting transfers between devices, reduced(): lax.ppermute(other, 'core', SWAP).astype(F32)  35.4 us
    ppermute x8, starting transfers between devices, all_tokens(): return row + [lax.ppermute(r, 'core', SWAP) for r in row]  34.7 us
    all_to_all x2, waiting for transfers between devices, reduced(): blocks = lax.all_to_all(pair.reshape(4, 64, -1), 'x', 0, 0, tiled=True)  34 us
    ppermute x3, waiting for transfers between devices, body(): q_far = [lax.ppermute(q, 'z', shift(k + 1)) for k, q in enumerate(q_send)]  30.6 us
    pallas_call x2, Pallas kernels, partial_outputs(): pl.pallas_call(lambda *refs: partial_kernel(low, high, *refs), grid=(8,),...  21.2 us
  transfers between devices with their start and end apart: 34, of which 14 were waited for; matrix products, arithmetic and copies ran while one was open for 1% of the time, Pallas kernels for 4%

profile of v2, /device:TPU:1, one launch (start us, length us, event | category | flops | bytes accessed | tf_op | source)
XLA Modules:
  0.0 912.8 jit_solution(12096441184839420104)
XLA Ops:
  3.5 448.5 %shard_map.55 = (bf16[512,896]{1,0:T(8,128)(2,1)}, bf16[896,512]{1,0:T(8,128)(2,1)}, bf16[2,896,768]{2,1,0:T(8,128)(2,1)}, bf16[2,896,768]{2,1,0:T(8,128)(2,1)},...) custom-call(s32[4]{0:T(128)} %pad_add_fusion.place_ref.refs_0_, ...), custom_call_target="tpu_custom_call" | custom-call | flops 1879048192 | bytes 35651584 | tf_op jit(solution)/shard_map/pallas_call | solution.py:72
  453.1 11.5 %shard_map.56 = (bf16[256,6144]{1,0:T(8,128)(2,1)S(1)}, bf16[256,6144]{1,0:T(8,128)(2,1)S(1)}) custom-call(bf16[512,896]{1,0:T(8,128)(2,1)S(1)} %copy-done.7, bf16[896,8192]{1,0:T(8,128)(2,1)} %bitcast.23), custom_call_target="tpu_custom_call" | custom-call | flops 5637144576 | bytes 25165824 | tf_op jit(solution)/shard_map/pallas_call | solution.py:108
  466.1 5.3 collective-permute-done.6
  474.2 4.8 all-to-all-start
  486.0 30.4 %all-to-all-done = bf16[4,64,6144]{2,1,0:T(8,128)(2,1)} async-done(((bf16[4,64,6144]{2,1,0:T(8,128)(2,1)}), bf16[4,64,6144]{2,1,0:T(8,128)(2,1)}, u32[]{:S(2)}, u32[]{:S(2)}) %all-to-all-start) | async-done | bytes 3145760 | tf_op jit(solution)/shard_map/all_to_all | solution.py:288
  522.3 3.8 collective-permute-start.5
  526.1 9.7 %shard_map.60 = (bf16[256,2048]{1,0:T(8,128)(2,1)S(1)}, bf16[256,2048]{1,0:T(8,128)(2,1)}) custom-call(bf16[512,896]{1,0:T(8,128)(2,1)S(1)} %copy-done.8, bf16[896,8192]{1,0:T(8,128)(2,1)} %bitcast.24), custom_call_target="tpu_custom_call" | custom-call | flops 1879048192 | bytes 25165824 | tf_op jit(solution)/shard_map/pallas_call | solution.py:108
  536.8 26.7 %collective-permute-done.1.refs_2_ = bf16[896,512]{1,0:T(8,128)(2,1)S(1)} collective-permute-done((bf16[896,512]{1,0:T(8,128)(2,1)S(1)}, bf16[896,512]{1,0:T(8,128)(2,1)S(1)}, u32[]{:S(2)}, u32[]{:S(2)}) %collective-permute-start.1) | collective-permute-done | bytes 917536 | tf_op jit(solution)/shard_map/ppermute | solution.py:282
  563.4 33.9 %collective-permute-start.18 = (bf16[256,2048]{1,0:T(8,128)(2,1)}, bf16[256,2048]{1,0:T(8,128)(2,1)}, u32[]{:S(2)}, u32[]{:S(2)}) collective-permute-start(bf16[256,2048]{1,0:T(8,128)(2,1)} %get-tuple-element.32), channel_id=1, source_target_pairs={{0,1},{1,0},{2,3},{3,2},{4,5},{5,4},{6,7},{7,6},{8,9},{9,8},{10,11... | collective-permute-start | bytes 3145736 | tf_op jit(solution)/shard_map/ppermute | solution.py:287
  599.9 3.9 all-to-all-start.1
  603.9 39.1 %collective-permute-done.refs_1_ = bf16[896,512]{1,0:T(8,128)(2,1)} collective-permute-done((bf16[896,512]{1,0:T(8,128)(2,1)S(1)}, bf16[896,512]{1,0:T(8,128)(2,1)}, u32[]{:S(2)}, u32[]{:S(2)}) %collective-permute-start) | collective-permute-done | bytes 917536 | tf_op jit(solution)/shard_map/ppermute | solution.py:282
  642.9 7.6 all-to-all-done.1.refs_8_
  656.3 12.2 %collective-permute-done.10.refs_11_ = bf16[4,64,1536]{2,1,0:T(8,128)(2,1)} collective-permute-done((bf16[4,64,1536]{2,1,0:T(8,128)(2,1)S(1)}, bf16[4,64,1536]{2,1,0:T(8,128)(2,1)}, u32[]{:S(2)}, u32[]{:S(2)}) %collective-permute-start.10) | collective-permute-done | bytes 786464 | tf_op jit(solution)/shard_map/ppermute | solution.py:295
  668.5 18.9 %collective-permute-start.14 = (bf16[4,64,1536]{2,1,0:T(8,128)(2,1)}, bf16[4,64,1536]{2,1,0:T(8,128)(2,1)}, u32[]{:S(2)}, u32[]{:S(2)}) collective-permute-start(bf16[4,64,1536]{2,1,0:T(8,128)(2,1)} %collective-permute-done.10.refs_11_), channel_id=1, source_target_pairs={{0,1},{1,0},{2,3},{3,2},{4,5},{5,4},{6,7},{7,6},{8,9},{9,8},{10,11... | collective-permute-start | bytes 2359304 | tf_op jit(solution)/shard_map/ppermute | solution.py:296
  694.1 4.2 all-to-all-start.2
  699.8 8.8 shard_map.59
  710.0 3.6 all-to-all-done.2
  718.1 108.9 %collective-permute-done.19.refs_2_ = bf16[64,2048]{1,0:T(8,128)(2,1)S(1)} collective-permute-done((bf16[64,2048]{1,0:T(8,128)(2,1)S(1)}, bf16[64,2048]{1,0:T(8,128)(2,1)S(1)}, u32[]{:S(2)}, u32[]{:S(2)}) %collective-permute-start.19) | collective-permute-done | bytes 262176 | tf_op jit(solution)/shard_map/ppermute | solution.py:292
  831.9 4.2 collective-permute-done.20
  842.4 7.9 collective-permute-start.27
  855.1 6.1 shard_map.62
  864.3 9.1 %shard_map.58.p_own = f32[2,896,768]{2,1,0:T(8,128)} custom-call(s32[4]{0:T(128)S(1)} %copy-done.9, bf16[896,512]{1,0:T(8,128)(2,1)S(1)} %copy-done.3, bf16[896,512]{1,0:T(8,128)(2,1)} %collective-permute-done.refs_1_, bf16[896,512]{1,0:T(8,128)(2,1)S(1)} %collective-permute-done.1.refs_2_, bf16[896,512]{1,0:T(8,128)(2,1)S(1)} %collective-permute-done.2.refs_3_, ...), custom_call_target="tpu_custom_call" | custom-call | flops 2818572288 | bytes 16777216 | tf_op jit(solution)/shard_map/pallas_call | solution.py:186
  873.4 30.3 %collective-permute-done.28.q_one = bf16[2,896,256]{2,1,0:T(8,128)(2,1)S(1)} collective-permute-done((bf16[2,896,256]{2,1,0:T(8,128)(2,1)S(1)}, bf16[2,896,256]{2,1,0:T(8,128)(2,1)S(1)}, u32[]{:S(2)}, u32[]{:S(2)}) %collective-permute-start.28) | collective-permute-done | bytes 917536 | tf_op jit(solution)/shard_map/ppermute | solution.py:316
  906.6 6.2 shard_map.63
  (94 shorter events, 67.0 us)
Async XLA Ops:
  474.2 42.2 %all-to-all-start = ((bf16[4,64,6144]{2,1,0:T(8,128)(2,1)}), bf16[4,64,6144]{2,1,0:T(8,128)(2,1)}, u32[]{:S(2)}, u32[]{:S(2)}) async-start(bf16[4,64,6144]{2,1,0:T(8,128)(2,1)} %bitcast.25), calls=%async_computation | async-start | bytes 6291456 | tf_op jit(solution)/shard_map/all_to_all | solution.py:288
  479.0 174.3 %collective-permute-start.3 = (bf16[2,896,768]{2,1,0:T(8,128)(2,1)}, bf16[2,896,768]{2,1,0:T(8,128)(2,1)}, u32[]{:S(2)}, u32[]{:S(2)}) collective-permute-start(bf16[2,896,768]{2,1,0:T(8,128)(2,1)} %get-tuple-element.23), channel_id=1, source_target_pairs={{0,16},{16,32},{32,48},{48,0},{1,17},{17,33},{33,49},{49,1},{2,18}... | collective-permute-start | bytes 8257544 | tf_op jit(solution)/shard_map/ppermute | solution.py:280
  480.8 41.4 %collective-permute-start.2 = (bf16[896,512]{1,0:T(8,128)(2,1)S(1)}, bf16[896,512]{1,0:T(8,128)(2,1)S(1)}, u32[]{:S(2)}, u32[]{:S(2)}) collective-permute-start(bf16[896,512]{1,0:T(8,128)(2,1)S(1)} %copy-done.3), channel_id=1, source_target_pairs={{0,48},{16,0},{32,16},{48,32},{1,49},{17,1},{33,17},{49,33},{2,50}... | collective-permute-start | bytes 2752520 | tf_op jit(solution)/shard_map/ppermute | solution.py:282
  483.1 80.4 %collective-permute-start.1 = (bf16[896,512]{1,0:T(8,128)(2,1)S(1)}, bf16[896,512]{1,0:T(8,128)(2,1)S(1)}, u32[]{:S(2)}, u32[]{:S(2)}) collective-permute-start(bf16[896,512]{1,0:T(8,128)(2,1)S(1)} %copy-done.3), channel_id=1, source_target_pairs={{0,32},{16,48},{32,0},{48,16},{1,33},{17,49},{33,1},{49,17},{2,34}... | collective-permute-start | bytes 2752520 | tf_op jit(solution)/shard_map/ppermute | solution.py:282
  484.3 169.7 %collective-permute-start.4 = (bf16[2,896,768]{2,1,0:T(8,128)(2,1)}, bf16[2,896,768]{2,1,0:T(8,128)(2,1)}, u32[]{:S(2)}, u32[]{:S(2)}) collective-permute-start(bf16[2,896,768]{2,1,0:T(8,128)(2,1)} %get-tuple-element.24), channel_id=1, source_target_pairs={{0,32},{16,48},{32,0},{48,16},{1,33},{17,49},{33,1},{49,17},{2,34}... | collective-permute-start | bytes 8257544 | tf_op jit(solution)/shard_map/ppermute | solution.py:280
  519.2 78.1 %collective-permute-start.7 = (bf16[64,6144]{1,0:T(8,128)(2,1)S(1)}, bf16[64,6144]{1,0:T(8,128)(2,1)S(1)}, u32[]{:S(2)}, u32[]{:S(2)}) collective-permute-start(bf16[64,6144]{1,0:T(8,128)(2,1)S(1)} %convert_element_type.34), channel_id=1, source_target_pairs={{0,8},{8,0},{1,9},{9,1},{2,10},{10,2},{3,11},{11,3},{4,12},{12,4},... | collective-permute-start | bytes 2359304 | tf_op jit(solution)/shard_map/ppermute | solution.py:292
  522.3 176.1 %collective-permute-start.5 = (bf16[2,896,768]{2,1,0:T(8,128)(2,1)}, bf16[2,896,768]{2,1,0:T(8,128)(2,1)}, u32[]{:S(2)}, u32[]{:S(2)}) collective-permute-start(bf16[2,896,768]{2,1,0:T(8,128)(2,1)} %get-tuple-element.25), channel_id=1, source_target_pairs={{0,48},{16,0},{32,16},{48,32},{1,49},{17,1},{33,17},{49,33},{2,50}... | collective-permute-start | bytes 8257544 | tf_op jit(solution)/shard_map/ppermute | solution.py:280
  563.4 89.4 %collective-permute-start.18 = (bf16[256,2048]{1,0:T(8,128)(2,1)}, bf16[256,2048]{1,0:T(8,128)(2,1)}, u32[]{:S(2)}, u32[]{:S(2)}) collective-permute-start(bf16[256,2048]{1,0:T(8,128)(2,1)} %get-tuple-element.32), channel_id=1, source_target_pairs={{0,1},{1,0},{2,3},{3,2},{4,5},{5,4},{6,7},{7,6},{8,9},{9,8},{10,11... | collective-permute-start | bytes 3145736 | tf_op jit(solution)/shard_map/ppermute | solution.py:287
  597.3 45.6 %collective-permute-start = (bf16[896,512]{1,0:T(8,128)(2,1)S(1)}, bf16[896,512]{1,0:T(8,128)(2,1)}, u32[]{:S(2)}, u32[]{:S(2)}) collective-permute-start(bf16[896,512]{1,0:T(8,128)(2,1)S(1)} %copy-done.3), channel_id=1, source_target_pairs={{0,16},{16,32},{32,48},{48,0},{1,17},{17,33},{33,49},{49,1},{2,18}... | collective-permute-start | bytes 2752520 | tf_op jit(solution)/shard_map/ppermute | solution.py:282
  599.9 50.6 %all-to-all-start.1 = ((bf16[4,64,1536]{2,1,0:T(8,128)(2,1)}), bf16[4,64,1536]{2,1,0:T(8,128)(2,1)S(1)}, u32[]{:S(2)}, u32[]{:S(2)}) async-start(bf16[4,64,1536]{2,1,0:T(8,128)(2,1)} %copy-done.4), calls=%async_computation.1 | async-start | bytes 1572864 | tf_op jit(solution)/shard_map/all_to_all | solution.py:310
  650.6 17.9 %collective-permute-start.10 = (bf16[4,64,1536]{2,1,0:T(8,128)(2,1)S(1)}, bf16[4,64,1536]{2,1,0:T(8,128)(2,1)}, u32[]{:S(2)}, u32[]{:S(2)}) collective-permute-start(bf16[4,64,1536]{2,1,0:T(8,128)(2,1)S(1)} %all-to-all-done.1.refs_8_), channel_id=1, source_target_pairs={{0,6},{2,0},{4,2},{6,4},{1,7},{3,1},{5,3},{7,5},{8,14},{10,8},{12,... | collective-permute-start | bytes 2359304 | tf_op jit(solution)/shard_map/ppermute | solution.py:295
  652.8 34.6 %collective-permute-start.9 = (bf16[4,64,1536]{2,1,0:T(8,128)(2,1)S(1)}, bf16[4,64,1536]{2,1,0:T(8,128)(2,1)}, u32[]{:S(2)}, u32[]{:S(2)}) collective-permute-start(bf16[4,64,1536]{2,1,0:T(8,128)(2,1)S(1)} %all-to-all-done.1.refs_8_), channel_id=1, source_target_pairs={{0,4},{2,6},{4,0},{6,2},{1,5},{3,7},{5,1},{7,3},{8,12},{10,14},{12... | collective-permute-start | bytes 2359304 | tf_op jit(solution)/shard_map/ppermute | solution.py:295
  653.4 37.4 %collective-permute-start.8 = (bf16[4,64,1536]{2,1,0:T(8,128)(2,1)S(1)}, bf16[4,64,1536]{2,1,0:T(8,128)(2,1)}, u32[]{:S(2)}, u32[]{:S(2)}) collective-permute-start(bf16[4,64,1536]{2,1,0:T(8,128)(2,1)S(1)} %all-to-all-done.1.refs_8_), channel_id=1, source_target_pairs={{0,2},{2,4},{4,6},{6,0},{1,3},{3,5},{5,7},{7,1},{8,10},{10,12},{12... | collective-permute-start | bytes 2359304 | tf_op jit(solution)/shard_map/ppermute | solution.py:295
  654.0 45.8 %collective-permute-start.11 = (bf16[4,64,1536]{2,1,0:T(8,128)(2,1)S(1)}, bf16[4,64,1536]{2,1,0:T(8,128)(2,1)}, u32[]{:S(2)}, u32[]{:S(2)}) collective-permute-start(bf16[4,64,1536]{2,1,0:T(8,128)(2,1)S(1)} %all-to-all-done.1.refs_8_), channel_id=1, source_target_pairs={{0,1},{1,0},{2,3},{3,2},{4,5},{5,4},{6,7},{7,6},{8,9},{9,8},{10,11... | collective-permute-start | bytes 2359304 | tf_op jit(solution)/shard_map/ppermute | solution.py:296
  668.5 31.3 %collective-permute-start.14 = (bf16[4,64,1536]{2,1,0:T(8,128)(2,1)}, bf16[4,64,1536]{2,1,0:T(8,128)(2,1)}, u32[]{:S(2)}, u32[]{:S(2)}) collective-permute-start(bf16[4,64,1536]{2,1,0:T(8,128)(2,1)} %collective-permute-done.10.refs_11_), channel_id=1, source_target_pairs={{0,1},{1,0},{2,3},{3,2},{4,5},{5,4},{6,7},{7,6},{8,9},{9,8},{10,11... | collective-permute-start | bytes 2359304 | tf_op jit(solution)/shard_map/ppermute | solution.py:296
  694.1 19.6 %all-to-all-start.2 = ((bf16[4,64,2048]{2,1,0:T(8,128)(2,1)}), bf16[4,64,2048]{2,1,0:T(8,128)(2,1)}, u32[]{:S(2)}, u32[]{:S(2)}) async-start(bf16[4,64,2048]{2,1,0:T(8,128)(2,1)} %bitcast.26), calls=%async_computation.2 | async-start | bytes 2097152 | tf_op jit(solution)/shard_map/all_to_all | solution.py:288
  698.4 140.9 %collective-permute-start.17 = (bf16[4,896,256]{2,1,0:T(8,128)(2,1)}, bf16[4,896,256]{2,1,0:T(8,128)(2,1)}, u32[]{:S(2)}, u32[]{:S(2)}) collective-permute-start(bf16[4,896,256]{2,1,0:T(8,128)(2,1)} %get-tuple-element.30), channel_id=1, source_target_pairs={{0,64},{64,0},{1,65},{65,1},{2,66},{66,2},{3,67},{67,3},{4,68},{68... | collective-permute-start | bytes 5505032 | tf_op jit(solution)/shard_map/ppermute | solution.py:281
  708.6 195.5 %collective-permute-start.15 = (bf16[2,896,768]{2,1,0:T(8,128)(2,1)}, bf16[2,896,768]{2,1,0:T(8,128)(2,1)}, u32[]{:S(2)}, u32[]{:S(2)}) collective-permute-start(bf16[2,896,768]{2,1,0:T(8,128)(2,1)} %shard_map.59), channel_id=1, source_target_pairs={{0,64},{64,0},{1,65},{65,1},{2,66},{66,2},{3,67},{67,3},{4,68},{68... | collective-permute-start | bytes 8257544 | tf_op jit(solution)/shard_map/ppermute | solution.py:314
  708.7 129.9 %collective-permute-start.16 = (bf16[896,512]{1,0:T(8,128)(2,1)S(1)}, bf16[896,512]{1,0:T(8,128)(2,1)}, u32[]{:S(2)}, u32[]{:S(2)}) collective-permute-start(bf16[896,512]{1,0:T(8,128)(2,1)S(1)} %copy-done.3), channel_id=1, source_target_pairs={{0,64},{64,0},{1,65},{65,1},{2,66},{66,2},{3,67},{67,3},{4,68},{68... | collective-permute-start | bytes 2752520 | tf_op jit(solution)/shard_map/ppermute | solution.py:283
  715.2 111.9 %collective-permute-start.19 = (bf16[64,2048]{1,0:T(8,128)(2,1)S(1)}, bf16[64,2048]{1,0:T(8,128)(2,1)S(1)}, u32[]{:S(2)}, u32[]{:S(2)}) collective-permute-start(bf16[64,2048]{1,0:T(8,128)(2,1)S(1)} %convert_element_type.39), channel_id=1, source_target_pairs={{0,8},{8,0},{1,9},{9,1},{2,10},{10,2},{3,11},{11,3},{4,12},{12,4},... | collective-permute-start | bytes 786440 | tf_op jit(solution)/shard_map/ppermute | solution.py:292
  839.2 14.7 %collective-permute-start.24 = (bf16[2,64,1024]{2,1,0:T(8,128)(2,1)S(1)}, bf16[2,64,1024]{2,1,0:T(8,128)(2,1)S(1)}, u32[]{:S(2)}, u32[]{:S(2)}) collective-permute-start(bf16[2,64,1024]{2,1,0:T(8,128)(2,1)S(1)} %pad_maximum_fusion.refs_4_), channel_id=1, source_target_pairs={{0,1},{1,0},{2,3},{3,2},{4,5},{5,4},{6,7},{7,6},{8,9},{9,8},{10,11... | collective-permute-start | bytes 786440 | tf_op jit(solution)/shard_map/ppermute | solution.py:296
  861.2 42.5 %collective-permute-start.28 = (bf16[2,896,256]{2,1,0:T(8,128)(2,1)S(1)}, bf16[2,896,256]{2,1,0:T(8,128)(2,1)S(1)}, u32[]{:S(2)}, u32[]{:S(2)}) collective-permute-start(bf16[2,896,256]{2,1,0:T(8,128)(2,1)S(1)} %get-tuple-element.34), channel_id=1, source_target_pairs={{0,16},{16,32},{32,48},{48,0},{1,17},{17,33},{33,49},{49,1},{2,18}... | collective-permute-start | bytes 2752520 | tf_op jit(solution)/shard_map/ppermute | solution.py:316
  861.3 42.4 %collective-permute-start.29 = (bf16[2,896,256]{2,1,0:T(8,128)(2,1)S(1)}, bf16[2,896,256]{2,1,0:T(8,128)(2,1)S(1)}, u32[]{:S(2)}, u32[]{:S(2)}) collective-permute-start(bf16[2,896,256]{2,1,0:T(8,128)(2,1)S(1)} %get-tuple-element.35), channel_id=1, source_target_pairs={{0,32},{16,48},{32,0},{48,16},{1,33},{17,49},{33,1},{49,17},{2,34}... | collective-permute-start | bytes 2752520 | tf_op jit(solution)/shard_map/ppermute | solution.py:316
  862.3 41.7 %collective-permute-start.30 = (bf16[2,896,256]{2,1,0:T(8,128)(2,1)S(1)}, bf16[2,896,256]{2,1,0:T(8,128)(2,1)S(1)}, u32[]{:S(2)}, u32[]{:S(2)}) collective-permute-start(bf16[2,896,256]{2,1,0:T(8,128)(2,1)S(1)} %get-tuple-element.36), channel_id=1, source_target_pairs={{0,48},{16,0},{32,16},{48,32},{1,49},{17,1},{33,17},{49,33},{2,50}... | collective-permute-start | bytes 2752520 | tf_op jit(solution)/shard_map/ppermute | solution.py:316
  (22 other events, 366.8 us)

commit v3 on v2

v3 whole, which is shorter than its diff:
```python
import math

import jax
import jax.numpy as jnp
from jax import lax
from jax.experimental import pallas as pl
from jax.experimental.pallas import tpu as pltpu
from jax.sharding import Mesh
from jax.sharding import PartitionSpec as P

FF = 14336
TOK = 512
POOL = 1024
UNITS = 896
D = 8192
WIDE = 1024
WP = 768
WQ = WIDE - WP
VMEM = 56 * 2**20
SHRINK = 1.0 / math.sqrt(FF)
SWAP = [(0, 1), (1, 0)]
BF = jnp.bfloat16
F32 = jnp.float32
SMALL = pl.CostEstimate(flops=1, bytes_accessed=1, transcendentals=0)


def shift(k):
    return [(i, (i + k) % 4) for i in range(4)]


def shape(*dims, dtype=BF):
    return jax.ShapeDtypeStruct(dims, dtype)


def hidden_kernel(rows_ref, gate_ref, up_ref, hidden_ref, squares_ref):
    pool = lax.broadcasted_iota(jnp.int32, (TOK, POOL), 1)
    pick = jnp.where(rows_ref[...] == pool, 1.0, 0.0).astype(BF)
    gate = jnp.dot(pick, gate_ref[...], preferred_element_type=F32)
    up = jnp.dot(pick, up_ref[...], preferred_element_type=F32)
    hidden = (gate / (1.0 + jnp.exp(-gate)) * up).astype(BF)
    hidden_ref[...] = hidden
    wide = hidden.astype(F32)
    squares_ref[...] = (wide * wide).T.astype(BF)


def make_hidden(rows, gate, up):
    step = 128
    return pl.pallas_call(
        hidden_kernel,
        grid=(UNITS // step,),
        in_specs=[
            pl.BlockSpec((TOK, 1), lambda i: (0, 0)),
            pl.BlockSpec((POOL, step), lambda i: (0, i)),
            pl.BlockSpec((POOL, step), lambda i: (0, i)),
        ],
        out_specs=[
            pl.BlockSpec((TOK, step), lambda i: (0, i)),
            pl.BlockSpec((step, TOK), lambda i: (i, 0)),
        ],
        out_shape=[shape(TOK, UNITS), shape(UNITS, TOK)],
        compiler_params=pltpu.CompilerParams(vmem_limit_bytes=VMEM),
        cost_estimate=SMALL,
    )(rows, gate, up)


def cut_kernel(place_ref, squares_ref, *refs):
    near, far = refs[:3], refs[3:7]
    side, one, three, far_2, near_2 = refs[7:]
    squares = squares_ref[...]
    for out, dz in ((one, 1), (three, 3)):
        out[:, :WP] = far[dz][:, :WP]
        out[:, WP : 2 * WP] = near[dz - 1][:, :WP]
        out[:, 2 * WP :] = squares
    far_2[...] = far[2][:, :WP]
    near_2[...] = near[1][:, :WP]
    for dz in range(4):
        side[:, dz * WQ : dz * WQ + WQ] = far[dz][:, WP:]
    side[:, 4 * WQ :] = squares


def cut(place, squares, projection):
    step = 128

    def columns(dy, dz):
        return pl.BlockSpec((step, WIDE), lambda i, s: (i, lax.rem(s[0] + dy, 2) * 4 + lax.rem(s[1] + dz, 4)))

    def rows_of(width):
        return pl.BlockSpec((step, width), lambda i, s: (i, 0))

    widths = [4 * WQ + TOK, 2 * WP + TOK, 2 * WP + TOK, WP, WP]
    return pl.pallas_call(
        cut_kernel,
        grid_spec=pltpu.PrefetchScalarGridSpec(
            num_scalar_prefetch=1,
            grid=(UNITS // step,),
            in_specs=[rows_of(TOK)]
            + [columns(0, dz) for dz in (1, 2, 3)]
            + [columns(1, dz) for dz in (0, 1, 2, 3)],
            out_specs=[rows_of(width) for width in widths],
        ),
        out_shape=[shape(UNITS, width) for width in widths],
        compiler_params=pltpu.CompilerParams(vmem_limit_bytes=VMEM),
        cost_estimate=SMALL,
    )(place, squares, *[projection] * 7)


def partial_kernel(hidden_ref, w_low, w_high, own_p, other_p, own_q, other_q):
    hidden = hidden_ref[...]
    low = (jnp.dot(hidden, w_low[...], preferred_element_type=F32) * SHRINK).astype(BF)
    high = (jnp.dot(hidden, w_high[...], preferred_element_type=F32) * SHRINK).astype(BF)
    edge = WP - WIDE // 2
    for ref_p, ref_q, rows in ((own_p, own_q, slice(0, 256)), (other_p, other_q, slice(256, 512))):
        ref_p[:, : WIDE // 2] = low[rows]
        ref_p[:, WIDE // 2 :] = high[rows, :edge]
        ref_q[...] = high[rows, edge:]


def partial_outputs(hidden, projection):
    half = WIDE // 2
    return pl.pallas_call(
        partial_kernel,
        grid=(8,),
        in_specs=[
            pl.BlockSpec((TOK, UNITS), lambda j: (0, 0)),
            pl.BlockSpec((UNITS, half), lambda j: (0, 2 * j)),
            pl.BlockSpec((UNITS, half), lambda j: (0, 2 * j + 1)),
        ],
        out_specs=[pl.BlockSpec((256, WP), lambda j: (0, j))] * 2
        + [pl.BlockSpec((256, WQ), lambda j: (0, j))] * 2,
        out_shape=[shape(256, 8 * WP)] * 2 + [shape(256, 8 * WQ)] * 2,
        compiler_params=pltpu.CompilerParams(vmem_limit_bytes=VMEM),
        cost_estimate=SMALL,
    )(hidden, projection, projection)


def square_kernel(low, high, put, place_ref, total_ref, far_ref, targets_ref, out_ref):
    width = high - low
    for j in range(4):
        columns = slice(j * width, j * width + width)
        outputs = total_ref[:, columns] + far_ref[:, columns].astype(F32)
        wanted = targets_ref[:, j * WIDE + low : j * WIDE + high].astype(F32)
        errors = (outputs - wanted).astype(BF).astype(F32)
        put(place_ref, out_ref, j, (errors * errors).astype(BF))


def put_p(place_ref, out_ref, j, value):
    out_ref[j] = value


def put_q(place_ref, out_ref, j, value):
    first = lax.rem(j + 4 - place_ref[1], 4) * WQ
    out_ref[0, :, pl.ds(pl.multiple_of(first, 128), WQ)] = value


def error_squares(place, total, far, targets, low, high, out_shape, out_spec, put):
    width = high - low
    return pl.pallas_call(
        lambda *refs: square_kernel(low, high, put, *refs),
        grid_spec=pltpu.PrefetchScalarGridSpec(
            num_scalar_prefetch=1,
            grid=(2,),
            in_specs=[
                pl.BlockSpec((64, 4 * width), lambda j, s: (0, j)),
                pl.BlockSpec((64, 4 * width), lambda j, s: (0, j)),
                pl.BlockSpec((64, 4 * WIDE), lambda j, s: (s[3] * 4 + s[2], j)),
            ],
            out_specs=out_spec,
        ),
        out_shape=out_shape,
        compiler_params=pltpu.CompilerParams(vmem_limit_bytes=VMEM),
        cost_estimate=SMALL,
    )(place, total, far, targets)


def place_tokens(parts, scratch, member_of):
    for c, part in enumerate(parts):
        for place in range(4):
            row = c * 256 + place * 64
            for k in range(scratch.shape[0]):
                scratch[k, row : row + 64, :] = part[place, member_of(k)]


def sums(units, weights, squares, number):
    numerator = denominator = None
    for k in range(number):
        fisher = jnp.dot(units[k], squares(k), preferred_element_type=F32) * (1.0 / TOK)
        weighted = (fisher * weights(k).astype(F32)).astype(BF).astype(F32)
        term = fisher.astype(BF).astype(F32)
        numerator = weighted if numerator is None else numerator + weighted
        denominator = term if denominator is None else denominator + term
    return numerator, denominator


def set_p_kernel(place_ref, own_units, *refs):
    halves, weights, parts, out_ref, scratch = refs[:6], refs[6:10], refs[10:12], refs[12], refs[13]
    z = place_ref[1]

    @pl.when(pl.program_id(0) == 0)
    def _():
        place_tokens(parts, scratch, lambda k: lax.rem(z + 4 - k, 4))

    units = [own_units[...]]
    units += [jnp.concatenate([halves[2 * k][...], halves[2 * k + 1][...]], axis=1) for k in range(3)]
    numerator, denominator = sums(units, lambda k: weights[k][:, :WP], lambda k: scratch[k], 4)
    out_ref[0] = numerator.astype(out_ref.dtype)
    out_ref[1] = denominator.astype(out_ref.dtype)


def set_p(place, squares, one, u_2, three, weight_2, projection, parts, dy, dtype):
    tall = 224
    half = TOK // 2

    def halves(first):
        return [pl.BlockSpec((tall, half), lambda u, s, i=i: (u, first // half + i)) for i in (0, 1)]

    def columns(i):
        return pl.BlockSpec((tall, WP), lambda u, s: (u, i))

    return pl.pallas_call(
        set_p_kernel,
        grid_spec=pltpu.PrefetchScalarGridSpec(
            num_scalar_prefetch=1,
            grid=(UNITS // tall,),
            in_specs=[pl.BlockSpec((tall, TOK), lambda u, s: (u, 0))]
            + [*halves(2 * WP), *[pl.BlockSpec((tall, half), lambda u, s: (u, 0))] * 2, *halves(2 * WP)]
            + [pl.BlockSpec((tall, WIDE), lambda u, s: (u, lax.rem(s[0] + dy, 2) * 4 + s[1]))]
            + [columns(1 - dy), columns(0), columns(1 - dy)]
            + [pl.BlockSpec((4, 4, 64, WP), lambda u, s: (0, 0, 0, dy))] * 2,
            out_specs=pl.BlockSpec((2, tall, WP), lambda u, s: (0, u, 0)),
            scratch_shapes=[pltpu.VMEM((4, TOK, WP), BF)],
        ),
        out_shape=shape(2, UNITS, WP, dtype=dtype),
        compiler_params=pltpu.CompilerParams(vmem_limit_bytes=VMEM),
        cost_estimate=SMALL,
    )(place, squares, one, one, *u_2, three, three, projection, one, weight_2, three, *parts)


def set_q_kernel(place_ref, own_units, far_units, own_0, own_1, own_2, own_3, far_weights, *refs):
    own_weights = (own_0, own_1, own_2, own_3)
    parts, outs, scratch = refs[:2], refs[2:6], refs[6]

    @pl.when(pl.program_id(0) == 0)
    def _():
        place_tokens(parts, scratch, lambda k: k)

    for dz in (1, 2, 3, 0):
        columns = slice(dz * WQ, dz * WQ + WQ)
        weights = (own_weights[dz][:, WP:], far_weights[:, columns])
        numerator, denominator = sums(
            [own_units[...], far_units[...]], lambda k: weights[k], lambda k: scratch[k, :, columns], 2
        )
        outs[dz][0] = numerator.astype(outs[dz].dtype)
        outs[dz][1] = denominator.astype(outs[dz].dtype)


def set_q(place, units, projection, far, parts):
    tall = 224

    def own(dz):
        return pl.BlockSpec((tall, WIDE), lambda u, s: (u, s[0] * 4 + lax.rem(s[1] + dz, 4)))

    return pl.pallas_call(
        set_q_kernel,
        grid_spec=pltpu.PrefetchScalarGridSpec(
            num_scalar_prefetch=1,
            grid=(UNITS // tall,),
            in_specs=[
                pl.BlockSpec((tall, TOK), lambda u, s: (u, 0)),
                pl.BlockSpec((tall, TOK), lambda u, s: (u, 4 * WQ // TOK)),
            ]
            + [own(dz) for dz in range(4)]
            + [pl.BlockSpec((tall, 4 * WQ), lambda u, s: (u, 0))]
            + [pl.BlockSpec((4, 2, 64, 4 * WQ), lambda u, s: (0, 0, 0, 0))] * 2,
            out_specs=[pl.BlockSpec((2, tall, WQ), lambda u, s: (0, u, 0))] * 4,
            scratch_shapes=[pltpu.VMEM((2, TOK, 4 * WQ), BF)],
        ),
        out_shape=[shape(2, UNITS, WQ, dtype=F32)] + [shape(2, UNITS, WQ)] * 3,
        compiler_params=pltpu.CompilerParams(vmem_limit_bytes=VMEM),
        cost_estimate=SMALL,
    )(place, units, far, projection, projection, projection, projection, far, *parts)


def quotient_kernel(p_own, p_far, q_own, q_one, q_two, q_three, out_ref):
    def wide(ref, i):
        return ref[i].astype(F32)

    out_ref[:, :WP] = (p_own[0] + wide(p_far, 0)) / (p_own[1] + wide(p_far, 1) + 1e-06)
    numerator = q_own[0] + wide(q_one, 0) + wide(q_two, 0) + wide(q_three, 0)
    denominator = q_own[1] + wide(q_one, 1) + wide(q_two, 1) + wide(q_three, 1)
    out_ref[:, WP:] = numerator / (denominator + 1e-06)


def quotient(p_own, p_far, q_own, q_far):
    tall = 128
    return pl.pallas_call(
        quotient_kernel,
        grid=(UNITS // tall,),
        in_specs=[pl.BlockSpec((2, tall, WP), lambda u: (0, u, 0))] * 2
        + [pl.BlockSpec((2, tall, WQ), lambda u: (0, u, 0))] * 4,
        out_specs=pl.BlockSpec((tall, WIDE), lambda u: (u, 0)),
        out_shape=shape(UNITS, WIDE, dtype=F32),
        compiler_params=pltpu.CompilerParams(vmem_limit_bytes=VMEM),
        cost_estimate=SMALL,
    )(p_own, p_far, q_own, *q_far)


def body(token_rows, gate_cache, up_cache, down_weight, targets):
    y, z, x, core = (lax.axis_index(name) for name in ("y_lo", "z", "x", "core"))
    place = jnp.stack([y, z, x, core]).astype(jnp.int32)
    projection = down_weight[0]

    def send(value, axis, k=1):
        return lax.ppermute(value, axis, shift(k) if axis in ("z", "x") else SWAP)

    together = lax.optimization_barrier

    picked = token_rows[0].reshape(2, TOK // 2)
    picked = jnp.where(core == 1, picked[::-1], picked).reshape(TOK, 1)
    hidden, squares = make_hidden(picked, gate_cache[0], up_cache[0])

    own_p, other_p, own_q, other_q = partial_outputs(hidden, projection)
    other_p, squares = together((other_p, squares))
    side, one, three, far_2, near_2 = cut(place, squares, projection)
    one, three, side = send(one, "z", 1), send(three, "z", 3), send(side, "y_lo")

    def pair(own, other):
        both = (own.astype(F32) + send(other, "core").astype(F32)).astype(BF)
        return both.reshape(4, 64, -1)

    def over_x(blocks):
        return lax.all_to_all(blocks, "x", 0, 0, tiled=True)

    def total(blocks):
        return jnp.sum(blocks.astype(F32), axis=0)

    def gathered(part):
        return over_x(jnp.broadcast_to(part[None], (4,) + part.shape))

    blocks_p = over_x(pair(own_p, other_p))
    pair_q = pair(own_q, other_q)
    blocks_p, pair_q = together((blocks_p, pair_q))
    total_p = total(blocks_p)
    half_p, side = together((total_p.astype(BF), side))
    far_p = send(half_p, "y_hi")
    total_q = total(over_x(pair_q))
    squares_p = error_squares(
        place, total_p, far_p, targets[0], 0, WP, shape(4, 64, 2 * WP),
        pl.BlockSpec((4, 64, WP), lambda j, s: (0, 0, lax.rem(j + s[0], 2))), put_p,
    )
    squares_p, one, three, total_q = together((squares_p, one, three, total_q))
    far_q = send(total_q.astype(BF), "y_hi")
    mine_p = lax.all_to_all(squares_p, "z", 0, 0, tiled=True)
    middle = 2 * WP + TOK // 2
    u_2 = (one[:, 2 * WP : middle], three[:, middle:])
    mine_p, far_q, far_2, u_2 = together((mine_p, far_q, far_2, u_2))

    u_2 = (send(u_2[0], "z", 1), send(u_2[1], "z", 3))
    far_2 = send(far_2, "z", 2)
    row_p = gathered(mine_p)
    squares_q = error_squares(
        place, total_q, far_q, targets[0], WP, WIDE, shape(2, 64, 4 * WQ),
        pl.BlockSpec((1, 64, 4 * WQ), lambda j, s: (lax.rem(j + s[0], 2), 0, 0)), put_q,
    )
    mine_q = jnp.stack([squares_q[0], send(squares_q[1], "y_lo")])
    row_p, far_2, u_2, mine_q, near_2 = together((row_p, far_2, u_2, mine_q, near_2))

    near_2 = send(near_2, "z", 2)
    parts_p = [row_p, send(row_p, "core")]
    p_far = send(set_p(place, squares, one, u_2, three, far_2, projection, parts_p, 1, BF), "y_lo")
    row_q = gathered(mine_q)
    parts_q = [row_q, send(row_q, "core")]
    q_sums = set_q(place, squares, projection, side, parts_q)
    q_sums, near_2 = together((q_sums, near_2))
    q_own, *q_send = q_sums
    q_far = [send(q, "z", k + 1) for k, q in enumerate(q_send)]
    p_own = set_p(place, squares, one, u_2, three, near_2, projection, parts_p, 0, F32)
    return quotient(p_own, p_far, q_own, q_far)


def solution(mesh):
    cut = Mesh(mesh.devices.reshape(2, 4, 2, 4, 2), ("y_lo", "z", "y_hi", "x", "core"))
    ft, tp = ("y_lo", "z"), ("y_hi", "x", "core")
    placed = (P(ft, None), P(ft, None, tp), P(ft, None, tp), P(ft, tp, None), P(ft, None, None))
    return jax.shard_map(body, mesh=cut, in_specs=placed, out_specs=P(tp, ft), check_vma=False)
```

time: 914 us -> 300 us (0.33)
  Pallas kernels: 503 us -> 81.1 us
  waiting for transfers between devices: 275 us -> 142 us
  starting transfers between devices: 112 us -> 46.3 us
    pallas_call x5, Pallas kernels: 473 us -> 42.4 us  [the longest x1 14.7 us: partial_outputs(): pl.pallas_call(partial_kernel, grid=(8,), in_specs=[pl.BlockSpec((TOK, UN...]
    ppermute x31 -> x18, waiting for transfers between devices: 233 us -> 106 us  [send(): return lax.ppermute(value, axis, shift(k) if axis in ('z', 'x') else SWAP)]
    ppermute x31 -> x18, starting transfers between devices: 99.3 us -> 25 us  [send(): return lax.ppermute(value, axis, shift(k) if axis in ('z', 'x') else SWAP)]
    all_to_all x3 -> x5, starting transfers between devices: 13 us -> 21.4 us  [the longest x4 16.3 us: over_x(): return lax.all_to_all(blocks, 'x', 0, 0, tiled=True)]
    all_to_all x3 -> x5, waiting for transfers between devices: 41.7 us -> 36.4 us  [the longest x4 33.9 us: over_x(): return lax.all_to_all(blocks, 'x', 0, 0, tiled=True)]
  transfers between devices with their start and end apart: 34 -> 23, of which waited for: 14 -> 14; matrix products, arithmetic and copies ran while one was open for 1% -> 5% of each run, Pallas kernels for 4% -> 17%
where the time goes in v3:
time: 300 us; the launch traced here: 298 us
  waiting for transfers between devices  142 us (47%)
  Pallas kernels  81.1 us (27%)
  starting transfers between devices  46.3 us (15%)
  local copies, waits for them, and re-layouts  17.3 us (6%)
  other arithmetic  11.3 us (4%)
    ppermute x18, waiting for transfers between devices, send(): return lax.ppermute(value, axis, shift(k) if axis in ('z', 'x') else SWAP)  106 us
    all_to_all x4, waiting for transfers between devices, over_x(): return lax.all_to_all(blocks, 'x', 0, 0, tiled=True)  33.9 us
    ppermute x18, starting transfers between devices, send(): return lax.ppermute(value, axis, shift(k) if axis in ('z', 'x') else SWAP)  25 us
    pallas_call x2, Pallas kernels, set_p(): pl.pallas_call(set_p_kernel, grid_spec=pltpu.PrefetchScalarGridSpec(num_s...  20.3 us
    all_to_all x4, starting transfers between devices, over_x(): return lax.all_to_all(blocks, 'x', 0, 0, tiled=True)  16.3 us
    pallas_call x1, Pallas kernels, partial_outputs(): pl.pallas_call(partial_kernel, grid=(8,), in_specs=[pl.BlockSpec((TOK, UN...  14.7 us
    pallas_call x1, Pallas kernels, cut(): pl.pallas_call(cut_kernel, grid_spec=pltpu.PrefetchScalarGridSpec(num_sca...  12.8 us
    pallas_call x1, Pallas kernels, set_q(): pl.pallas_call(set_q_kernel, grid_spec=pltpu.PrefetchScalarGridSpec(num_s...  9.83 us
  transfers between devices with their start and end apart: 23, of which 14 were waited for; matrix products, arithmetic and copies ran while one was open for 5% of the time, Pallas kernels for 17%

profile of v3, /device:TPU:1, one launch (start us, length us, event | category | flops | bytes accessed | tf_op | source)
XLA Modules:
  0.0 298.0 jit_solution(11826071280330336130)
XLA Ops:
  2.8 8.5 %shard_map.55 = (bf16[512,896]{1,0:T(8,128)(2,1)}, bf16[896,512]{1,0:T(8,128)(2,1)}) custom-call(s32[512,1]{1,0:T(8,128)} %bitcast.38, bf16[1024,896]{1,0:T(8,128)(2,1)} %bitcast.36, bf16[1024,896]{1,0:T(8,128)(2,1)} %bitcast.37), custom_call_target="tpu_custom_call" | custom-call | flops 1 | bytes 1 | tf_op jit(solution)/shard_map/pallas_call | solution.py:48
  11.4 14.7 %shard_map.56 = (bf16[256,6144]{1,0:T(8,128)(2,1)}, bf16[256,6144]{1,0:T(8,128)(2,1)}, bf16[256,2048]{1,0:T(8,128)(2,1)}, bf16[256,2048]{1,0:T(8,128)(2,1)}) custom-call(bf16[512,896]{1,0:T(8,128)(2,1)} %get-tuple-element.46.hidden_ref, bf16[896,8192]{1,0:T(8,128)(2,1)} %bitcast.18, bf16[896,8192]{1,0:T(8,128)(2,1)} %bitcast.19), custom_call_target="tpu_custom_call" | custom-call | flops 1 | bytes 1 | tf_op jit(solution)/shard_map/pallas_call | solution.py:120
  28.1 12.8 %shard_map.57 = (bf16[896,1536]{1,0:T(8,128)(2,1)}, bf16[896,2048]{1,0:T(8,128)(2,1)}, bf16[896,2048]{1,0:T(8,128)(2,1)}, bf16[896,768]{1,0:T(8,128)(2,1)}, bf16[896,768]{1,0:T(8,128)(2,1)}) custom-call(s32[4]{0:T(128)} %pad_add_fusion.place_ref.refs_0_, bf16[896,512]{1,0:T(8,128)(2,1)} %get-tuple-element.49.squares_ref.own_units, ...), custom_call_target="tpu_custom_call" | custom-call | flops 1 | bytes 1 | tf_op jit(solution)/shard_map/pallas_call | solution.py:91
  49.0 4.0 %all-to-all-start = ((bf16[4,64,6144]{2,1,0:T(8,128)(2,1)}), bf16[4,64,6144]{2,1,0:T(8,128)(2,1)S(1)}, u32[]{:S(2)}, u32[]{:S(2)}) async-start(bf16[4,64,6144]{2,1,0:T(8,128)(2,1)} %bitcast.35), calls=%async_computation | async-start | bytes 6291456 | tf_op jit(solution)/shard_map/all_to_all | solution.py:331
  58.9 30.8 %all-to-all-done = bf16[4,64,6144]{2,1,0:T(8,128)(2,1)S(1)} async-done(((bf16[4,64,6144]{2,1,0:T(8,128)(2,1)}), bf16[4,64,6144]{2,1,0:T(8,128)(2,1)S(1)}, u32[]{:S(2)}, u32[]{:S(2)}) %all-to-all-start) | async-done | bytes 3145760 | tf_op jit(solution)/shard_map/all_to_all | solution.py:331
  95.1 7.5 %collective-permute-done.2.far_units.far_weights = bf16[896,1536]{1,0:T(8,128)(2,1)} collective-permute-done((bf16[896,1536]{1,0:T(8,128)(2,1)}, bf16[896,1536]{1,0:T(8,128)(2,1)}, u32[]{:S(2)}, u32[]{:S(2)}) %collective-permute-start.2) | collective-permute-done | bytes 2752544 | tf_op jit(solution)/shard_map/ppermute | solution.py:313
  102.6 3.0 %collective-permute-start.3 = (bf16[64,6144]{1,0:T(8,128)(2,1)}, bf16[64,6144]{1,0:T(8,128)(2,1)S(1)}, u32[]{:S(2)}, u32[]{:S(2)}) collective-permute-start(bf16[64,6144]{1,0:T(8,128)(2,1)} %convert_element_type.37), channel_id=1, source_target_pairs={{0,8},{8,0},{1,9},{9,1},{2,10},{10,2},{3,11},{11,3},{4,12},{12,4},... | collective-permute-start | bytes 2359304 | tf_op jit(solution)/shard_map/ppermute | solution.py:313
  105.6 4.0 %all-to-all-start.1 = ((bf16[4,64,2048]{2,1,0:T(8,128)(2,1)}), bf16[4,64,2048]{2,1,0:T(8,128)(2,1)S(1)}, u32[]{:S(2)}, u32[]{:S(2)}) async-start(bf16[4,64,2048]{2,1,0:T(8,128)(2,1)} %bitcast.8), calls=%async_computation.1 | async-start | bytes 2097152 | tf_op jit(solution)/shard_map/all_to_all | solution.py:331
  109.6 13.0 %collective-permute-done.3.refs_2_ = bf16[64,6144]{1,0:T(8,128)(2,1)S(1)} collective-permute-done((bf16[64,6144]{1,0:T(8,128)(2,1)}, bf16[64,6144]{1,0:T(8,128)(2,1)S(1)}, u32[]{:S(2)}, u32[]{:S(2)}) %collective-permute-start.3) | collective-permute-done | bytes 786464 | tf_op jit(solution)/shard_map/ppermute | solution.py:313
  123.5 3.6 %shard_map.58 = bf16[4,64,1536]{2,1,0:T(8,128)(2,1)} custom-call(s32[4]{0:T(128)} %pad_add_fusion.place_ref.refs_0_, f32[64,6144]{1,0:T(8,128)} %copy-done.1, bf16[64,6144]{1,0:T(8,128)(2,1)} %copy-done.12, bf16[512,8192]{1,0:T(8,128)(2,1)} %bitcast.33), custom_call_target="tpu_custom_call" | custom-call | flops 1 | bytes 1 | tf_op jit(solution)/shard_map/pallas_call | solution.py:157
  127.3 5.1 %all-to-all-start.2 = ((bf16[4,64,1536]{2,1,0:T(8,128)(2,1)}), bf16[4,64,1536]{2,1,0:T(8,128)(2,1)S(1)}, u32[]{:S(2)}, u32[]{:S(2)}) async-start(bf16[4,64,1536]{2,1,0:T(8,128)(2,1)} %shard_map.58), calls=%async_computation.2 | async-start | bytes 1572864 | tf_op jit(solution)/shard_map/all_to_all | solution.py:352
  132.4 3.1 %collective-permute-start.6 = (bf16[64,2048]{1,0:T(8,128)(2,1)S(1)}, bf16[64,2048]{1,0:T(8,128)(2,1)S(1)}, u32[]{:S(2)}, u32[]{:S(2)}) collective-permute-start(bf16[64,2048]{1,0:T(8,128)(2,1)S(1)} %convert_element_type.39), channel_id=1, source_target_pairs={{0,8},{8,0},{1,9},{9,1},{2,10},{10,2},{3,11},{11,3},{4,12},{12,4},... | collective-permute-start | bytes 786440 | tf_op jit(solution)/shard_map/ppermute | solution.py:313
  144.4 4.0 %all-to-all-start.3 = ((bf16[4,4,64,1536]{3,2,1,0:T(8,128)(2,1)}), bf16[4,4,64,1536]{3,2,1,0:T(8,128)(2,1)S(1)}, u32[]{:S(2)}, u32[]{:S(2)}) async-start(bf16[4,4,64,1536]{3,2,1,0:T(8,128)(2,1)} %broadcast_in_dim.4), calls=%async_computation.3 | async-start | bytes 6291456 | tf_op jit(solution)/shard_map/all_to_all | solution.py:331
  149.0 2.9 shard_map.59
  160.0 32.1 %collective-permute-done.8.refs_2_ = bf16[896,256]{1,0:T(8,128)(2,1)S(1)} collective-permute-done((bf16[896,256]{1,0:T(8,128)(2,1)S(1)}, bf16[896,256]{1,0:T(8,128)(2,1)S(1)}, u32[]{:S(2)}, u32[]{:S(2)}) %collective-permute-start.8) | collective-permute-done | bytes 458784 | tf_op jit(solution)/shard_map/ppermute | solution.py:313
  195.7 4.3 %all-to-all-start.4 = ((bf16[4,2,64,1024]{3,2,1,0:T(8,128)(2,1)}), bf16[4,2,64,1024]{3,2,1,0:T(8,128)(2,1)}, u32[]{:S(2)}, u32[]{:S(2)}) async-start(bf16[4,2,64,1024]{3,2,1,0:T(8,128)(2,1)} %broadcast_in_dim.5), calls=%async_computation.4 | async-start | bytes 2097152 | tf_op jit(solution)/shard_map/all_to_all | solution.py:331
  200.0 9.8 %shard_map.62 = bf16[2,896,768]{2,1,0:T(8,128)(2,1)} custom-call(s32[4]{0:T(128)} %pad_add_fusion.place_ref.refs_0_, bf16[896,512]{1,0:T(8,128)(2,1)} %get-tuple-element.49.squares_ref.own_units, bf16[896,2048]{1,0:T(8,128)(2,1)} %collective-permute-done.4.refs_0_.refs_1_.refs_7_, bf16[896,2048]{1,0:T(8,128)(2,1)} %collective-permute-done.4.refs_0_.refs_1_.refs_7_, ...), custom_call_target="tpu_custom_call" | custom-call | flops 1 | bytes 1 | tf_op jit(solution)/shard_map/pallas_call | solution.py:219
  212.0 3.1 %all-to-all-done.4.refs_0_ = bf16[4,2,64,1024]{3,2,1,0:T(8,128)(2,1)} async-done(((bf16[4,2,64,1024]{3,2,1,0:T(8,128)(2,1)}), bf16[4,2,64,1024]{3,2,1,0:T(8,128)(2,1)}, u32[]{:S(2)}, u32[]{:S(2)}) %all-to-all-start.4) | async-done | bytes 1048608 | tf_op jit(solution)/shard_map/all_to_all | solution.py:331
  219.7 9.8 %shard_map.60 = (f32[2,896,256]{2,1,0:T(8,128)}, bf16[2,896,256]{2,1,0:T(8,128)(2,1)}, bf16[2,896,256]{2,1,0:T(8,128)(2,1)}, bf16[2,896,256]{2,1,0:T(8,128)(2,1)}) custom-call(s32[4]{0:T(128)} %pad_add_fusion.place_ref.refs_0_, bf16[896,512]{1,0:T(8,128)(2,1)} %get-tuple-element.49.squares_ref.own_units, ...), custom_call_target="tpu_custom_call" | custom-call | flops 1 | bytes 1 | tf_op jit(solution)/shard_map/pallas_call | solution.py:262
  229.5 15.1 %collective-permute-done.12.refs_8_ = bf16[896,768]{1,0:T(8,128)(2,1)} collective-permute-done((bf16[896,768]{1,0:T(8,128)(2,1)}, bf16[896,768]{1,0:T(8,128)(2,1)}, u32[]{:S(2)}, u32[]{:S(2)}) %collective-permute-start.12) | collective-permute-done | bytes 1376288 | tf_op jit(solution)/shard_map/ppermute | solution.py:313
  247.3 10.5 %shard_map.61.p_own = f32[2,896,768]{2,1,0:T(8,128)} custom-call(s32[4]{0:T(128)} %pad_add_fusion.place_ref.refs_0_, bf16[896,512]{1,0:T(8,128)(2,1)} %get-tuple-element.49.squares_ref.own_units, bf16[896,2048]{1,0:T(8,128)(2,1)} %collective-permute-done.4.refs_0_.refs_1_.refs_7_, bf16[896,2048]{1,0:T(8,128)(2,1)} %collective-permute-done.4.refs_0_.refs_1_.refs_7_, ...), custom_call_target="tpu_custom_call" | custom-call | flops 1 | bytes 1 | tf_op jit(solution)/shard_map/pallas_call | solution.py:219
  257.8 10.7 %collective-permute-done.15.q_one = bf16[2,896,256]{2,1,0:T(8,128)(2,1)S(1)} collective-permute-done((bf16[2,896,256]{2,1,0:T(8,128)(2,1)}, bf16[2,896,256]{2,1,0:T(8,128)(2,1)S(1)}, u32[]{:S(2)}, u32[]{:S(2)}) %collective-permute-start.15) | collective-permute-done | bytes 917536 | tf_op jit(solution)/shard_map/ppermute | solution.py:313
  268.5 15.9 %collective-permute-done.16.q_two = bf16[2,896,256]{2,1,0:T(8,128)(2,1)S(1)} collective-permute-done((bf16[2,896,256]{2,1,0:T(8,128)(2,1)}, bf16[2,896,256]{2,1,0:T(8,128)(2,1)S(1)}, u32[]{:S(2)}, u32[]{:S(2)}) %collective-permute-start.16) | collective-permute-done | bytes 917536 | tf_op jit(solution)/shard_map/ppermute | solution.py:313
  289.5 8.6 %shard_map.63 = f32[896,1024]{1,0:T(8,128)} custom-call(f32[2,896,768]{2,1,0:T(8,128)} %shard_map.61.p_own, bf16[2,896,768]{2,1,0:T(8,128)(2,1)} %copy-done.5, f32[2,896,256]{2,1,0:T(8,128)} %get-tuple-element.83.q_own, bf16[2,896,256]{2,1,0:T(8,128)(2,1)} %copy-done.9, bf16[2,896,256]{2,1,0:T(8,128)(2,1)} %copy-done.10, bf16[2,896,256]{2,1,0:T(8,128)(2,1)} %copy-done.11), custom_call_target="tpu_custom_call" | custom-call | flops 1 | bytes 1 | tf_op jit(solution)/shard_map/pallas_call | solution.py:295
  (83 shorter events, 61.1 us)
Async XLA Ops:
  26.0 20.1 %collective-permute-start = (bf16[256,6144]{1,0:T(8,128)(2,1)}, bf16[256,6144]{1,0:T(8,128)(2,1)S(1)}, u32[]{:S(2)}, u32[]{:S(2)}) collective-permute-start(bf16[256,6144]{1,0:T(8,128)(2,1)} %get-tuple-element.51), channel_id=1, source_target_pairs={{0,1},{1,0},{2,3},{3,2},{4,5},{5,4},{6,7},{7,6},{8,9},{9,8},{10,11... | collective-permute-start | bytes 9437192 | tf_op jit(solution)/shard_map/ppermute | solution.py:313
  40.9 61.7 %collective-permute-start.2 = (bf16[896,1536]{1,0:T(8,128)(2,1)}, bf16[896,1536]{1,0:T(8,128)(2,1)}, u32[]{:S(2)}, u32[]{:S(2)}) collective-permute-start(bf16[896,1536]{1,0:T(8,128)(2,1)} %get-tuple-element.55), channel_id=1, source_target_pairs={{0,64},{64,0},{1,65},{65,1},{2,66},{66,2},{3,67},{67,3},{4,68},{68... | collective-permute-start | bytes 8257544 | tf_op jit(solution)/shard_map/ppermute | solution.py:313
  42.3 85.0 %collective-permute-start.4 = (bf16[896,2048]{1,0:T(8,128)(2,1)}, bf16[896,2048]{1,0:T(8,128)(2,1)}, u32[]{:S(2)}, u32[]{:S(2)}) collective-permute-start(bf16[896,2048]{1,0:T(8,128)(2,1)} %get-tuple-element.57), channel_id=1, source_target_pairs={{0,16},{16,32},{32,48},{48,0},{1,17},{17,33},{33,49},{49,1},{2,18}... | collective-permute-start | bytes 11010056 | tf_op jit(solution)/shard_map/ppermute | solution.py:313
  44.0 83.3 %collective-permute-start.5 = (bf16[896,2048]{1,0:T(8,128)(2,1)}, bf16[896,2048]{1,0:T(8,128)(2,1)}, u32[]{:S(2)}, u32[]{:S(2)}) collective-permute-start(bf16[896,2048]{1,0:T(8,128)(2,1)} %get-tuple-element.58), channel_id=1, source_target_pairs={{0,48},{16,0},{32,16},{48,32},{1,49},{17,1},{33,17},{49,33},{2,50}... | collective-permute-start | bytes 11010056 | tf_op jit(solution)/shard_map/ppermute | solution.py:313
  49.0 40.8 %all-to-all-start = ((bf16[4,64,6144]{2,1,0:T(8,128)(2,1)}), bf16[4,64,6144]{2,1,0:T(8,128)(2,1)S(1)}, u32[]{:S(2)}, u32[]{:S(2)}) async-start(bf16[4,64,6144]{2,1,0:T(8,128)(2,1)} %bitcast.35), calls=%async_computation | async-start | bytes 6291456 | tf_op jit(solution)/shard_map/all_to_all | solution.py:331
  53.0 3.4 %collective-permute-start.1 = (bf16[256,2048]{1,0:T(8,128)(2,1)}, bf16[256,2048]{1,0:T(8,128)(2,1)S(1)}, u32[]{:S(2)}, u32[]{:S(2)}) collective-permute-start(bf16[256,2048]{1,0:T(8,128)(2,1)} %get-tuple-element.53), channel_id=1, source_target_pairs={{0,1},{1,0},{2,3},{3,2},{4,5},{5,4},{6,7},{7,6},{8,9},{9,8},{10,11... | collective-permute-start | bytes 3145736 | tf_op jit(solution)/shard_map/ppermute | solution.py:313
  94.0 28.7 %copy-start.1 = (f32[64,6144]{1,0:T(8,128)}, f32[64,6144]{1,0:T(8,128)S(1)}, u32[]{:S(2)}) copy-start(f32[64,6144]{1,0:T(8,128)S(1)} %convert_reduce_fusion.refs_1_) | copy-start | bytes 4718596
  102.6 20.0 %collective-permute-start.3 = (bf16[64,6144]{1,0:T(8,128)(2,1)}, bf16[64,6144]{1,0:T(8,128)(2,1)S(1)}, u32[]{:S(2)}, u32[]{:S(2)}) collective-permute-start(bf16[64,6144]{1,0:T(8,128)(2,1)} %convert_element_type.37), channel_id=1, source_target_pairs={{0,8},{8,0},{1,9},{9,1},{2,10},{10,2},{3,11},{11,3},{4,12},{12,4},... | collective-permute-start | bytes 2359304 | tf_op jit(solution)/shard_map/ppermute | solution.py:313
  105.6 21.6 %all-to-all-start.1 = ((bf16[4,64,2048]{2,1,0:T(8,128)(2,1)}), bf16[4,64,2048]{2,1,0:T(8,128)(2,1)S(1)}, u32[]{:S(2)}, u32[]{:S(2)}) async-start(bf16[4,64,2048]{2,1,0:T(8,128)(2,1)} %bitcast.8), calls=%async_computation.1 | async-start | bytes 2097152 | tf_op jit(solution)/shard_map/all_to_all | solution.py:331
  127.3 15.1 %all-to-all-start.2 = ((bf16[4,64,1536]{2,1,0:T(8,128)(2,1)}), bf16[4,64,1536]{2,1,0:T(8,128)(2,1)S(1)}, u32[]{:S(2)}, u32[]{:S(2)}) async-start(bf16[4,64,1536]{2,1,0:T(8,128)(2,1)} %shard_map.58), calls=%async_computation.2 | async-start | bytes 1572864 | tf_op jit(solution)/shard_map/all_to_all | solution.py:352
  132.4 7.5 %collective-permute-start.6 = (bf16[64,2048]{1,0:T(8,128)(2,1)S(1)}, bf16[64,2048]{1,0:T(8,128)(2,1)S(1)}, u32[]{:S(2)}, u32[]{:S(2)}) collective-permute-start(bf16[64,2048]{1,0:T(8,128)(2,1)S(1)} %convert_element_type.39), channel_id=1, source_target_pairs={{0,8},{8,0},{1,9},{9,1},{2,10},{10,2},{3,11},{11,3},{4,12},{12,4},... | collective-permute-start | bytes 786440 | tf_op jit(solution)/shard_map/ppermute | solution.py:313
  144.4 49.2 %all-to-all-start.3 = ((bf16[4,4,64,1536]{3,2,1,0:T(8,128)(2,1)}), bf16[4,4,64,1536]{3,2,1,0:T(8,128)(2,1)S(1)}, u32[]{:S(2)}, u32[]{:S(2)}) async-start(bf16[4,4,64,1536]{3,2,1,0:T(8,128)(2,1)} %broadcast_in_dim.4), calls=%async_computation.3 | async-start | bytes 6291456 | tf_op jit(solution)/shard_map/all_to_all | solution.py:331
  148.4 45.2 %collective-permute-start.7 = (bf16[896,768]{1,0:T(8,128)(2,1)}, bf16[896,768]{1,0:T(8,128)(2,1)}, u32[]{:S(2)}, u32[]{:S(2)}) collective-permute-start(bf16[896,768]{1,0:T(8,128)(2,1)} %get-tuple-element.66), channel_id=1, source_target_pairs={{0,32},{16,48},{32,0},{48,16},{1,33},{17,49},{33,1},{49,17},{2,34}... | collective-permute-start | bytes 4128776 | tf_op jit(solution)/shard_map/ppermute | solution.py:313
  151.9 40.2 %collective-permute-start.8 = (bf16[896,256]{1,0:T(8,128)(2,1)S(1)}, bf16[896,256]{1,0:T(8,128)(2,1)S(1)}, u32[]{:S(2)}, u32[]{:S(2)}) collective-permute-start(bf16[896,256]{1,0:T(8,128)(2,1)S(1)} %copy-done.14), channel_id=1, source_target_pairs={{0,16},{16,32},{32,48},{48,0},{1,17},{17,33},{33,49},{49,1},{2,18}... | collective-permute-start | bytes 1376264 | tf_op jit(solution)/shard_map/ppermute | solution.py:313
  153.1 39.0 %collective-permute-start.9 = (bf16[896,256]{1,0:T(8,128)(2,1)S(1)}, bf16[896,256]{1,0:T(8,128)(2,1)S(1)}, u32[]{:S(2)}, u32[]{:S(2)}) collective-permute-start(bf16[896,256]{1,0:T(8,128)(2,1)S(1)} %copy-done.13), channel_id=1, source_target_pairs={{0,48},{16,0},{32,16},{48,32},{1,49},{17,1},{33,17},{49,33},{2,50}... | collective-permute-start | bytes 1376264 | tf_op jit(solution)/shard_map/ppermute | solution.py:313
  155.6 4.4 %collective-permute-start.10 = (bf16[64,1024]{1,0:T(8,128)(2,1)S(1)}, bf16[64,1024]{1,0:T(8,128)(2,1)S(1)}, u32[]{:S(2)}, u32[]{:S(2)}) collective-permute-start(bf16[64,1024]{1,0:T(8,128)(2,1)S(1)} %get-tuple-element.88), channel_id=1, source_target_pairs={{0,64},{64,0},{1,65},{65,1},{2,66},{66,2},{3,67},{67,3},{4,68},{68... | collective-permute-start | bytes 393224 | tf_op jit(solution)/shard_map/ppermute | solution.py:313
  193.6 6.4 %collective-permute-start.13 = (bf16[4,4,64,1536]{3,2,1,0:T(8,128)(2,1)S(1)}, bf16[4,4,64,1536]{3,2,1,0:T(8,128)(2,1)}, u32[]{:S(2)}, u32[]{:S(2)}) collective-permute-start(bf16[4,4,64,1536]{3,2,1,0:T(8,128)(2,1)S(1)} %all-to-all-done.3.refs_10_), channel_id=1, source_target_pairs={{0,1},{1,0},{2,3},{3,2},{4,5},{5,4},{6,7},{7,6},{8,9},{9,8},{10,11... | collective-permute-start | bytes 9437192 | tf_op jit(solution)/shard_map/ppermute | solution.py:313
  195.7 19.4 %all-to-all-start.4 = ((bf16[4,2,64,1024]{3,2,1,0:T(8,128)(2,1)}), bf16[4,2,64,1024]{3,2,1,0:T(8,128)(2,1)}, u32[]{:S(2)}, u32[]{:S(2)}) async-start(bf16[4,2,64,1024]{3,2,1,0:T(8,128)(2,1)} %broadcast_in_dim.5), calls=%async_computation.4 | async-start | bytes 2097152 | tf_op jit(solution)/shard_map/all_to_all | solution.py:331
  209.8 77.2 %collective-permute-start.14 = (bf16[2,896,768]{2,1,0:T(8,128)(2,1)}, bf16[2,896,768]{2,1,0:T(8,128)(2,1)S(1)}, u32[]{:S(2)}, u32[]{:S(2)}) collective-permute-start(bf16[2,896,768]{2,1,0:T(8,128)(2,1)} %shard_map.62), channel_id=1, source_target_pairs={{0,64},{64,0},{1,65},{65,1},{2,66},{66,2},{3,67},{67,3},{4,68},{68... | collective-permute-start | bytes 8257544 | tf_op jit(solution)/shard_map/ppermute | solution.py:313
  211.5 33.1 %collective-permute-start.12 = (bf16[896,768]{1,0:T(8,128)(2,1)}, bf16[896,768]{1,0:T(8,128)(2,1)}, u32[]{:S(2)}, u32[]{:S(2)}) collective-permute-start(bf16[896,768]{1,0:T(8,128)(2,1)} %get-tuple-element.79), channel_id=1, source_target_pairs={{0,32},{16,48},{32,0},{48,16},{1,33},{17,49},{33,1},{49,17},{2,34}... | collective-permute-start | bytes 4128776 | tf_op jit(solution)/shard_map/ppermute | solution.py:313
  215.1 3.5 %collective-permute-start.11 = (bf16[4,2,64,1024]{3,2,1,0:T(8,128)(2,1)}, bf16[4,2,64,1024]{3,2,1,0:T(8,128)(2,1)S(1)}, u32[]{:S(2)}, u32[]{:S(2)}) collective-permute-start(bf16[4,2,64,1024]{3,2,1,0:T(8,128)(2,1)} %all-to-all-done.4.refs_0_), channel_id=1, source_target_pairs={{0,1},{1,0},{2,3},{3,2},{4,5},{5,4},{6,7},{7,6},{8,9},{9,8},{10,11... | collective-permute-start | bytes 3145736 | tf_op jit(solution)/shard_map/ppermute | solution.py:313
  244.6 23.9 %collective-permute-start.15 = (bf16[2,896,256]{2,1,0:T(8,128)(2,1)}, bf16[2,896,256]{2,1,0:T(8,128)(2,1)S(1)}, u32[]{:S(2)}, u32[]{:S(2)}) collective-permute-start(bf16[2,896,256]{2,1,0:T(8,128)(2,1)} %get-tuple-element.84), channel_id=1, source_target_pairs={{0,16},{16,32},{32,48},{48,0},{1,17},{17,33},{33,49},{49,1},{2,18}... | collective-permute-start | bytes 2752520 | tf_op jit(solution)/shard_map/ppermute | solution.py:313
  244.6 39.8 %collective-permute-start.16 = (bf16[2,896,256]{2,1,0:T(8,128)(2,1)}, bf16[2,896,256]{2,1,0:T(8,128)(2,1)S(1)}, u32[]{:S(2)}, u32[]{:S(2)}) collective-permute-start(bf16[2,896,256]{2,1,0:T(8,128)(2,1)} %get-tuple-element.85), channel_id=1, source_target_pairs={{0,32},{16,48},{32,0},{48,16},{1,33},{17,49},{33,1},{49,17},{2,34}... | collective-permute-start | bytes 2752520 | tf_op jit(solution)/shard_map/ppermute | solution.py:313
  245.7 41.3 %collective-permute-start.17 = (bf16[2,896,256]{2,1,0:T(8,128)(2,1)}, bf16[2,896,256]{2,1,0:T(8,128)(2,1)S(1)}, u32[]{:S(2)}, u32[]{:S(2)}) collective-permute-start(bf16[2,896,256]{2,1,0:T(8,128)(2,1)} %get-tuple-element.86), channel_id=1, source_target_pairs={{0,48},{16,0},{32,16},{48,32},{1,49},{17,1},{33,17},{49,33},{2,50}... | collective-permute-start | bytes 2752520 | tf_op jit(solution)/shard_map/ppermute | solution.py:313
  (15 other events, 82.8 us)

commit v4 on v3

v4 whole, which is shorter than its diff:
```python
import math

import jax
import jax.numpy as jnp
from jax import lax
from jax.experimental import pallas as pl
from jax.experimental.pallas import tpu as pltpu
from jax.sharding import Mesh
from jax.sharding import PartitionSpec as P

FF = 14336
TOK = 512
POOL = 1024
UNITS = 896
D = 8192
WIDE = 1024
WP = 768
WQ = WIDE - WP
WN = 640
VMEM = 56 * 2**20
SHRINK = 1.0 / math.sqrt(FF)
SWAP = [(0, 1), (1, 0)]
BF = jnp.bfloat16
F32 = jnp.float32
SMALL = pl.CostEstimate(flops=1, bytes_accessed=1, transcendentals=0)


def shift(k):
    return [(i, (i + k) % 4) for i in range(4)]


def shape(*dims, dtype=BF):
    return jax.ShapeDtypeStruct(dims, dtype)


def hidden_kernel(place_ref, rows_ref, gate_ref, up_ref, hidden_ref, squares_ref, pick):
    @pl.when(pl.program_id(0) == 0)
    def _():
        rows = rows_ref[...]
        other = jnp.concatenate([rows[:, TOK // 2 :], rows[:, : TOK // 2]], axis=1)
        rows = jnp.where(place_ref[3] == 1, other, rows)
        pool = lax.broadcasted_iota(jnp.int32, (POOL, TOK), 0)
        pick[...] = jnp.where(rows == pool, 1.0, 0.0).astype(BF)

    def picked(ref):
        return lax.dot_general(ref[...], pick[...], (((0,), (0,)), ((), ())), preferred_element_type=F32)

    gate, up = picked(gate_ref), picked(up_ref)
    hidden = (gate / (1.0 + jnp.exp(-gate)) * up).astype(BF)
    wide = hidden.astype(F32)
    hidden_ref[...] = wide.T.astype(BF)
    squares_ref[...] = (wide * wide).astype(BF)


def make_hidden(place, rows, gate, up):
    step = 128
    return pl.pallas_call(
        hidden_kernel,
        grid_spec=pltpu.PrefetchScalarGridSpec(
            num_scalar_prefetch=1,
            grid=(UNITS // step,),
            in_specs=[
                pl.BlockSpec((1, TOK), lambda i, s: (0, 0)),
                pl.BlockSpec((POOL, step), lambda i, s: (0, i)),
                pl.BlockSpec((POOL, step), lambda i, s: (0, i)),
            ],
            out_specs=[
                pl.BlockSpec((TOK, step), lambda i, s: (0, i)),
                pl.BlockSpec((step, TOK), lambda i, s: (i, 0)),
            ],
            scratch_shapes=[pltpu.VMEM((POOL, TOK), BF)],
        ),
        out_shape=[shape(TOK, UNITS), shape(UNITS, TOK)],
        compiler_params=pltpu.CompilerParams(vmem_limit_bytes=VMEM),
        cost_estimate=SMALL,
    )(place, rows, gate, up)


def cut_first_kernel(place_ref, squares_ref, near_1, near_3, far_0, far_1, far_2, far_3, side, one, three):
    squares = squares_ref[...]
    for out, far, near in ((one, far_1, near_1), (three, far_3, near_3)):
        out[:, :WP] = far[:, :WP]
        out[:, WP : 2 * WP] = near[:, :WP]
        out[:, 2 * WP :] = squares
    for dz, far in enumerate((far_0, far_1, far_2, far_3)):
        side[:, dz * WQ : dz * WQ + WQ] = far[:, WP:]


def cut_second_kernel(place_ref, near, far, near_low, near_high, far_two):
    near_low[...] = near[:, :WN]
    near_high[...] = near[:, WN:WP]
    far_two[...] = far[:, :WP]


def cut(kernel, place, extra, projection, places, widths):
    step = 128

    def columns(dy, dz):
        return pl.BlockSpec((step, WIDE), lambda i, s: (i, lax.rem(s[0] + dy, 2) * 4 + lax.rem(s[1] + dz, 4)))

    def rows_of(width):
        return pl.BlockSpec((step, width), lambda i, s: (i, 0))

    return pl.pallas_call(
        kernel,
        grid_spec=pltpu.PrefetchScalarGridSpec(
            num_scalar_prefetch=1,
            grid=(UNITS // step,),
            in_specs=[rows_of(TOK)] * len(extra) + [columns(dy, dz) for dy, dz in places],
            out_specs=[rows_of(width) for width in widths],
        ),
        out_shape=[shape(UNITS, width) for width in widths],
        compiler_params=pltpu.CompilerParams(vmem_limit_bytes=VMEM),
        cost_estimate=SMALL,
    )(place, *extra, *[projection] * len(places))


def partial_kernel(hidden_ref, w_low, w_high, own_p, other_p, own_q, other_q):
    hidden = hidden_ref[...]
    low = (jnp.dot(hidden, w_low[...], preferred_element_type=F32) * SHRINK).astype(BF)
    high = (jnp.dot(hidden, w_high[...], preferred_element_type=F32) * SHRINK).astype(BF)
    edge = WP - WIDE // 2
    for ref_p, ref_q, rows in ((own_p, own_q, slice(0, 256)), (other_p, other_q, slice(256, 512))):
        ref_p[:, : WIDE // 2] = low[rows]
        ref_p[:, WIDE // 2 :] = high[rows, :edge]
        ref_q[...] = high[rows, edge:]


def partial_outputs(hidden, projection):
    half = WIDE // 2
    return pl.pallas_call(
        partial_kernel,
        grid=(8,),
        in_specs=[
            pl.BlockSpec((TOK, UNITS), lambda j: (0, 0)),
            pl.BlockSpec((UNITS, half), lambda j: (0, 2 * j)),
            pl.BlockSpec((UNITS, half), lambda j: (0, 2 * j + 1)),
        ],
        out_specs=[pl.BlockSpec((256, WP), lambda j: (0, j))] * 2
        + [pl.BlockSpec((256, WQ), lambda j: (0, j))] * 2,
        out_shape=[shape(256, 8 * WP)] * 2 + [shape(256, 8 * WQ)] * 2,
        compiler_params=pltpu.CompilerParams(vmem_limit_bytes=VMEM),
        cost_estimate=SMALL,
    )(hidden, projection, projection)


def square_kernel(low, high, put, place_ref, total_ref, far_ref, targets_ref, *outs):
    width = high - low
    for k in range(4):
        place = lax.rem(place_ref[1] + k, 4)
        columns = pl.ds(pl.multiple_of(place * width, 128), width)
        outputs = total_ref[:, columns].astype(F32) + far_ref[:, columns].astype(F32)
        wanted = targets_ref[:, pl.ds(pl.multiple_of(place * WIDE + low, 128), width)].astype(F32)
        errors = (outputs - wanted).astype(BF).astype(F32)
        put(outs, k, (errors * errors).astype(BF))


def put_p(outs, k, value):
    outs[k][...] = value


def put_q(outs, k, value):
    outs[0][0, :, k * WQ : k * WQ + WQ] = value


def error_squares(place, total, far, targets, low, high, out_shape, out_spec, put):
    width = high - low
    return pl.pallas_call(
        lambda *refs: square_kernel(low, high, put, *refs),
        grid_spec=pltpu.PrefetchScalarGridSpec(
            num_scalar_prefetch=1,
            grid=(2,),
            in_specs=[
                pl.BlockSpec((64, 4 * width), lambda j, s: (0, j)),
                pl.BlockSpec((64, 4 * width), lambda j, s: (0, j)),
                pl.BlockSpec((64, 4 * WIDE), lambda j, s: (s[3] * 4 + s[2], j)),
            ],
            out_specs=out_spec,
        ),
        out_shape=out_shape,
        compiler_params=pltpu.CompilerParams(vmem_limit_bytes=VMEM),
        cost_estimate=SMALL,
    )(place, total, far, targets)


def place_tokens(parts, scratch):
    for c, part in enumerate(parts):
        for place in range(4):
            row = c * 256 + place * 64
            for k in range(scratch.shape[0]):
                scratch[k, row : row + 64, :] = part[place, k]


def sums(units, weights, squares, number):
    numerator = denominator = None
    for k in range(number):
        fisher = jnp.dot(units[k], squares(k), preferred_element_type=F32) * (1.0 / TOK)
        weighted = (fisher * weights(k).astype(F32)).astype(BF).astype(F32)
        term = fisher.astype(BF).astype(F32)
        numerator = weighted if numerator is None else numerator + weighted
        denominator = term if denominator is None else denominator + term
    return numerator, denominator


def set_p_kernel(n_two, place_ref, own_units, *refs):
    halves, own, one, two, three = refs[:6], refs[6], refs[7], refs[8 : 8 + n_two], refs[8 + n_two]
    parts, (out_ref, scratch) = refs[9 + n_two : 11 + n_two], refs[11 + n_two :]

    @pl.when(pl.program_id(0) == 0)
    def _():
        place_tokens(parts, scratch)

    def whole(*parts):
        return jnp.concatenate([part[...] for part in parts], axis=1)

    units = [own_units[...]] + [whole(halves[2 * k], halves[2 * k + 1]) for k in range(3)]
    weights = [own[:, :WP], one[...], whole(*two), three[...]]
    numerator, denominator = sums(units, lambda k: weights[k], lambda k: scratch[k], 4)
    out_ref[0] = numerator.astype(out_ref.dtype)
    out_ref[1] = denominator.astype(out_ref.dtype)


def set_p(place, squares, one, u_2, three, two, projection, parts, dy, dtype):
    tall = 224
    half = TOK // 2

    def halves(first):
        return [pl.BlockSpec((tall, half), lambda u, s, i=i: (u, first // half + i)) for i in (0, 1)]

    def columns(i):
        return pl.BlockSpec((tall, WP), lambda u, s: (u, i))

    from_two = [pl.BlockSpec((tall, part.shape[1]), lambda u, s: (u, 0)) for part in two]

    return pl.pallas_call(
        lambda *refs: set_p_kernel(len(two), *refs),
        grid_spec=pltpu.PrefetchScalarGridSpec(
            num_scalar_prefetch=1,
            grid=(UNITS // tall,),
            in_specs=[pl.BlockSpec((tall, TOK), lambda u, s: (u, 0))]
            + [*halves(2 * WP), *[pl.BlockSpec((tall, half), lambda u, s: (u, 0))] * 2, *halves(2 * WP)]
            + [pl.BlockSpec((tall, WIDE), lambda u, s: (u, lax.rem(s[0] + dy, 2) * 4 + s[1]))]
            + [columns(1 - dy), *from_two, columns(1 - dy)]
            + [pl.BlockSpec((4, 4, 64, WP), lambda u, s: (0, 0, 0, dy))] * 2,
            out_specs=pl.BlockSpec((2, tall, WP), lambda u, s: (0, u, 0)),
            scratch_shapes=[pltpu.VMEM((4, TOK, WP), BF)],
        ),
        out_shape=shape(2, UNITS, WP, dtype=dtype),
        compiler_params=pltpu.CompilerParams(vmem_limit_bytes=VMEM),
        cost_estimate=SMALL,
    )(place, squares, one, one, *u_2, three, three, projection, one, *two, three, *parts)


def set_q_kernel(place_ref, own_units, far_units, own_0, own_1, own_2, own_3, far_weights, *refs):
    own_weights = (own_0, own_1, own_2, own_3)
    parts, outs, scratch = refs[:2], refs[2:6], refs[6]

    @pl.when(pl.program_id(0) == 0)
    def _():
        place_tokens(parts, scratch)

    for dz in (1, 2, 3, 0):
        columns = slice(dz * WQ, dz * WQ + WQ)
        weights = (own_weights[dz][:, WP:], far_weights[:, columns])
        numerator, denominator = sums(
            [own_units[...], far_units[...]], lambda k: weights[k], lambda k: scratch[k, :, columns], 2
        )
        outs[dz][0] = numerator.astype(outs[dz].dtype)
        outs[dz][1] = denominator.astype(outs[dz].dtype)


def set_q(place, units, far_units, projection, far, parts):
    tall = 224

    def own(dz):
        return pl.BlockSpec((tall, WIDE), lambda u, s: (u, s[0] * 4 + lax.rem(s[1] + dz, 4)))

    return pl.pallas_call(
        set_q_kernel,
        grid_spec=pltpu.PrefetchScalarGridSpec(
            num_scalar_prefetch=1,
            grid=(UNITS // tall,),
            in_specs=[
                pl.BlockSpec((tall, TOK), lambda u, s: (u, 0)),
                pl.BlockSpec((tall, TOK), lambda u, s: (u, 0)),
            ]
            + [own(dz) for dz in range(4)]
            + [pl.BlockSpec((tall, 4 * WQ), lambda u, s: (u, 0))]
            + [pl.BlockSpec((4, 2, 64, 4 * WQ), lambda u, s: (0, 0, 0, 0))] * 2,
            out_specs=[pl.BlockSpec((2, tall, WQ), lambda u, s: (0, u, 0))] * 4,
            scratch_shapes=[pltpu.VMEM((2, TOK, 4 * WQ), BF)],
        ),
        out_shape=[shape(2, UNITS, WQ, dtype=F32)] + [shape(2, UNITS, WQ)] * 3,
        compiler_params=pltpu.CompilerParams(vmem_limit_bytes=VMEM),
        cost_estimate=SMALL,
    )(place, units, far_units, projection, projection, projection, projection, far, *parts)


def quotient_kernel(columns, *refs):
    out_ref = refs[-1]

    def total(i):
        value = refs[0][i]
        for ref in refs[1 : -1 - (columns.start > 0)]:
            value = value + ref[i].astype(F32)
        return value

    out_ref[...] = total(0) / (total(1) + 1e-06)


def quotient(columns, terms, before=None):
    tall = 224
    width = columns.stop - columns.start
    place = columns.start // width
    given = [] if before is None else [before]
    return pl.pallas_call(
        lambda *refs: quotient_kernel(columns, *refs),
        grid=(UNITS // tall,),
        in_specs=[pl.BlockSpec((2, tall, width), lambda u: (0, u, 0))] * len(terms)
        + [pl.BlockSpec(memory_space=pl.ANY)] * len(given),
        out_specs=pl.BlockSpec((tall, width), lambda u: (u, place)),
        out_shape=shape(UNITS, WIDE, dtype=F32),
        input_output_aliases={len(terms): 0} if given else {},
        compiler_params=pltpu.CompilerParams(vmem_limit_bytes=VMEM),
        cost_estimate=SMALL,
    )(*terms, *given)


def body(token_rows, gate_cache, up_cache, down_weight, targets):
    y, z, x, core = (lax.axis_index(name) for name in ("y_lo", "z", "x", "core"))
    place = jnp.stack([y, z, x, core]).astype(jnp.int32)
    projection = down_weight[0]

    def send(value, axis, k=1):
        return lax.ppermute(value, axis, shift(k) if axis in ("z", "x") else SWAP)

    together = lax.optimization_barrier

    hidden, squares = make_hidden(place, token_rows, gate_cache[0], up_cache[0])

    own_p, other_p, own_q, other_q = partial_outputs(hidden, projection)
    other_p, squares = together((other_p, squares))
    side, one, three = cut(
        cut_first_kernel, place, [squares], projection,
        [(0, 1), (0, 3), (1, 0), (1, 1), (1, 2), (1, 3)], [4 * WQ, 2 * WP + TOK, 2 * WP + TOK],
    )
    one, three, side = send(one, "z", 1), send(three, "z", 3), send(side, "y_lo")

    def pair(own, other):
        both = (own.astype(F32) + send(other, "core").astype(F32)).astype(BF)
        return both.reshape(4, 64, -1)

    def over_x(blocks):
        return lax.all_to_all(blocks, "x", 0, 0, tiled=True)

    def total(blocks):
        return jnp.sum(blocks.astype(F32), axis=0).astype(BF)

    def gathered(part):
        return over_x(jnp.broadcast_to(part[None], (4,) + part.shape))

    blocks_p = over_x(pair(own_p, other_p))
    pair_q = pair(own_q, other_q)
    blocks_p, pair_q = together((blocks_p, pair_q))
    total_p = total(blocks_p)
    total_p, side = together((total_p, side))
    far_p = send(total_p, "y_hi")
    total_q = total(over_x(pair_q))
    squares_p = error_squares(
        place, total_p, far_p, targets[0], 0, WP, [shape(64, 2 * WP)] * 4,
        [pl.BlockSpec((64, WP), lambda j, s: (0, lax.rem(j + s[0], 2)))] * 4, put_p,
    )
    near_low, near_high, far_2 = cut(
        cut_second_kernel, place, [], projection, [(0, 2), (1, 2)], [WN, WP - WN, WP]
    )
    squares_p, one, three, total_q, far_2, near_low, near_high = together(
        (squares_p, one, three, total_q, far_2, near_low, near_high)
    )
    far_q = send(total_q, "y_hi")
    mine_p = jnp.stack([squares_p[0]] + [send(squares_p[k], "z", k) for k in (1, 2, 3)])
    middle = 2 * WP + TOK // 2
    u_2 = (one[:, 2 * WP : middle], three[:, middle:])
    mine_p, far_q, far_2, u_2, squares_late = together((mine_p, far_q, far_2, u_2, squares))

    u_2 = (send(u_2[0], "z", 1), send(u_2[1], "z", 3))
    far_2, u_side = send(far_2, "z", 2), send(squares_late, "y_lo")
    row_p = gathered(mine_p)
    squares_q = error_squares(
        place, total_q, far_q, targets[0], WP, WIDE, shape(2, 64, 4 * WQ),
        pl.BlockSpec((1, 64, 4 * WQ), lambda j, s: (lax.rem(j + s[0], 2), 0, 0)), put_q,
    )
    mine_q = jnp.stack([squares_q[0], send(squares_q[1], "y_lo")])
    row_p, far_2, u_2, u_side, mine_q, near_low, near_high = together(
        (row_p, far_2, u_2, u_side, mine_q, near_low, near_high)
    )

    near_low = send(near_low, "z", 2)
    parts_p = [row_p, send(row_p, "core")]
    p_far = send(set_p(place, squares, one, u_2, three, [far_2], projection, parts_p, 1, BF), "y_lo")
    row_q, near_low, near_high = together((gathered(mine_q), near_low, near_high))
    near_high = send(near_high, "z", 2)
    parts_q = [row_q, send(row_q, "core")]
    q_sums = set_q(place, squares, u_side, projection, side, parts_q)
    q_sums, near_high = together((q_sums, near_high))
    q_own, *q_send = q_sums
    q_far = [send(q, "z", k + 1) for k, q in enumerate(q_send)]
    p_own = set_p(place, squares, one, u_2, three, [near_low, near_high], projection, parts_p, 0, F32)
    merged = quotient(slice(0, WP), [p_own, p_far])
    return quotient(slice(WP, WIDE), [q_own, *q_far], merged)


def solution(mesh):
    cut = Mesh(mesh.devices.reshape(2, 4, 2, 4, 2), ("y_lo", "z", "y_hi", "x", "core"))
    ft, tp = ("y_lo", "z"), ("y_hi", "x", "core")
    placed = (P(ft, None), P(ft, None, tp), P(ft, None, tp), P(ft, tp, None), P(ft, None, None))
    return jax.shard_map(body, mesh=cut, in_specs=placed, out_specs=P(tp, ft), check_vma=False)
```

time: 300 us -> 279 us (0.930)
  waiting for transfers between devices: 142 us -> 116 us
  starting transfers between devices: 46.3 us -> 52.5 us
  Pallas kernels: 81.1 us -> 86 us
  other arithmetic: 11.3 us -> 8.01 us
    ppermute x18 -> x23, waiting for transfers between devices: 106 us -> 82.3 us  [send(): return lax.ppermute(value, axis, shift(k) if axis in ('z', 'x') else SWAP)]
    ppermute x18 -> x23, starting transfers between devices: 25 us -> 36.1 us  [send(): return lax.ppermute(value, axis, shift(k) if axis in ('z', 'x') else SWAP)]
    pallas_call x5 -> x7, Pallas kernels: 50.1 us -> 55.4 us  [the longest x2 20.4 us: set_p(): pl.pallas_call(lambda *refs: set_p_kernel(len(two), *refs), grid_spec=plt...]
    all_to_all x1 -> x0, starting transfers between devices: 5.07 us -> none  [body(): mine_p = lax.all_to_all(squares_p, 'z', 0, 0, tiled=True)]
    unnamed x35 -> x34, local copies, waits for them, and re-layouts: 9.08 us -> 7.24 us
  transfers between devices with their start and end apart: 23 -> 27, of which waited for: 14 -> 13; matrix products, arithmetic and copies ran while one was open for 5% -> 5% of each run, Pallas kernels for 17% -> 21%
where the time goes in v4:
time: 279 us; the launch traced here: 277 us
  waiting for transfers between devices  116 us (42%)
  Pallas kernels  86 us (31%)
  starting transfers between devices  52.5 us (19%)
  local copies, waits for them, and re-layouts  14.9 us (5%)
  other arithmetic  8.01 us (3%)
    ppermute x23, waiting for transfers between devices, send(): return lax.ppermute(value, axis, shift(k) if axis in ('z', 'x') else SWAP)  82.3 us
    ppermute x23, starting transfers between devices, send(): return lax.ppermute(value, axis, shift(k) if axis in ('z', 'x') else SWAP)  36.1 us
    all_to_all x4, waiting for transfers between devices, over_x(): return lax.all_to_all(blocks, 'x', 0, 0, tiled=True)  33.3 us
    pallas_call x2, Pallas kernels, set_p(): pl.pallas_call(lambda *refs: set_p_kernel(len(two), *refs), grid_spec=plt...  20.4 us
    pallas_call x2, Pallas kernels, cut(): pl.pallas_call(kernel, grid_spec=pltpu.PrefetchScalarGridSpec(num_scalar_...  17.3 us
    all_to_all x4, starting transfers between devices, over_x(): return lax.all_to_all(blocks, 'x', 0, 0, tiled=True)  16.4 us
    pallas_call x1, Pallas kernels, partial_outputs(): pl.pallas_call(partial_kernel, grid=(8,), in_specs=[pl.BlockSpec((TOK, UN...  14.7 us
    pallas_call x1, Pallas kernels, set_q(): pl.pallas_call(set_q_kernel, grid_spec=pltpu.PrefetchScalarGridSpec(num_s...  9.83 us
  transfers between devices with their start and end apart: 27, of which 13 were waited for; matrix products, arithmetic and copies ran while one was open for 5% of the time, Pallas kernels for 21%

profile of v4, /device:TPU:1, one launch (start us, length us, event | category | flops | bytes accessed | tf_op | source)
XLA Modules:
  0.0 277.1 jit_solution(11770622139733848605)
XLA Ops:
  0.6 8.1 %shard_map.55 = (bf16[512,896]{1,0:T(8,128)(2,1)}, bf16[896,512]{1,0:T(8,128)(2,1)}) custom-call(s32[4]{0:T(128)} %pad_add_fusion.place_ref.refs_0_, s32[1,512]{1,0:T(1,128)} %rows_ref.1, bf16[1024,896]{1,0:T(8,128)(2,1)} %bitcast.37, bf16[1024,896]{1,0:T(8,128)(2,1)} %bitcast.38), custom_call_target="tpu_custom_call" | custom-call | flops 1 | bytes 1 | tf_op jit(solution)/shard_map/pallas_call | solution.py:57
  8.8 14.7 %shard_map.56 = (bf16[256,6144]{1,0:T(8,128)(2,1)}, bf16[256,6144]{1,0:T(8,128)(2,1)}, bf16[256,2048]{1,0:T(8,128)(2,1)}, bf16[256,2048]{1,0:T(8,128)(2,1)}) custom-call(bf16[512,896]{1,0:T(8,128)(2,1)} %get-tuple-element.63.hidden_ref, bf16[896,8192]{1,0:T(8,128)(2,1)} %bitcast.17, bf16[896,8192]{1,0:T(8,128)(2,1)} %bitcast.18), custom_call_target="tpu_custom_call" | custom-call | flops 1 | bytes 1 | tf_op jit(solution)/shard_map/pallas_call | solution.py:131
  24.9 10.9 %shard_map.57 = (bf16[896,1024]{1,0:T(8,128)(2,1)}, bf16[896,2048]{1,0:T(8,128)(2,1)}, bf16[896,2048]{1,0:T(8,128)(2,1)}) custom-call(s32[4]{0:T(128)} %pad_add_fusion.place_ref.refs_0_, bf16[896,512]{1,0:T(8,128)(2,1)} %get-tuple-element.96.squares_ref.own_units.refs_1_, bf16[896,8192]{1,0:T(8,128)(2,1)} %bitcast.19, bf16[896,8192]{1,0:T(8,128)(2,1)} %bitcast.20, ...), custom_call_target="tpu_custom_call" | custom-call | flops 1 | bytes 1 | tf_op jit(solution)/shard_map/pallas_call | solution.py:104
  42.6 4.0 %all-to-all-start = ((bf16[4,64,6144]{2,1,0:T(8,128)(2,1)}), bf16[4,64,6144]{2,1,0:T(8,128)(2,1)S(1)}, u32[]{:S(2)}, u32[]{:S(2)}) async-start(bf16[4,64,6144]{2,1,0:T(8,128)(2,1)} %bitcast.35), calls=%async_computation | async-start | bytes 6291456 | tf_op jit(solution)/shard_map/all_to_all | solution.py:354
  53.9 29.8 %all-to-all-done = bf16[4,64,6144]{2,1,0:T(8,128)(2,1)S(1)} async-done(((bf16[4,64,6144]{2,1,0:T(8,128)(2,1)}), bf16[4,64,6144]{2,1,0:T(8,128)(2,1)S(1)}, u32[]{:S(2)}, u32[]{:S(2)}) %all-to-all-start) | async-done | bytes 3145760 | tf_op jit(solution)/shard_map/all_to_all | solution.py:354
  87.9 2.9 %collective-permute-start.3 = (bf16[64,6144]{1,0:T(8,128)(2,1)}, bf16[64,6144]{1,0:T(8,128)(2,1)S(1)}, u32[]{:S(2)}, u32[]{:S(2)}) collective-permute-start(bf16[64,6144]{1,0:T(8,128)(2,1)} %reduce_sum.24.refs_1_), channel_id=1, source_target_pairs={{0,8},{8,0},{1,9},{9,1},{2,10},{10,2},{3,11},{11,3},{4,12},{12,4},... | collective-permute-start | bytes 2359304 | tf_op jit(solution)/shard_map/ppermute | solution.py:335
  90.8 3.9 %all-to-all-start.1 = ((bf16[4,64,2048]{2,1,0:T(8,128)(2,1)}), bf16[4,64,2048]{2,1,0:T(8,128)(2,1)S(1)}, u32[]{:S(2)}, u32[]{:S(2)}) async-start(bf16[4,64,2048]{2,1,0:T(8,128)(2,1)} %bitcast.36), calls=%async_computation.1 | async-start | bytes 2097152 | tf_op jit(solution)/shard_map/all_to_all | solution.py:354
  94.7 6.4 %shard_map.59 = (bf16[896,640]{1,0:T(8,128)(2,1)}, bf16[896,128]{1,0:T(8,128)(2,1)}, bf16[896,768]{1,0:T(8,128)(2,1)}) custom-call(s32[4]{0:T(128)} %pad_add_fusion.place_ref.refs_0_, bf16[896,8192]{1,0:T(8,128)(2,1)} %bitcast.25, bf16[896,8192]{1,0:T(8,128)(2,1)} %bitcast.26), custom_call_target="tpu_custom_call" | custom-call | flops 1 | bytes 1 | tf_op jit(solution)/shard_map/pallas_call | solution.py:104
  101.2 6.1 %collective-permute-done.3.refs_2_ = bf16[64,6144]{1,0:T(8,128)(2,1)S(1)} collective-permute-done((bf16[64,6144]{1,0:T(8,128)(2,1)}, bf16[64,6144]{1,0:T(8,128)(2,1)S(1)}, u32[]{:S(2)}, u32[]{:S(2)}) %collective-permute-start.3) | collective-permute-done | bytes 786464 | tf_op jit(solution)/shard_map/ppermute | solution.py:335
  108.1 3.3 %shard_map.58 = (bf16[64,1536]{1,0:T(8,128)(2,1)}, bf16[64,1536]{1,0:T(8,128)(2,1)}, bf16[64,1536]{1,0:T(8,128)(2,1)}, bf16[64,1536]{1,0:T(8,128)(2,1)}) custom-call(s32[4]{0:T(128)} %pad_add_fusion.place_ref.refs_0_, bf16[64,6144]{1,0:T(8,128)(2,1)} %reduce_sum.24.refs_1_, bf16[64,6144]{1,0:T(8,128)(2,1)} %copy-done.11, bf16[512,8192]{1,0:T(8,128)(2,1)} %bitcast.33), custom_call_target="tpu_custom_call" | custom-call | flops 1 | bytes 1 | tf_op jit(solution)/shard_map/pallas_call | solution.py:168
  111.6 8.1 %collective-permute-done.4.refs_2_.refs_3_.refs_9_ = bf16[896,2048]{1,0:T(8,128)(2,1)} collective-permute-done((bf16[896,2048]{1,0:T(8,128)(2,1)}, bf16[896,2048]{1,0:T(8,128)(2,1)}, u32[]{:S(2)}, u32[]{:S(2)}) %collective-permute-start.4) | collective-permute-done | bytes 3670048 | tf_op jit(solution)/shard_map/ppermute | solution.py:335
  120.2 3.3 %collective-permute-start.7 = (bf16[64,1536]{1,0:T(8,128)(2,1)}, bf16[64,1536]{1,0:T(8,128)(2,1)S(1)}, u32[]{:S(2)}, u32[]{:S(2)}) collective-permute-start(bf16[64,1536]{1,0:T(8,128)(2,1)} %get-tuple-element.86), channel_id=1, source_target_pairs={{0,32},{16,48},{32,0},{48,16},{1,33},{17,49},{33,1},{49,17},{2,34}... | collective-permute-start | bytes 589832 | tf_op jit(solution)/shard_map/ppermute | solution.py:335
  134.2 4.0 %all-to-all-start.2 = ((bf16[4,4,64,1536]{3,2,1,0:T(8,128)(2,1)}), bf16[4,4,64,1536]{3,2,1,0:T(8,128)(2,1)S(1)}, u32[]{:S(2)}, u32[]{:S(2)}) async-start(bf16[4,4,64,1536]{3,2,1,0:T(8,128)(2,1)} %broadcast_in_dim.4), calls=%async_computation.2 | async-start | bytes 6291456 | tf_op jit(solution)/shard_map/all_to_all | solution.py:354
  148.2 14.6 %collective-permute-done.14 = bf16[64,1024]{1,0:T(8,128)(2,1)S(1)} collective-permute-done((bf16[64,1024]{1,0:T(8,128)(2,1)S(1)}, bf16[64,1024]{1,0:T(8,128)(2,1)S(1)}, u32[]{:S(2)}, u32[]{:S(2)}) %collective-permute-start.14) | collective-permute-done | bytes 131104 | tf_op jit(solution)/shard_map/ppermute | solution.py:335
  162.9 19.0 %collective-permute-done.11.refs_4_ = bf16[896,256]{1,0:T(8,128)(2,1)S(1)} collective-permute-done((bf16[896,256]{1,0:T(8,128)(2,1)S(1)}, bf16[896,256]{1,0:T(8,128)(2,1)S(1)}, u32[]{:S(2)}, u32[]{:S(2)}) %collective-permute-start.11) | collective-permute-done | bytes 458784 | tf_op jit(solution)/shard_map/ppermute | solution.py:335
  188.1 4.4 %all-to-all-start.3 = ((bf16[4,2,64,1024]{3,2,1,0:T(8,128)(2,1)}), bf16[4,2,64,1024]{3,2,1,0:T(8,128)(2,1)}, u32[]{:S(2)}, u32[]{:S(2)}) async-start(bf16[4,2,64,1024]{3,2,1,0:T(8,128)(2,1)} %broadcast_in_dim.5), calls=%async_computation.3 | async-start | bytes 2097152 | tf_op jit(solution)/shard_map/all_to_all | solution.py:354
  192.6 9.9 %shard_map.63 = bf16[2,896,768]{2,1,0:T(8,128)(2,1)} custom-call(s32[4]{0:T(128)} %pad_add_fusion.place_ref.refs_0_, bf16[896,512]{1,0:T(8,128)(2,1)} %get-tuple-element.96.squares_ref.own_units.refs_1_, bf16[896,2048]{1,0:T(8,128)(2,1)} %collective-permute-done.4.refs_2_.refs_3_.refs_9_, bf16[896,2048]{1,0:T(8,128)(2,1)} %collective-permute-done.4.refs_2_.refs_3_.refs_9_, ...), custom_call_target="tpu_custom_call" | custom-call | flops 1 | bytes 1 | tf_op jit(solution)/shard_map/pallas_call | solution.py:235
  203.9 3.4 %all-to-all-done.3.refs_0_ = bf16[4,2,64,1024]{3,2,1,0:T(8,128)(2,1)} async-done(((bf16[4,2,64,1024]{3,2,1,0:T(8,128)(2,1)}), bf16[4,2,64,1024]{3,2,1,0:T(8,128)(2,1)}, u32[]{:S(2)}, u32[]{:S(2)}) %all-to-all-start.3) | async-done | bytes 1048608 | tf_op jit(solution)/shard_map/all_to_all | solution.py:354
  207.3 6.0 %collective-permute-done.15.refs_10_ = bf16[896,640]{1,0:T(8,128)(2,1)} collective-permute-done((bf16[896,640]{1,0:T(8,128)(2,1)}, bf16[896,640]{1,0:T(8,128)(2,1)}, u32[]{:S(2)}, u32[]{:S(2)}) %collective-permute-start.15) | collective-permute-done | bytes 1146912 | tf_op jit(solution)/shard_map/ppermute | solution.py:335
  217.6 9.8 %shard_map.61 = (f32[2,896,256]{2,1,0:T(8,128)}, bf16[2,896,256]{2,1,0:T(8,128)(2,1)}, bf16[2,896,256]{2,1,0:T(8,128)(2,1)}, bf16[2,896,256]{2,1,0:T(8,128)(2,1)}) custom-call(s32[4]{0:T(128)} %pad_add_fusion.place_ref.refs_0_, bf16[896,512]{1,0:T(8,128)(2,1)} %get-tuple-element.96.squares_ref.own_units.refs_1_, bf16[896,512]{1,0:T(8,128)(2,1)} %copy-done.7, ...), custom_call_target="tpu_custom_call" | custom-call | flops 1 | bytes 1 | tf_op jit(solution)/shard_map/pallas_call | solution.py:278
  232.0 10.5 %shard_map.62.refs_0_ = f32[2,896,768]{2,1,0:T(8,128)} custom-call(s32[4]{0:T(128)} %pad_add_fusion.place_ref.refs_0_, bf16[896,512]{1,0:T(8,128)(2,1)} %get-tuple-element.96.squares_ref.own_units.refs_1_, bf16[896,2048]{1,0:T(8,128)(2,1)} %collective-permute-done.4.refs_2_.refs_3_.refs_9_, bf16[896,2048]{1,0:T(8,128)(2,1)} %collective-permute-done.4.refs_2_.refs_3_.refs_9_, ...), custom_call_target="tpu_custom_call" | custom-call | flops 1 | bytes 1 | tf_op jit(solution)/shard_map/pallas_call | solution.py:235
  242.5 21.1 %collective-permute-done.22.refs_1_ = bf16[2,896,768]{2,1,0:T(8,128)(2,1)S(1)} collective-permute-done((bf16[2,896,768]{2,1,0:T(8,128)(2,1)}, bf16[2,896,768]{2,1,0:T(8,128)(2,1)S(1)}, u32[]{:S(2)}, u32[]{:S(2)}) %collective-permute-start.22) | collective-permute-done | bytes 2752544 | tf_op jit(solution)/shard_map/ppermute | solution.py:335
  265.2 5.4 %shard_map.64.refs_4_ = f32[896,1024]{1,0:T(8,128)} custom-call(f32[2,896,768]{2,1,0:T(8,128)} %shard_map.62.refs_0_, bf16[2,896,768]{2,1,0:T(8,128)(2,1)} %copy-done.2), custom_call_target="tpu_custom_call" | custom-call | flops 1 | bytes 1 | tf_op jit(solution)/shard_map/pallas_call | solution.py:316
  273.0 4.2 %shard_map.65 = f32[896,1024]{1,0:T(8,128)} custom-call(f32[2,896,256]{2,1,0:T(8,128)} %get-tuple-element.111.refs_0_, bf16[2,896,256]{2,1,0:T(8,128)(2,1)} %copy-done.8, bf16[2,896,256]{2,1,0:T(8,128)(2,1)} %copy-done.9, bf16[2,896,256]{2,1,0:T(8,128)(2,1)} %copy-done.10, f32[896,1024]{1,0:T(8,128)} %shard_map.64.refs_4_), custom_call_target="tpu_custom_call", output_to_operand_aliasing={{}: (4, {})} | custom-call | flops 1 | bytes 1 | tf_op jit(solution)/shard_map/pallas_call | solution.py:316
  (87 shorter events, 63.1 us)
Async XLA Ops:
  23.4 16.4 %collective-permute-start = (bf16[256,6144]{1,0:T(8,128)(2,1)}, bf16[256,6144]{1,0:T(8,128)(2,1)S(1)}, u32[]{:S(2)}, u32[]{:S(2)}) collective-permute-start(bf16[256,6144]{1,0:T(8,128)(2,1)} %get-tuple-element.68), channel_id=1, source_target_pairs={{0,1},{1,0},{2,3},{3,2},{4,5},{5,4},{6,7},{7,6},{8,9},{9,8},{10,11... | collective-permute-start | bytes 9437192 | tf_op jit(solution)/shard_map/ppermute | solution.py:335
  35.7 84.0 %collective-permute-start.4 = (bf16[896,2048]{1,0:T(8,128)(2,1)}, bf16[896,2048]{1,0:T(8,128)(2,1)}, u32[]{:S(2)}, u32[]{:S(2)}) collective-permute-start(bf16[896,2048]{1,0:T(8,128)(2,1)} %get-tuple-element.78), channel_id=1, source_target_pairs={{0,16},{16,32},{32,48},{48,0},{1,17},{17,33},{33,49},{49,1},{2,18}... | collective-permute-start | bytes 11010056 | tf_op jit(solution)/shard_map/ppermute | solution.py:335
  37.6 82.1 %collective-permute-start.5 = (bf16[896,2048]{1,0:T(8,128)(2,1)}, bf16[896,2048]{1,0:T(8,128)(2,1)}, u32[]{:S(2)}, u32[]{:S(2)}) collective-permute-start(bf16[896,2048]{1,0:T(8,128)(2,1)} %get-tuple-element.79), channel_id=1, source_target_pairs={{0,48},{16,0},{32,16},{48,32},{1,49},{17,1},{33,17},{49,33},{2,50}... | collective-permute-start | bytes 11010056 | tf_op jit(solution)/shard_map/ppermute | solution.py:335
  42.6 41.1 %all-to-all-start = ((bf16[4,64,6144]{2,1,0:T(8,128)(2,1)}), bf16[4,64,6144]{2,1,0:T(8,128)(2,1)S(1)}, u32[]{:S(2)}, u32[]{:S(2)}) async-start(bf16[4,64,6144]{2,1,0:T(8,128)(2,1)} %bitcast.35), calls=%async_computation | async-start | bytes 6291456 | tf_op jit(solution)/shard_map/all_to_all | solution.py:354
  46.6 41.3 %collective-permute-start.2 = (bf16[896,1024]{1,0:T(8,128)(2,1)}, bf16[896,1024]{1,0:T(8,128)(2,1)}, u32[]{:S(2)}, u32[]{:S(2)}) collective-permute-start(bf16[896,1024]{1,0:T(8,128)(2,1)} %get-tuple-element.72), channel_id=1, source_target_pairs={{0,64},{64,0},{1,65},{65,1},{2,66},{66,2},{3,67},{67,3},{4,68},{68... | collective-permute-start | bytes 5505032 | tf_op jit(solution)/shard_map/ppermute | solution.py:335
  87.9 19.3 %collective-permute-start.3 = (bf16[64,6144]{1,0:T(8,128)(2,1)}, bf16[64,6144]{1,0:T(8,128)(2,1)S(1)}, u32[]{:S(2)}, u32[]{:S(2)}) collective-permute-start(bf16[64,6144]{1,0:T(8,128)(2,1)} %reduce_sum.24.refs_1_), channel_id=1, source_target_pairs={{0,8},{8,0},{1,9},{9,1},{2,10},{10,2},{3,11},{11,3},{4,12},{12,4},... | collective-permute-start | bytes 2359304 | tf_op jit(solution)/shard_map/ppermute | solution.py:335
  90.8 20.5 %all-to-all-start.1 = ((bf16[4,64,2048]{2,1,0:T(8,128)(2,1)}), bf16[4,64,2048]{2,1,0:T(8,128)(2,1)S(1)}, u32[]{:S(2)}, u32[]{:S(2)}) async-start(bf16[4,64,2048]{2,1,0:T(8,128)(2,1)} %bitcast.36), calls=%async_computation.1 | async-start | bytes 2097152 | tf_op jit(solution)/shard_map/all_to_all | solution.py:354
  119.7 10.7 %collective-permute-start.6 = (bf16[64,1536]{1,0:T(8,128)(2,1)}, bf16[64,1536]{1,0:T(8,128)(2,1)S(1)}, u32[]{:S(2)}, u32[]{:S(2)}) collective-permute-start(bf16[64,1536]{1,0:T(8,128)(2,1)} %get-tuple-element.85), channel_id=1, source_target_pairs={{0,16},{16,32},{32,48},{48,0},{1,17},{17,33},{33,49},{49,1},{2,18}... | collective-permute-start | bytes 589832 | tf_op jit(solution)/shard_map/ppermute | solution.py:335
  120.2 12.0 %collective-permute-start.7 = (bf16[64,1536]{1,0:T(8,128)(2,1)}, bf16[64,1536]{1,0:T(8,128)(2,1)S(1)}, u32[]{:S(2)}, u32[]{:S(2)}) collective-permute-start(bf16[64,1536]{1,0:T(8,128)(2,1)} %get-tuple-element.86), channel_id=1, source_target_pairs={{0,32},{16,48},{32,0},{48,16},{1,33},{17,49},{33,1},{49,17},{2,34}... | collective-permute-start | bytes 589832 | tf_op jit(solution)/shard_map/ppermute | solution.py:335
  123.4 8.7 %collective-permute-start.8 = (bf16[64,1536]{1,0:T(8,128)(2,1)}, bf16[64,1536]{1,0:T(8,128)(2,1)S(1)}, u32[]{:S(2)}, u32[]{:S(2)}) collective-permute-start(bf16[64,1536]{1,0:T(8,128)(2,1)} %get-tuple-element.87), channel_id=1, source_target_pairs={{0,48},{16,0},{32,16},{48,32},{1,49},{17,1},{33,17},{49,33},{2,50}... | collective-permute-start | bytes 589832 | tf_op jit(solution)/shard_map/ppermute | solution.py:335
  134.2 49.5 %all-to-all-start.2 = ((bf16[4,4,64,1536]{3,2,1,0:T(8,128)(2,1)}), bf16[4,4,64,1536]{3,2,1,0:T(8,128)(2,1)S(1)}, u32[]{:S(2)}, u32[]{:S(2)}) async-start(bf16[4,4,64,1536]{3,2,1,0:T(8,128)(2,1)} %broadcast_in_dim.4), calls=%async_computation.2 | async-start | bytes 6291456 | tf_op jit(solution)/shard_map/all_to_all | solution.py:354
  138.2 45.5 %collective-permute-start.10 = (bf16[896,768]{1,0:T(8,128)(2,1)}, bf16[896,768]{1,0:T(8,128)(2,1)}, u32[]{:S(2)}, u32[]{:S(2)}) collective-permute-start(bf16[896,768]{1,0:T(8,128)(2,1)} %get-tuple-element.93), channel_id=1, source_target_pairs={{0,32},{16,48},{32,0},{48,16},{1,33},{17,49},{33,1},{49,17},{2,34}... | collective-permute-start | bytes 4128776 | tf_op jit(solution)/shard_map/ppermute | solution.py:335
  140.0 41.9 %collective-permute-start.13 = (bf16[896,512]{1,0:T(8,128)(2,1)}, bf16[896,512]{1,0:T(8,128)(2,1)S(1)}, u32[]{:S(2)}, u32[]{:S(2)}) collective-permute-start(bf16[896,512]{1,0:T(8,128)(2,1)} %get-tuple-element.96.squares_ref.own_units.refs_1_), channel_id=1, source_target_pairs={{0,64},{64,0},{1,65},{65,1},{2,66},{66,2},{3,67},{67,3},{4,68},{68... | collective-permute-start | bytes 2752520 | tf_op jit(solution)/shard_map/ppermute | solution.py:335
  144.1 37.8 %collective-permute-start.11 = (bf16[896,256]{1,0:T(8,128)(2,1)S(1)}, bf16[896,256]{1,0:T(8,128)(2,1)S(1)}, u32[]{:S(2)}, u32[]{:S(2)}) collective-permute-start(bf16[896,256]{1,0:T(8,128)(2,1)S(1)} %copy-done.13), channel_id=1, source_target_pairs={{0,16},{16,32},{32,48},{48,0},{1,17},{17,33},{33,49},{49,1},{2,18}... | collective-permute-start | bytes 1376264 | tf_op jit(solution)/shard_map/ppermute | solution.py:335
  145.8 36.1 %collective-permute-start.12 = (bf16[896,256]{1,0:T(8,128)(2,1)S(1)}, bf16[896,256]{1,0:T(8,128)(2,1)S(1)}, u32[]{:S(2)}, u32[]{:S(2)}) collective-permute-start(bf16[896,256]{1,0:T(8,128)(2,1)S(1)} %copy-done.12), channel_id=1, source_target_pairs={{0,48},{16,0},{32,16},{48,32},{1,49},{17,1},{33,17},{49,33},{2,50}... | collective-permute-start | bytes 1376264 | tf_op jit(solution)/shard_map/ppermute | solution.py:335
  148.0 14.9 %collective-permute-start.14 = (bf16[64,1024]{1,0:T(8,128)(2,1)S(1)}, bf16[64,1024]{1,0:T(8,128)(2,1)S(1)}, u32[]{:S(2)}, u32[]{:S(2)}) collective-permute-start(bf16[64,1024]{1,0:T(8,128)(2,1)S(1)} %get-tuple-element.122), channel_id=1, source_target_pairs={{0,64},{64,0},{1,65},{65,1},{2,66},{66,2},{3,67},{67,3},{4,68},{68... | collective-permute-start | bytes 393224 | tf_op jit(solution)/shard_map/ppermute | solution.py:335
  183.8 8.8 %collective-permute-start.21 = (bf16[4,4,64,1536]{3,2,1,0:T(8,128)(2,1)S(1)}, bf16[4,4,64,1536]{3,2,1,0:T(8,128)(2,1)}, u32[]{:S(2)}, u32[]{:S(2)}) collective-permute-start(bf16[4,4,64,1536]{3,2,1,0:T(8,128)(2,1)S(1)} %all-to-all-done.2.refs_13_.refs_12_), channel_id=1, source_target_pairs={{0,1},{1,0},{2,3},{3,2},{4,5},{5,4},{6,7},{7,6},{8,9},{9,8},{10,11... | collective-permute-start | bytes 9437192 | tf_op jit(solution)/shard_map/ppermute | solution.py:335
  184.7 28.6 %collective-permute-start.15 = (bf16[896,640]{1,0:T(8,128)(2,1)}, bf16[896,640]{1,0:T(8,128)(2,1)}, u32[]{:S(2)}, u32[]{:S(2)}) collective-permute-start(bf16[896,640]{1,0:T(8,128)(2,1)} %get-tuple-element.103), channel_id=1, source_target_pairs={{0,32},{16,48},{32,0},{48,16},{1,33},{17,49},{33,1},{49,17},{2,34}... | collective-permute-start | bytes 3440648 | tf_op jit(solution)/shard_map/ppermute | solution.py:335
  188.1 19.2 %all-to-all-start.3 = ((bf16[4,2,64,1024]{3,2,1,0:T(8,128)(2,1)}), bf16[4,2,64,1024]{3,2,1,0:T(8,128)(2,1)}, u32[]{:S(2)}, u32[]{:S(2)}) async-start(bf16[4,2,64,1024]{3,2,1,0:T(8,128)(2,1)} %broadcast_in_dim.5), calls=%async_computation.3 | async-start | bytes 2097152 | tf_op jit(solution)/shard_map/all_to_all | solution.py:354
  202.5 61.1 %collective-permute-start.22 = (bf16[2,896,768]{2,1,0:T(8,128)(2,1)}, bf16[2,896,768]{2,1,0:T(8,128)(2,1)S(1)}, u32[]{:S(2)}, u32[]{:S(2)}) collective-permute-start(bf16[2,896,768]{2,1,0:T(8,128)(2,1)} %shard_map.63), channel_id=1, source_target_pairs={{0,64},{64,0},{1,65},{65,1},{2,66},{66,2},{3,67},{67,3},{4,68},{68... | collective-permute-start | bytes 8257544 | tf_op jit(solution)/shard_map/ppermute | solution.py:335
  214.2 13.3 %collective-permute-start.17 = (bf16[896,128]{1,0:T(8,128)(2,1)S(1)}, bf16[896,128]{1,0:T(8,128)(2,1)S(1)}, u32[]{:S(2)}, u32[]{:S(2)}) collective-permute-start(bf16[896,128]{1,0:T(8,128)(2,1)S(1)} %copy-done.16), channel_id=1, source_target_pairs={{0,32},{16,48},{32,0},{48,16},{1,33},{17,49},{33,1},{49,17},{2,34}... | collective-permute-start | bytes 688136 | tf_op jit(solution)/shard_map/ppermute | solution.py:335
  227.5 43.1 %collective-permute-start.18 = (bf16[2,896,256]{2,1,0:T(8,128)(2,1)}, bf16[2,896,256]{2,1,0:T(8,128)(2,1)S(1)}, u32[]{:S(2)}, u32[]{:S(2)}) collective-permute-start(bf16[2,896,256]{2,1,0:T(8,128)(2,1)} %get-tuple-element.112), channel_id=1, source_target_pairs={{0,16},{16,32},{32,48},{48,0},{1,17},{17,33},{33,49},{49,1},{2,18}... | collective-permute-start | bytes 2752520 | tf_op jit(solution)/shard_map/ppermute | solution.py:335
  229.2 41.8 %collective-permute-start.19 = (bf16[2,896,256]{2,1,0:T(8,128)(2,1)}, bf16[2,896,256]{2,1,0:T(8,128)(2,1)S(1)}, u32[]{:S(2)}, u32[]{:S(2)}) collective-permute-start(bf16[2,896,256]{2,1,0:T(8,128)(2,1)} %get-tuple-element.113), channel_id=1, source_target_pairs={{0,32},{16,48},{32,0},{48,16},{1,33},{17,49},{33,1},{49,17},{2,34}... | collective-permute-start | bytes 2752520 | tf_op jit(solution)/shard_map/ppermute | solution.py:335
  231.1 40.0 %collective-permute-start.20 = (bf16[2,896,256]{2,1,0:T(8,128)(2,1)}, bf16[2,896,256]{2,1,0:T(8,128)(2,1)S(1)}, u32[]{:S(2)}, u32[]{:S(2)}) collective-permute-start(bf16[2,896,256]{2,1,0:T(8,128)(2,1)} %get-tuple-element.114), channel_id=1, source_target_pairs={{0,48},{16,0},{32,16},{48,32},{1,49},{17,1},{33,17},{49,33},{2,50}... | collective-permute-start | bytes 2752520 | tf_op jit(solution)/shard_map/ppermute | solution.py:335
  (20 other events, 132.1 us)

commit v5 on v4

--- a/solution.py
+++ b/solution.py
@@ -17,6 +17,7 @@
 WP = 768
 WQ = WIDE - WP
 WN = 640
+WN2 = 512
 VMEM = 56 * 2**20
 SHRINK = 1.0 / math.sqrt(FF)
 SWAP = [(0, 1), (1, 0)]
@@ -33,42 +34,35 @@
     return jax.ShapeDtypeStruct(dims, dtype)
 
 
-def hidden_kernel(place_ref, rows_ref, gate_ref, up_ref, hidden_ref, squares_ref, pick):
-    @pl.when(pl.program_id(0) == 0)
-    def _():
-        rows = rows_ref[...]
-        other = jnp.concatenate([rows[:, TOK // 2 :], rows[:, : TOK // 2]], axis=1)
-        rows = jnp.where(place_ref[3] == 1, other, rows)
-        pool = lax.broadcasted_iota(jnp.int32, (POOL, TOK), 0)
-        pick[...] = jnp.where(rows == pool, 1.0, 0.0).astype(BF)
-
-    def picked(ref):
-        return lax.dot_general(ref[...], pick[...], (((0,), (0,)), ((), ())), preferred_element_type=F32)
-
-    gate, up = picked(gate_ref), picked(up_ref)
+def hidden_kernel(place_ref, rows_ref, gate_ref, up_ref, hidden_ref, squares_ref):
+    rows = rows_ref[...]
+    other = jnp.concatenate([rows[:, TOK // 2 :], rows[:, : TOK // 2]], axis=1)
+    rows = jnp.where(place_ref[3] == 1, other, rows)
+    pool = lax.broadcasted_iota(jnp.int32, (POOL, TOK), 0)
+    pick = jnp.where(rows == pool, 1.0, 0.0).T.astype(BF)
+    gate = jnp.dot(pick, gate_ref[...], preferred_element_type=F32)
+    up = jnp.dot(pick, up_ref[...], preferred_element_type=F32)
     hidden = (gate / (1.0 + jnp.exp(-gate)) * up).astype(BF)
+    hidden_ref[...] = hidden
     wide = hidden.astype(F32)
-    hidden_ref[...] = wide.T.astype(BF)
-    squares_ref[...] = (wide * wide).astype(BF)
+    squares_ref[...] = (wide * wide).T.astype(BF)
 
 
 def make_hidden(place, rows, gate, up):
-    step = 128
     return pl.pallas_call(
         hidden_kernel,
         grid_spec=pltpu.PrefetchScalarGridSpec(
             num_scalar_prefetch=1,
-            grid=(UNITS // step,),
+            grid=(1,),
             in_specs=[
                 pl.BlockSpec((1, TOK), lambda i, s: (0, 0)),
-                pl.BlockSpec((POOL, step), lambda i, s: (0, i)),
-                pl.BlockSpec((POOL, step), lambda i, s: (0, i)),
+                pl.BlockSpec((POOL, UNITS), lambda i, s: (0, 0)),
+                pl.BlockSpec((POOL, UNITS), lambda i, s: (0, 0)),
             ],
             out_specs=[
-                pl.BlockSpec((TOK, step), lambda i, s: (0, i)),
-                pl.BlockSpec((step, TOK), lambda i, s: (i, 0)),
+                pl.BlockSpec((TOK, UNITS), lambda i, s: (0, 0)),
+                pl.BlockSpec((UNITS, TOK), lambda i, s: (0, 0)),
             ],
-            scratch_shapes=[pltpu.VMEM((POOL, TOK), BF)],
         ),
         out_shape=[shape(TOK, UNITS), shape(UNITS, TOK)],
         compiler_params=pltpu.CompilerParams(vmem_limit_bytes=VMEM),
@@ -80,20 +74,22 @@
     squares = squares_ref[...]
     for out, far, near in ((one, far_1, near_1), (three, far_3, near_3)):
         out[:, :WP] = far[:, :WP]
-        out[:, WP : 2 * WP] = near[:, :WP]
-        out[:, 2 * WP :] = squares
+        out[:, WP : WP + TOK] = squares
+        out[:, WP + TOK :] = near[:, :WN]
     for dz, far in enumerate((far_0, far_1, far_2, far_3)):
         side[:, dz * WQ : dz * WQ + WQ] = far[:, WP:]
 
 
-def cut_second_kernel(place_ref, near, far, near_low, near_high, far_two):
-    near_low[...] = near[:, :WN]
-    near_high[...] = near[:, WN:WP]
-    far_two[...] = far[:, :WP]
+def cut_second_kernel(place_ref, near_1, near_2, near_3, far_2, late_1, early_2, late_2, late_3, far_two):
+    late_1[...] = near_1[:, WN:WP]
+    late_3[...] = near_3[:, WN:WP]
+    early_2[...] = near_2[:, :WN2]
+    late_2[...] = near_2[:, WN2:WP]
+    far_two[...] = far_2[:, :WP]
 
 
 def cut(kernel, place, extra, projection, places, widths):
-    step = 128
+    step = 224
 
     def columns(dy, dz):
         return pl.BlockSpec((step, WIDE), lambda i, s: (i, lax.rem(s[0] + dy, 2) * 4 + lax.rem(s[1] + dz, 4)))
@@ -202,53 +198,45 @@
     return numerator, denominator
 
 
-def set_p_kernel(n_two, place_ref, own_units, *refs):
-    halves, own, one, two, three = refs[:6], refs[6], refs[7], refs[8 : 8 + n_two], refs[8 + n_two]
-    parts, (out_ref, scratch) = refs[9 + n_two : 11 + n_two], refs[11 + n_two :]
+def set_p_kernel(counts, place_ref, own_units, own, *refs):
+    refs = list(refs)
+    groups = []
+    for count in counts:
+        groups.append(jnp.concatenate([ref[...] for ref in refs[:count]], axis=1))
+        del refs[:count]
+    parts, (out_ref, scratch) = refs[:2], refs[2:]
 
     @pl.when(pl.program_id(0) == 0)
     def _():
         place_tokens(parts, scratch)
 
-    def whole(*parts):
-        return jnp.concatenate([part[...] for part in parts], axis=1)
-
-    units = [own_units[...]] + [whole(halves[2 * k], halves[2 * k + 1]) for k in range(3)]
-    weights = [own[:, :WP], one[...], whole(*two), three[...]]
+    units, weights = [own_units[...]] + groups[:3], [own[:, :WP]] + groups[3:]
     numerator, denominator = sums(units, lambda k: weights[k], lambda k: scratch[k], 4)
     out_ref[0] = numerator.astype(out_ref.dtype)
     out_ref[1] = denominator.astype(out_ref.dtype)
 
 
-def set_p(place, squares, one, u_2, three, two, projection, parts, dy, dtype):
+def set_p(place, squares, projection, moved, parts, dy, dtype, first=0, count=4):
     tall = 224
-    half = TOK // 2
-
-    def halves(first):
-        return [pl.BlockSpec((tall, half), lambda u, s, i=i: (u, first // half + i)) for i in (0, 1)]
-
-    def columns(i):
-        return pl.BlockSpec((tall, WP), lambda u, s: (u, i))
-
-    from_two = [pl.BlockSpec((tall, part.shape[1]), lambda u, s: (u, 0)) for part in two]
-
-    return pl.pallas_call(
-        lambda *refs: set_p_kernel(len(two), *refs),
+    pieces = [piece for group in moved for piece in group]
+    return pl.pallas_call(
+        lambda *refs: set_p_kernel([len(group) for group in moved], *refs),
         grid_spec=pltpu.PrefetchScalarGridSpec(
             num_scalar_prefetch=1,
-            grid=(UNITS // tall,),
-            in_specs=[pl.BlockSpec((tall, TOK), lambda u, s: (u, 0))]
-            + [*halves(2 * WP), *[pl.BlockSpec((tall, half), lambda u, s: (u, 0))] * 2, *halves(2 * WP)]
-            + [pl.BlockSpec((tall, WIDE), lambda u, s: (u, lax.rem(s[0] + dy, 2) * 4 + s[1]))]
-            + [columns(1 - dy), *from_two, columns(1 - dy)]
+            grid=(count,),
+            in_specs=[
+                pl.BlockSpec((tall, TOK), lambda u, s: (u + first, 0)),
+                pl.BlockSpec((tall, WIDE), lambda u, s: (u + first, lax.rem(s[0] + dy, 2) * 4 + s[1])),
+            ]
+            + [pl.BlockSpec((tall, width), lambda u, s, i=i: (u + first, i)) for _, width, i in pieces]
             + [pl.BlockSpec((4, 4, 64, WP), lambda u, s: (0, 0, 0, dy))] * 2,
             out_specs=pl.BlockSpec((2, tall, WP), lambda u, s: (0, u, 0)),
             scratch_shapes=[pltpu.VMEM((4, TOK, WP), BF)],
         ),
-        out_shape=shape(2, UNITS, WP, dtype=dtype),
-        compiler_params=pltpu.CompilerParams(vmem_limit_bytes=VMEM),
-        cost_estimate=SMALL,
-    )(place, squares, one, one, *u_2, three, three, projection, one, *two, three, *parts)
+        out_shape=shape(2, count * tall, WP, dtype=dtype),
+        compiler_params=pltpu.CompilerParams(vmem_limit_bytes=VMEM),
+        cost_estimate=SMALL,
+    )(place, squares, projection, *[array for array, _, _ in pieces], *parts)
 
 
 def set_q_kernel(place_ref, own_units, far_units, own_0, own_1, own_2, own_3, far_weights, *refs):
@@ -261,7 +249,7 @@
 
     for dz in (1, 2, 3, 0):
         columns = slice(dz * WQ, dz * WQ + WQ)
-        weights = (own_weights[dz][:, WP:], far_weights[:, columns])
+        weights = (own_weights[dz][...], far_weights[:, columns])
         numerator, denominator = sums(
             [own_units[...], far_units[...]], lambda k: weights[k], lambda k: scratch[k, :, columns], 2
         )
@@ -273,7 +261,7 @@
     tall = 224
 
     def own(dz):
-        return pl.BlockSpec((tall, WIDE), lambda u, s: (u, s[0] * 4 + lax.rem(s[1] + dz, 4)))
+        return pl.BlockSpec((tall, WQ), lambda u, s: (u, (s[0] * 4 + lax.rem(s[1] + dz, 4)) * (WIDE // WQ) + WP // WQ))
 
     return pl.pallas_call(
         set_q_kernel,
@@ -296,29 +284,32 @@
     )(place, units, far_units, projection, projection, projection, projection, far, *parts)
 
 
-def quotient_kernel(columns, *refs):
+def quotient_kernel(n_given, *refs):
     out_ref = refs[-1]
 
     def total(i):
         value = refs[0][i]
-        for ref in refs[1 : -1 - (columns.start > 0)]:
+        for ref in refs[1 : -1 - n_given]:
             value = value + ref[i].astype(F32)
         return value
 
     out_ref[...] = total(0) / (total(1) + 1e-06)
 
 
-def quotient(columns, terms, before=None):
+def quotient(columns, terms, before=None, first=0, count=4):
     tall = 224
     width = columns.stop - columns.start
     place = columns.start // width
     given = [] if before is None else [before]
     return pl.pallas_call(
-        lambda *refs: quotient_kernel(columns, *refs),
-        grid=(UNITS // tall,),
-        in_specs=[pl.BlockSpec((2, tall, width), lambda u: (0, u, 0))] * len(terms)
+        lambda *refs: quotient_kernel(len(given), *refs),
+        grid=(count,),
+        in_specs=[
+            pl.BlockSpec((2, tall, width), lambda u, start=first * (term.shape[1] == UNITS): (0, u + start, 0))
+            for term in terms
+        ]
         + [pl.BlockSpec(memory_space=pl.ANY)] * len(given),
-        out_specs=pl.BlockSpec((tall, width), lambda u: (u, place)),
+        out_specs=pl.BlockSpec((tall, width), lambda u: (u + first, place)),
         out_shape=shape(UNITS, WIDE, dtype=F32),
         input_output_aliases={len(terms): 0} if given else {},
         compiler_params=pltpu.CompilerParams(vmem_limit_bytes=VMEM),
@@ -342,7 +333,7 @@
     other_p, squares = together((other_p, squares))
     side, one, three = cut(
         cut_first_kernel, place, [squares], projection,
-        [(0, 1), (0, 3), (1, 0), (1, 1), (1, 2), (1, 3)], [4 * WQ, 2 * WP + TOK, 2 * WP + TOK],
+        [(0, 1), (0, 3), (1, 0), (1, 1), (1, 2), (1, 3)], [4 * WQ, WP + WN + TOK, WP + WN + TOK],
     )
     one, three, side = send(one, "z", 1), send(three, "z", 3), send(side, "y_lo")
 
@@ -370,16 +361,17 @@
         place, total_p, far_p, targets[0], 0, WP, [shape(64, 2 * WP)] * 4,
         [pl.BlockSpec((64, WP), lambda j, s: (0, lax.rem(j + s[0], 2)))] * 4, put_p,
     )
-    near_low, near_high, far_2 = cut(
-        cut_second_kernel, place, [], projection, [(0, 2), (1, 2)], [WN, WP - WN, WP]
-    )
-    squares_p, one, three, total_q, far_2, near_low, near_high = together(
-        (squares_p, one, three, total_q, far_2, near_low, near_high)
+    late_1, early_2, late_2, late_3, far_2 = cut(
+        cut_second_kernel, place, [], projection,
+        [(0, 1), (0, 2), (0, 3), (1, 2)], [WP - WN, WN2, WP - WN2, WP - WN, WP],
+    )
+    squares_p, one, three, total_q, far_2, early_2, late = together(
+        (squares_p, one, three, total_q, far_2, early_2, (late_1, late_2, late_3))
     )
     far_q = send(total_q, "y_hi")
     mine_p = jnp.stack([squares_p[0]] + [send(squares_p[k], "z", k) for k in (1, 2, 3)])
-    middle = 2 * WP + TOK // 2
-    u_2 = (one[:, 2 * WP : middle], three[:, middle:])
+    middle = WP + TOK // 2
+    u_2 = (one[:, WP:middle], three[:, middle : WP + TOK])
     mine_p, far_q, far_2, u_2, squares_late = together((mine_p, far_q, far_2, u_2, squares))
 
     u_2 = (send(u_2[0], "z", 1), send(u_2[1], "z", 3))
@@ -390,21 +382,36 @@
         pl.BlockSpec((1, 64, 4 * WQ), lambda j, s: (lax.rem(j + s[0], 2), 0, 0)), put_q,
     )
     mine_q = jnp.stack([squares_q[0], send(squares_q[1], "y_lo")])
-    row_p, far_2, u_2, u_side, mine_q, near_low, near_high = together(
-        (row_p, far_2, u_2, u_side, mine_q, near_low, near_high)
-    )
-
-    near_low = send(near_low, "z", 2)
+    row_p, far_2, u_2, u_side, mine_q, early_2, late = together(
+        (row_p, far_2, u_2, u_side, mine_q, early_2, late)
+    )
+
+    half = TOK // 2
+
+    def units_in(array):
+        return [(array, half, WP // half), (array, half, WP // half + 1)]
+
+    def near_in(array, late):
+        return [(array, WN, (WP + TOK) // WN), (late, WP - WN, 0)]
+
+    units = [units_in(one), [(u, half, 0) for u in u_2], units_in(three)]
+    fars = [[(array, WP, 0)] for array in (one, far_2, three)]
+    early_2 = send(early_2, "z", 2)
     parts_p = [row_p, send(row_p, "core")]
-    p_far = send(set_p(place, squares, one, u_2, three, [far_2], projection, parts_p, 1, BF), "y_lo")
-    row_q, near_low, near_high = together((gathered(mine_q), near_low, near_high))
-    near_high = send(near_high, "z", 2)
+    p_far = send(set_p(place, squares, projection, units + fars, parts_p, 1, BF), "y_lo")
+    row_q, early_2, late = together((gathered(mine_q), early_2, late))
+    late = [send(piece, "z", k + 1) for k, piece in enumerate(late)]
     parts_q = [row_q, send(row_q, "core")]
     q_sums = set_q(place, squares, u_side, projection, side, parts_q)
-    q_sums, near_high = together((q_sums, near_high))
+    q_sums, late = together((q_sums, late))
     q_own, *q_send = q_sums
     q_far = [send(q, "z", k + 1) for k, q in enumerate(q_send)]
-    p_own = set_p(place, squares, one, u_2, three, [near_low, near_high], projection, parts_p, 0, F32)
+    nears = [
+        near_in(one, late[0]),
+        [(early_2, WN2, 0), (late[1], WP - WN2, 0)],
+        near_in(three, late[2]),
+    ]
+    p_own = set_p(place, squares, projection, units + nears, parts_p, 0, F32)
     merged = quotient(slice(0, WP), [p_own, p_far])
     return quotient(slice(WP, WIDE), [q_own, *q_far], merged)
 

time: 279 us -> 272 us (0.975)
  starting transfers between devices: 52.5 us -> 45 us
  other arithmetic: 8.01 us -> 14.7 us
  Pallas kernels: 86 us -> 80.3 us
    ppermute x23 -> x25, starting transfers between devices: 36.1 us -> 27.6 us  [send(): return lax.ppermute(value, axis, shift(k) if axis in ('z', 'x') else SWAP)]
    reduce_sum x2, other arithmetic: 1.84 us -> 5.67 us  [total(): return jnp.sum(blocks.astype(F32), axis=0).astype(BF)]
    pallas_call x2, Pallas kernels: 17.3 us -> 14.4 us  [cut(): pl.pallas_call(kernel, grid_spec=pltpu.PrefetchScalarGridSpec(num_scalar_...]
    unnamed x34 -> x28, local copies, waits for them, and re-layouts: 7.24 us -> 5.73 us
    ppermute x23 -> x25, waiting for transfers between devices: 82.3 us -> 83.1 us  [send(): return lax.ppermute(value, axis, shift(k) if axis in ('z', 'x') else SWAP)]
  transfers between devices with their start and end apart: 27 -> 29, of which waited for: 13 -> 14; matrix products, arithmetic and copies ran while one was open for 5% -> 7% of each run, Pallas kernels for 21% -> 20%
where the time goes in v5:
time: 272 us; the launch traced here: 270 us
  waiting for transfers between devices  117 us (43%)
  Pallas kernels  80.3 us (30%)
  starting transfers between devices  45 us (17%)
  other arithmetic  14.7 us (5%)
  local copies, waits for them, and re-layouts  12.7 us (5%)
    ppermute x25, waiting for transfers between devices, send(): return lax.ppermute(value, axis, shift(k) if axis in ('z', 'x') else SWAP)  83.1 us
    all_to_all x4, waiting for transfers between devices, over_x(): return lax.all_to_all(blocks, 'x', 0, 0, tiled=True)  33.7 us
    ppermute x25, starting transfers between devices, send(): return lax.ppermute(value, axis, shift(k) if axis in ('z', 'x') else SWAP)  27.6 us
    pallas_call x2, Pallas kernels, set_p(): pl.pallas_call(lambda *refs: set_p_kernel([len(group) for group in moved]...  20.6 us
    all_to_all x4, starting transfers between devices, over_x(): return lax.all_to_all(blocks, 'x', 0, 0, tiled=True)  17.4 us
    pallas_call x1, Pallas kernels, partial_outputs(): pl.pallas_call(partial_kernel, grid=(8,), in_specs=[pl.BlockSpec((TOK, UN...  14.6 us
    pallas_call x2, Pallas kernels, cut(): pl.pallas_call(kernel, grid_spec=pltpu.PrefetchScalarGridSpec(num_scalar_...  14.4 us
    pallas_call x2, Pallas kernels, quotient(): pl.pallas_call(lambda *refs: quotient_kernel(len(given), *refs), grid=(co...  9.59 us
  transfers between devices with their start and end apart: 29, of which 14 were waited for; matrix products, arithmetic and copies ran while one was open for 7% of the time, Pallas kernels for 20%

profile of v5, /device:TPU:1, one launch (start us, length us, event | category | flops | bytes accessed | tf_op | source)
XLA Modules:
  0.0 269.6 jit_solution(7773742484538589668)
XLA Ops:
  0.6 6.5 %shard_map.55 = (bf16[512,896]{1,0:T(8,128)(2,1)}, bf16[896,512]{1,0:T(8,128)(2,1)}) custom-call(s32[4]{0:T(128)} %pad_add_fusion.place_ref.refs_0_, s32[1,512]{1,0:T(1,128)} %rows_ref.1, bf16[1024,896]{1,0:T(8,128)(2,1)} %bitcast.39, bf16[1024,896]{1,0:T(8,128)(2,1)} %bitcast.40), custom_call_target="tpu_custom_call" | custom-call | flops 1 | bytes 1 | tf_op jit(solution)/shard_map/pallas_call | solution.py:52
  7.1 14.6 %shard_map.56 = (bf16[256,6144]{1,0:T(8,128)(2,1)}, bf16[256,6144]{1,0:T(8,128)(2,1)}, bf16[256,2048]{1,0:T(8,128)(2,1)}, bf16[256,2048]{1,0:T(8,128)(2,1)}) custom-call(bf16[512,896]{1,0:T(8,128)(2,1)} %get-tuple-element.73.hidden_ref, bf16[896,8192]{1,0:T(8,128)(2,1)} %bitcast.17, bf16[896,8192]{1,0:T(8,128)(2,1)} %bitcast.18), custom_call_target="tpu_custom_call" | custom-call | flops 1 | bytes 1 | tf_op jit(solution)/shard_map/pallas_call | solution.py:127
  23.2 8.6 %shard_map.57 = (bf16[896,1024]{1,0:T(8,128)(2,1)}, bf16[896,1920]{1,0:T(8,128)(2,1)}, bf16[896,1920]{1,0:T(8,128)(2,1)}) custom-call(s32[4]{0:T(128)} %pad_add_fusion.place_ref.refs_0_, bf16[896,512]{1,0:T(8,128)(2,1)} %get-tuple-element.108.squares_ref.own_units.refs_1_, bf16[896,8192]{1,0:T(8,128)(2,1)} %bitcast.19, bf16[896,8192]{1,0:T(8,128)(2,1)} %bitcast.20, ...), custom_call_target="tpu_custom_call" | custom-call | flops 1 | bytes 1 | tf_op jit(solution)/shard_map/pallas_call | solution.py:100
  35.9 4.7 %add_convert_fusion = bf16[256,6144]{1,0:T(8,128)(2,1)} fusion(bf16[256,6144]{1,0:T(8,128)(2,1)} %collective-permute-done, bf16[256,6144]{1,0:T(8,128)(2,1)S(1)} %copy-done.2), kind=kLoop, calls=%fused_computation | loop fusion | flops 6291456 | bytes 9437184 | tf_op jit(solution)/shard_map/convert_element_type | solution.py:341
  40.6 4.6 %all-to-all-start = ((bf16[4,64,6144]{2,1,0:T(8,128)(2,1)}), bf16[4,64,6144]{2,1,0:T(8,128)(2,1)}, u32[]{:S(2)}, u32[]{:S(2)}) async-start(bf16[4,64,6144]{2,1,0:T(8,128)(2,1)} %bitcast.37), calls=%async_computation | async-start | bytes 6291456 | tf_op jit(solution)/shard_map/all_to_all | solution.py:345
  52.3 30.4 %all-to-all-done = bf16[4,64,6144]{2,1,0:T(8,128)(2,1)} async-done(((bf16[4,64,6144]{2,1,0:T(8,128)(2,1)}), bf16[4,64,6144]{2,1,0:T(8,128)(2,1)}, u32[]{:S(2)}, u32[]{:S(2)}) %all-to-all-start) | async-done | bytes 3145760 | tf_op jit(solution)/shard_map/all_to_all | solution.py:345
  82.7 3.5 %reduce_sum.24.refs_1_ = bf16[64,6144]{1,0:T(8,128)(2,1)} reduce(bf16[4,64,6144]{2,1,0:T(8,128)(2,1)} %all-to-all-done, bf16[]{:T(256)} %constant.19.clone.1), dimensions={0}, to_apply=%region_0.0 | reduce | flops 1179648 | bytes 3932162 | tf_op jit(solution)/shard_map/reduce_sum | solution.py:348
  89.8 4.3 %all-to-all-start.1 = ((bf16[4,64,2048]{2,1,0:T(8,128)(2,1)}), bf16[4,64,2048]{2,1,0:T(8,128)(2,1)}, u32[]{:S(2)}, u32[]{:S(2)}) async-start(bf16[4,64,2048]{2,1,0:T(8,128)(2,1)} %bitcast.38), calls=%async_computation.1 | async-start | bytes 2097152 | tf_op jit(solution)/shard_map/all_to_all | solution.py:345
  94.1 5.9 %shard_map.59 = (bf16[896,128]{1,0:T(8,128)(2,1)}, bf16[896,512]{1,0:T(8,128)(2,1)}, bf16[896,256]{1,0:T(8,128)(2,1)}, bf16[896,128]{1,0:T(8,128)(2,1)}, bf16[896,768]{1,0:T(8,128)(2,1)}) custom-call(s32[4]{0:T(128)} %pad_add_fusion.place_ref.refs_0_, bf16[896,8192]{1,0:T(8,128)(2,1)} %bitcast.25, bf16[896,8192]{1,0:T(8,128)(2,1)} %bitcast.26, ...), custom_call_target="tpu_custom_call" | custom-call | flops 1 | bytes 1 | tf_op jit(solution)/shard_map/pallas_call | solution.py:100
  99.9 6.7 %collective-permute-done.3.refs_2_ = bf16[64,6144]{1,0:T(8,128)(2,1)} collective-permute-done((bf16[64,6144]{1,0:T(8,128)(2,1)}, bf16[64,6144]{1,0:T(8,128)(2,1)}, u32[]{:S(2)}, u32[]{:S(2)}) %collective-permute-start.3) | collective-permute-done | bytes 786464 | tf_op jit(solution)/shard_map/ppermute | solution.py:326
  119.7 5.3 %collective-permute-done.6 = bf16[64,1536]{1,0:T(8,128)(2,1)S(1)} collective-permute-done((bf16[64,1536]{1,0:T(8,128)(2,1)}, bf16[64,1536]{1,0:T(8,128)(2,1)S(1)}, u32[]{:S(2)}, u32[]{:S(2)}) %collective-permute-start.6) | collective-permute-done | bytes 196640 | tf_op jit(solution)/shard_map/ppermute | solution.py:326
  128.1 4.2 %all-to-all-start.2 = ((bf16[4,4,64,1536]{3,2,1,0:T(8,128)(2,1)}), bf16[4,4,64,1536]{3,2,1,0:T(8,128)(2,1)S(1)}, u32[]{:S(2)}, u32[]{:S(2)}) async-start(bf16[4,4,64,1536]{3,2,1,0:T(8,128)(2,1)} %broadcast_in_dim.4), calls=%async_computation.2 | async-start | bytes 6291456 | tf_op jit(solution)/shard_map/all_to_all | solution.py:345
  140.5 14.5 %collective-permute-done.14 = bf16[64,1024]{1,0:T(8,128)(2,1)S(1)} collective-permute-done((bf16[64,1024]{1,0:T(8,128)(2,1)S(1)}, bf16[64,1024]{1,0:T(8,128)(2,1)S(1)}, u32[]{:S(2)}, u32[]{:S(2)}) %collective-permute-start.14) | collective-permute-done | bytes 131104 | tf_op jit(solution)/shard_map/ppermute | solution.py:326
  155.0 20.9 %collective-permute-done.11.refs_5_ = bf16[896,256]{1,0:T(8,128)(2,1)S(1)} collective-permute-done((bf16[896,256]{1,0:T(8,128)(2,1)}, bf16[896,256]{1,0:T(8,128)(2,1)S(1)}, u32[]{:S(2)}, u32[]{:S(2)}) %collective-permute-start.11) | collective-permute-done | bytes 458784 | tf_op jit(solution)/shard_map/ppermute | solution.py:326
  179.9 4.2 %all-to-all-start.3 = ((bf16[4,2,64,1024]{3,2,1,0:T(8,128)(2,1)}), bf16[4,2,64,1024]{3,2,1,0:T(8,128)(2,1)}, u32[]{:S(2)}, u32[]{:S(2)}) async-start(bf16[4,2,64,1024]{3,2,1,0:T(8,128)(2,1)} %broadcast_in_dim.5), calls=%async_computation.3 | async-start | bytes 2097152 | tf_op jit(solution)/shard_map/all_to_all | solution.py:345
  184.1 10.0 %shard_map.63 = bf16[2,896,768]{2,1,0:T(8,128)(2,1)} custom-call(s32[4]{0:T(128)} %pad_add_fusion.place_ref.refs_0_, bf16[896,512]{1,0:T(8,128)(2,1)} %get-tuple-element.108.squares_ref.own_units.refs_1_, bf16[896,8192]{1,0:T(8,128)(2,1)} %bitcast.29, bf16[896,1920]{1,0:T(8,128)(2,1)} %copy-done, bf16[896,1920]{1,0:T(8,128)(2,1)} %copy-done, ...), custom_call_target="tpu_custom_call" | custom-call | flops 1 | bytes 1 | tf_op jit(solution)/shard_map/pallas_call | solution.py:222
  195.3 3.3 %all-to-all-done.3.refs_0_ = bf16[4,2,64,1024]{3,2,1,0:T(8,128)(2,1)} async-done(((bf16[4,2,64,1024]{3,2,1,0:T(8,128)(2,1)}), bf16[4,2,64,1024]{3,2,1,0:T(8,128)(2,1)}, u32[]{:S(2)}, u32[]{:S(2)}) %all-to-all-start.3) | async-done | bytes 1048608 | tf_op jit(solution)/shard_map/all_to_all | solution.py:345
  198.6 3.6 %collective-permute-done.15.refs_11_ = bf16[896,512]{1,0:T(8,128)(2,1)} collective-permute-done((bf16[896,512]{1,0:T(8,128)(2,1)}, bf16[896,512]{1,0:T(8,128)(2,1)}, u32[]{:S(2)}, u32[]{:S(2)}) %collective-permute-start.15) | collective-permute-done | bytes 917536 | tf_op jit(solution)/shard_map/ppermute | solution.py:326
  206.7 8.5 %shard_map.61 = (f32[2,896,256]{2,1,0:T(8,128)}, bf16[2,896,256]{2,1,0:T(8,128)(2,1)}, bf16[2,896,256]{2,1,0:T(8,128)(2,1)}, bf16[2,896,256]{2,1,0:T(8,128)(2,1)}) custom-call(s32[4]{0:T(128)} %pad_add_fusion.place_ref.refs_0_, bf16[896,512]{1,0:T(8,128)(2,1)} %get-tuple-element.108.squares_ref.own_units.refs_1_, bf16[896,512]{1,0:T(8,128)(2,1)} %copy-done.7, ...), custom_call_target="tpu_custom_call" | custom-call | flops 1 | bytes 1 | tf_op jit(solution)/shard_map/pallas_call | solution.py:266
  215.2 6.4 %collective-permute-done.17.refs_10_ = bf16[896,128]{1,0:T(8,128)(2,1)S(1)} collective-permute-done((bf16[896,128]{1,0:T(8,128)(2,1)}, bf16[896,128]{1,0:T(8,128)(2,1)S(1)}, u32[]{:S(2)}, u32[]{:S(2)}) %collective-permute-start.17) | collective-permute-done | bytes 229408 | tf_op jit(solution)/shard_map/ppermute | solution.py:326
  224.4 10.5 %shard_map.62.refs_0_ = f32[2,896,768]{2,1,0:T(8,128)} custom-call(s32[4]{0:T(128)} %pad_add_fusion.place_ref.refs_0_, bf16[896,512]{1,0:T(8,128)(2,1)} %get-tuple-element.108.squares_ref.own_units.refs_1_, bf16[896,8192]{1,0:T(8,128)(2,1)} %bitcast.34, bf16[896,1920]{1,0:T(8,128)(2,1)} %copy-done, bf16[896,1920]{1,0:T(8,128)(2,1)} %copy-done, ...), custom_call_target="tpu_custom_call" | custom-call | flops 1 | bytes 1 | tf_op jit(solution)/shard_map/pallas_call | solution.py:222
  234.9 20.0 %collective-permute-done.24.refs_1_ = bf16[2,896,768]{2,1,0:T(8,128)(2,1)S(1)} collective-permute-done((bf16[2,896,768]{2,1,0:T(8,128)(2,1)}, bf16[2,896,768]{2,1,0:T(8,128)(2,1)S(1)}, u32[]{:S(2)}, u32[]{:S(2)}) %collective-permute-start.24) | collective-permute-done | bytes 2752544 | tf_op jit(solution)/shard_map/ppermute | solution.py:326
  256.5 5.4 %shard_map.64.refs_4_ = f32[896,1024]{1,0:T(8,128)} custom-call(f32[2,896,768]{2,1,0:T(8,128)} %shard_map.62.refs_0_, bf16[2,896,768]{2,1,0:T(8,128)(2,1)} %copy-done.3), custom_call_target="tpu_custom_call" | custom-call | flops 1 | bytes 1 | tf_op jit(solution)/shard_map/pallas_call | solution.py:304
  265.4 4.2 %shard_map.65 = f32[896,1024]{1,0:T(8,128)} custom-call(f32[2,896,256]{2,1,0:T(8,128)} %get-tuple-element.129.refs_0_, bf16[2,896,256]{2,1,0:T(8,128)(2,1)} %copy-done.8, bf16[2,896,256]{2,1,0:T(8,128)(2,1)} %copy-done.9, bf16[2,896,256]{2,1,0:T(8,128)(2,1)} %copy-done.10, f32[896,1024]{1,0:T(8,128)} %shard_map.64.refs_4_), custom_call_target="tpu_custom_call", output_to_operand_aliasing={{}: (4, {})} | custom-call | flops 1 | bytes 1 | tf_op jit(solution)/shard_map/pallas_call | solution.py:304
  (85 shorter events, 58.6 us)
Async XLA Ops:
  21.7 14.1 %collective-permute-start = (bf16[256,6144]{1,0:T(8,128)(2,1)}, bf16[256,6144]{1,0:T(8,128)(2,1)}, u32[]{:S(2)}, u32[]{:S(2)}) collective-permute-start(bf16[256,6144]{1,0:T(8,128)(2,1)} %get-tuple-element.78), channel_id=1, source_target_pairs={{0,1},{1,0},{2,3},{3,2},{4,5},{5,4},{6,7},{7,6},{8,9},{9,8},{10,11... | collective-permute-start | bytes 9437192 | tf_op jit(solution)/shard_map/ppermute | solution.py:326
  31.8 80.3 %collective-permute-start.4 = (bf16[896,1920]{1,0:T(8,128)(2,1)}, bf16[896,1920]{1,0:T(8,128)(2,1)S(1)}, u32[]{:S(2)}, u32[]{:S(2)}) collective-permute-start(bf16[896,1920]{1,0:T(8,128)(2,1)} %get-tuple-element.88), channel_id=1, source_target_pairs={{0,16},{16,32},{32,48},{48,0},{1,17},{17,33},{33,49},{49,1},{2,18}... | collective-permute-start | bytes 10321928 | tf_op jit(solution)/shard_map/ppermute | solution.py:326
  33.7 78.4 %collective-permute-start.5 = (bf16[896,1920]{1,0:T(8,128)(2,1)}, bf16[896,1920]{1,0:T(8,128)(2,1)}, u32[]{:S(2)}, u32[]{:S(2)}) collective-permute-start(bf16[896,1920]{1,0:T(8,128)(2,1)} %get-tuple-element.89), channel_id=1, source_target_pairs={{0,48},{16,0},{32,16},{48,32},{1,49},{17,1},{33,17},{49,33},{2,50}... | collective-permute-start | bytes 10321928 | tf_op jit(solution)/shard_map/ppermute | solution.py:326
  40.6 42.1 %all-to-all-start = ((bf16[4,64,6144]{2,1,0:T(8,128)(2,1)}), bf16[4,64,6144]{2,1,0:T(8,128)(2,1)}, u32[]{:S(2)}, u32[]{:S(2)}) async-start(bf16[4,64,6144]{2,1,0:T(8,128)(2,1)} %bitcast.37), calls=%async_computation | async-start | bytes 6291456 | tf_op jit(solution)/shard_map/all_to_all | solution.py:345
  45.2 41.7 %collective-permute-start.2 = (bf16[896,1024]{1,0:T(8,128)(2,1)}, bf16[896,1024]{1,0:T(8,128)(2,1)}, u32[]{:S(2)}, u32[]{:S(2)}) collective-permute-start(bf16[896,1024]{1,0:T(8,128)(2,1)} %get-tuple-element.82), channel_id=1, source_target_pairs={{0,64},{64,0},{1,65},{65,1},{2,66},{66,2},{3,67},{67,3},{4,68},{68... | collective-permute-start | bytes 5505032 | tf_op jit(solution)/shard_map/ppermute | solution.py:326
  86.9 19.7 %collective-permute-start.3 = (bf16[64,6144]{1,0:T(8,128)(2,1)}, bf16[64,6144]{1,0:T(8,128)(2,1)}, u32[]{:S(2)}, u32[]{:S(2)}) collective-permute-start(bf16[64,6144]{1,0:T(8,128)(2,1)} %reduce_sum.24.refs_1_), channel_id=1, source_target_pairs={{0,8},{8,0},{1,9},{9,1},{2,10},{10,2},{3,11},{11,3},{4,12},{12,4},... | collective-permute-start | bytes 2359304 | tf_op jit(solution)/shard_map/ppermute | solution.py:326
  89.8 20.1 %all-to-all-start.1 = ((bf16[4,64,2048]{2,1,0:T(8,128)(2,1)}), bf16[4,64,2048]{2,1,0:T(8,128)(2,1)}, u32[]{:S(2)}, u32[]{:S(2)}) async-start(bf16[4,64,2048]{2,1,0:T(8,128)(2,1)} %bitcast.38), calls=%async_computation.1 | async-start | bytes 2097152 | tf_op jit(solution)/shard_map/all_to_all | solution.py:345
  113.4 11.7 %collective-permute-start.6 = (bf16[64,1536]{1,0:T(8,128)(2,1)}, bf16[64,1536]{1,0:T(8,128)(2,1)S(1)}, u32[]{:S(2)}, u32[]{:S(2)}) collective-permute-start(bf16[64,1536]{1,0:T(8,128)(2,1)} %get-tuple-element.97), channel_id=1, source_target_pairs={{0,16},{16,32},{32,48},{48,0},{1,17},{17,33},{33,49},{49,1},{2,18}... | collective-permute-start | bytes 589832 | tf_op jit(solution)/shard_map/ppermute | solution.py:326
  114.0 12.1 %collective-permute-start.9 = (bf16[64,2048]{1,0:T(8,128)(2,1)}, bf16[64,2048]{1,0:T(8,128)(2,1)}, u32[]{:S(2)}, u32[]{:S(2)}) collective-permute-start(bf16[64,2048]{1,0:T(8,128)(2,1)} %reduce_sum.25.refs_1_), channel_id=1, source_target_pairs={{0,8},{8,0},{1,9},{9,1},{2,10},{10,2},{3,11},{11,3},{4,12},{12,4},... | collective-permute-start | bytes 786440 | tf_op jit(solution)/shard_map/ppermute | solution.py:326
  128.1 49.8 %all-to-all-start.2 = ((bf16[4,4,64,1536]{3,2,1,0:T(8,128)(2,1)}), bf16[4,4,64,1536]{3,2,1,0:T(8,128)(2,1)S(1)}, u32[]{:S(2)}, u32[]{:S(2)}) async-start(bf16[4,4,64,1536]{3,2,1,0:T(8,128)(2,1)} %broadcast_in_dim.4), calls=%async_computation.2 | async-start | bytes 6291456 | tf_op jit(solution)/shard_map/all_to_all | solution.py:345
  132.3 45.6 %collective-permute-start.10 = (bf16[896,768]{1,0:T(8,128)(2,1)}, bf16[896,768]{1,0:T(8,128)(2,1)}, u32[]{:S(2)}, u32[]{:S(2)}) collective-permute-start(bf16[896,768]{1,0:T(8,128)(2,1)} %get-tuple-element.105), channel_id=1, source_target_pairs={{0,32},{16,48},{32,0},{48,16},{1,33},{17,49},{33,1},{49,17},{2,34}... | collective-permute-start | bytes 4128776 | tf_op jit(solution)/shard_map/ppermute | solution.py:326
  132.3 43.7 %collective-permute-start.13 = (bf16[896,512]{1,0:T(8,128)(2,1)}, bf16[896,512]{1,0:T(8,128)(2,1)S(1)}, u32[]{:S(2)}, u32[]{:S(2)}) collective-permute-start(bf16[896,512]{1,0:T(8,128)(2,1)} %get-tuple-element.108.squares_ref.own_units.refs_1_), channel_id=1, source_target_pairs={{0,64},{64,0},{1,65},{65,1},{2,66},{66,2},{3,67},{67,3},{4,68},{68... | collective-permute-start | bytes 2752520 | tf_op jit(solution)/shard_map/ppermute | solution.py:326
  133.6 42.4 %collective-permute-start.11 = (bf16[896,256]{1,0:T(8,128)(2,1)}, bf16[896,256]{1,0:T(8,128)(2,1)S(1)}, u32[]{:S(2)}, u32[]{:S(2)}) collective-permute-start(bf16[896,256]{1,0:T(8,128)(2,1)} %slice.12), channel_id=1, source_target_pairs={{0,16},{16,32},{32,48},{48,0},{1,17},{17,33},{33,49},{49,1},{2,18}... | collective-permute-start | bytes 1376264 | tf_op jit(solution)/shard_map/ppermute | solution.py:326
  133.6 42.4 %collective-permute-start.12 = (bf16[896,256]{1,0:T(8,128)(2,1)}, bf16[896,256]{1,0:T(8,128)(2,1)S(1)}, u32[]{:S(2)}, u32[]{:S(2)}) collective-permute-start(bf16[896,256]{1,0:T(8,128)(2,1)} %slice.13), channel_id=1, source_target_pairs={{0,48},{16,0},{32,16},{48,32},{1,49},{17,1},{33,17},{49,33},{2,50}... | collective-permute-start | bytes 1376264 | tf_op jit(solution)/shard_map/ppermute | solution.py:326
  140.1 14.9 %collective-permute-start.14 = (bf16[64,1024]{1,0:T(8,128)(2,1)S(1)}, bf16[64,1024]{1,0:T(8,128)(2,1)S(1)}, u32[]{:S(2)}, u32[]{:S(2)}) collective-permute-start(bf16[64,1024]{1,0:T(8,128)(2,1)S(1)} %get-tuple-element.142), channel_id=1, source_target_pairs={{0,64},{64,0},{1,65},{65,1},{2,66},{66,2},{3,67},{67,3},{4,68},{68... | collective-permute-start | bytes 393224 | tf_op jit(solution)/shard_map/ppermute | solution.py:326
  178.5 23.7 %collective-permute-start.15 = (bf16[896,512]{1,0:T(8,128)(2,1)}, bf16[896,512]{1,0:T(8,128)(2,1)}, u32[]{:S(2)}, u32[]{:S(2)}) collective-permute-start(bf16[896,512]{1,0:T(8,128)(2,1)} %get-tuple-element.117), channel_id=1, source_target_pairs={{0,32},{16,48},{32,0},{48,16},{1,33},{17,49},{33,1},{49,17},{2,34}... | collective-permute-start | bytes 2752520 | tf_op jit(solution)/shard_map/ppermute | solution.py:326
  179.9 18.8 %all-to-all-start.3 = ((bf16[4,2,64,1024]{3,2,1,0:T(8,128)(2,1)}), bf16[4,2,64,1024]{3,2,1,0:T(8,128)(2,1)}, u32[]{:S(2)}, u32[]{:S(2)}) async-start(bf16[4,2,64,1024]{3,2,1,0:T(8,128)(2,1)} %broadcast_in_dim.5), calls=%async_computation.3 | async-start | bytes 2097152 | tf_op jit(solution)/shard_map/all_to_all | solution.py:345
  194.2 60.8 %collective-permute-start.24 = (bf16[2,896,768]{2,1,0:T(8,128)(2,1)}, bf16[2,896,768]{2,1,0:T(8,128)(2,1)S(1)}, u32[]{:S(2)}, u32[]{:S(2)}) collective-permute-start(bf16[2,896,768]{2,1,0:T(8,128)(2,1)} %shard_map.63), channel_id=1, source_target_pairs={{0,64},{64,0},{1,65},{65,1},{2,66},{66,2},{3,67},{67,3},{4,68},{68... | collective-permute-start | bytes 8257544 | tf_op jit(solution)/shard_map/ppermute | solution.py:326
  203.1 18.5 %collective-permute-start.18 = (bf16[896,256]{1,0:T(8,128)(2,1)}, bf16[896,256]{1,0:T(8,128)(2,1)S(1)}, u32[]{:S(2)}, u32[]{:S(2)}) collective-permute-start(bf16[896,256]{1,0:T(8,128)(2,1)} %get-tuple-element.127), channel_id=1, source_target_pairs={{0,32},{16,48},{32,0},{48,16},{1,33},{17,49},{33,1},{49,17},{2,34}... | collective-permute-start | bytes 1376264 | tf_op jit(solution)/shard_map/ppermute | solution.py:326
  203.1 18.5 %collective-permute-start.17 = (bf16[896,128]{1,0:T(8,128)(2,1)}, bf16[896,128]{1,0:T(8,128)(2,1)S(1)}, u32[]{:S(2)}, u32[]{:S(2)}) collective-permute-start(bf16[896,128]{1,0:T(8,128)(2,1)} %get-tuple-element.126), channel_id=1, source_target_pairs={{0,16},{16,32},{32,48},{48,0},{1,17},{17,33},{33,49},{49,1},{2,18}... | collective-permute-start | bytes 688136 | tf_op jit(solution)/shard_map/ppermute | solution.py:326
  204.0 17.6 %collective-permute-start.19 = (bf16[896,128]{1,0:T(8,128)(2,1)}, bf16[896,128]{1,0:T(8,128)(2,1)S(1)}, u32[]{:S(2)}, u32[]{:S(2)}) collective-permute-start(bf16[896,128]{1,0:T(8,128)(2,1)} %get-tuple-element.128), channel_id=1, source_target_pairs={{0,48},{16,0},{32,16},{48,32},{1,49},{17,1},{33,17},{49,33},{2,50}... | collective-permute-start | bytes 688136 | tf_op jit(solution)/shard_map/ppermute | solution.py:326
  221.6 40.4 %collective-permute-start.20 = (bf16[2,896,256]{2,1,0:T(8,128)(2,1)}, bf16[2,896,256]{2,1,0:T(8,128)(2,1)S(1)}, u32[]{:S(2)}, u32[]{:S(2)}) collective-permute-start(bf16[2,896,256]{2,1,0:T(8,128)(2,1)} %get-tuple-element.130), channel_id=1, source_target_pairs={{0,16},{16,32},{32,48},{48,0},{1,17},{17,33},{33,49},{49,1},{2,18}... | collective-permute-start | bytes 2752520 | tf_op jit(solution)/shard_map/ppermute | solution.py:326
  221.7 41.9 %collective-permute-start.21 = (bf16[2,896,256]{2,1,0:T(8,128)(2,1)}, bf16[2,896,256]{2,1,0:T(8,128)(2,1)S(1)}, u32[]{:S(2)}, u32[]{:S(2)}) collective-permute-start(bf16[2,896,256]{2,1,0:T(8,128)(2,1)} %get-tuple-element.131), channel_id=1, source_target_pairs={{0,32},{16,48},{32,0},{48,16},{1,33},{17,49},{33,1},{49,17},{2,34}... | collective-permute-start | bytes 2752520 | tf_op jit(solution)/shard_map/ppermute | solution.py:326
  223.7 40.5 %collective-permute-start.22 = (bf16[2,896,256]{2,1,0:T(8,128)(2,1)}, bf16[2,896,256]{2,1,0:T(8,128)(2,1)S(1)}, u32[]{:S(2)}, u32[]{:S(2)}) collective-permute-start(bf16[2,896,256]{2,1,0:T(8,128)(2,1)} %get-tuple-element.132), channel_id=1, source_target_pairs={{0,48},{16,0},{32,16},{48,32},{1,49},{17,1},{33,17},{49,33},{2,50}... | collective-permute-start | bytes 2752520 | tf_op jit(solution)/shard_map/ppermute | solution.py:326
  (19 other events, 80.8 us)

commit v6 on v5

--- a/solution.py
+++ b/solution.py
@@ -17,7 +17,7 @@
 WP = 768
 WQ = WIDE - WP
 WN = 640
-WN2 = 512
+WN2 = 640
 VMEM = 56 * 2**20
 SHRINK = 1.0 / math.sqrt(FF)
 SWAP = [(0, 1), (1, 0)]
@@ -106,38 +106,35 @@
             out_specs=[rows_of(width) for width in widths],
         ),
         out_shape=[shape(UNITS, width) for width in widths],
-        compiler_params=pltpu.CompilerParams(vmem_limit_bytes=VMEM),
+        compiler_params=pltpu.CompilerParams(vmem_limit_bytes=50 * 2**20),
         cost_estimate=SMALL,
     )(place, *extra, *[projection] * len(places))
 
 
-def partial_kernel(hidden_ref, w_low, w_high, own_p, other_p, own_q, other_q):
+def partial_kernel(hidden_ref, *refs):
     hidden = hidden_ref[...]
-    low = (jnp.dot(hidden, w_low[...], preferred_element_type=F32) * SHRINK).astype(BF)
-    high = (jnp.dot(hidden, w_high[...], preferred_element_type=F32) * SHRINK).astype(BF)
-    edge = WP - WIDE // 2
-    for ref_p, ref_q, rows in ((own_p, own_q, slice(0, 256)), (other_p, other_q, slice(256, 512))):
-        ref_p[:, : WIDE // 2] = low[rows]
-        ref_p[:, WIDE // 2 :] = high[rows, :edge]
-        ref_q[...] = high[rows, edge:]
-
-
-def partial_outputs(hidden, projection):
-    half = WIDE // 2
+    *streams, own, other = refs
+    for i, stream in enumerate(streams):
+        columns = slice(i * WQ, i * WQ + WQ)
+        product = (jnp.dot(hidden, stream[...], preferred_element_type=F32) * SHRINK).astype(BF)
+        own[:, columns] = product[:256]
+        other[:, columns] = product[256:]
+
+
+def partial_outputs(hidden, projection, low, high):
+    width = high - low
+    streams = [
+        pl.BlockSpec((UNITS, WQ), lambda j, i=i: (0, j * (WIDE // WQ) + i)) for i in range(low // WQ, high // WQ)
+    ]
     return pl.pallas_call(
         partial_kernel,
         grid=(8,),
-        in_specs=[
-            pl.BlockSpec((TOK, UNITS), lambda j: (0, 0)),
-            pl.BlockSpec((UNITS, half), lambda j: (0, 2 * j)),
-            pl.BlockSpec((UNITS, half), lambda j: (0, 2 * j + 1)),
-        ],
-        out_specs=[pl.BlockSpec((256, WP), lambda j: (0, j))] * 2
-        + [pl.BlockSpec((256, WQ), lambda j: (0, j))] * 2,
-        out_shape=[shape(256, 8 * WP)] * 2 + [shape(256, 8 * WQ)] * 2,
-        compiler_params=pltpu.CompilerParams(vmem_limit_bytes=VMEM),
-        cost_estimate=SMALL,
-    )(hidden, projection, projection)
+        in_specs=[pl.BlockSpec((TOK, UNITS), lambda j: (0, 0)), *streams],
+        out_specs=[pl.BlockSpec((256, width), lambda j: (0, j))] * 2,
+        out_shape=[shape(256, 8 * width)] * 2,
+        compiler_params=pltpu.CompilerParams(vmem_limit_bytes=50 * 2**20),
+        cost_estimate=SMALL,
+    )(hidden, *[projection] * len(streams))
 
 
 def square_kernel(low, high, put, place_ref, total_ref, far_ref, targets_ref, *outs):
@@ -278,7 +275,7 @@
             out_specs=[pl.BlockSpec((2, tall, WQ), lambda u, s: (0, u, 0))] * 4,
             scratch_shapes=[pltpu.VMEM((2, TOK, 4 * WQ), BF)],
         ),
-        out_shape=[shape(2, UNITS, WQ, dtype=F32)] + [shape(2, UNITS, WQ)] * 3,
+        out_shape=[shape(2, UNITS, WQ)] * 4,
         compiler_params=pltpu.CompilerParams(vmem_limit_bytes=VMEM),
         cost_estimate=SMALL,
     )(place, units, far_units, projection, projection, projection, projection, far, *parts)
@@ -288,7 +285,7 @@
     out_ref = refs[-1]
 
     def total(i):
-        value = refs[0][i]
+        value = refs[0][i].astype(F32)
         for ref in refs[1 : -1 - n_given]:
             value = value + ref[i].astype(F32)
         return value
@@ -329,7 +326,7 @@
 
     hidden, squares = make_hidden(place, token_rows, gate_cache[0], up_cache[0])
 
-    own_p, other_p, own_q, other_q = partial_outputs(hidden, projection)
+    own_p, other_p = partial_outputs(hidden, projection, 0, WP)
     other_p, squares = together((other_p, squares))
     side, one, three = cut(
         cut_first_kernel, place, [squares], projection,
@@ -350,13 +347,14 @@
     def gathered(part):
         return over_x(jnp.broadcast_to(part[None], (4,) + part.shape))
 
-    blocks_p = over_x(pair(own_p, other_p))
-    pair_q = pair(own_q, other_q)
+    pair_p, hidden = together((pair(own_p, other_p), hidden))
+    blocks_p = over_x(pair_p)
+    pair_q = pair(*partial_outputs(hidden, projection, WP, WIDE))
     blocks_p, pair_q = together((blocks_p, pair_q))
     total_p = total(blocks_p)
     total_p, side = together((total_p, side))
     far_p = send(total_p, "y_hi")
-    total_q = total(over_x(pair_q))
+    blocks_q = over_x(pair_q)
     squares_p = error_squares(
         place, total_p, far_p, targets[0], 0, WP, [shape(64, 2 * WP)] * 4,
         [pl.BlockSpec((64, WP), lambda j, s: (0, lax.rem(j + s[0], 2)))] * 4, put_p,
@@ -365,14 +363,15 @@
         cut_second_kernel, place, [], projection,
         [(0, 1), (0, 2), (0, 3), (1, 2)], [WP - WN, WN2, WP - WN2, WP - WN, WP],
     )
-    squares_p, one, three, total_q, far_2, early_2, late = together(
-        (squares_p, one, three, total_q, far_2, early_2, (late_1, late_2, late_3))
-    )
+    squares_p, one, three, blocks_q, far_2, early_2, late = together(
+        (squares_p, one, three, blocks_q, far_2, early_2, (late_1, late_2, late_3))
+    )
+    total_q = total(blocks_q)
     far_q = send(total_q, "y_hi")
     mine_p = jnp.stack([squares_p[0]] + [send(squares_p[k], "z", k) for k in (1, 2, 3)])
     middle = WP + TOK // 2
     u_2 = (one[:, WP:middle], three[:, middle : WP + TOK])
-    mine_p, far_q, far_2, u_2, squares_late = together((mine_p, far_q, far_2, u_2, squares))
+    mine_p, far_2, u_2, squares_late = together((mine_p, far_2, u_2, squares))
 
     u_2 = (send(u_2[0], "z", 1), send(u_2[1], "z", 3))
     far_2, u_side = send(far_2, "z", 2), send(squares_late, "y_lo")
@@ -403,15 +402,15 @@
     late = [send(piece, "z", k + 1) for k, piece in enumerate(late)]
     parts_q = [row_q, send(row_q, "core")]
     q_sums = set_q(place, squares, u_side, projection, side, parts_q)
-    q_sums, late = together((q_sums, late))
     q_own, *q_send = q_sums
+    q_send[1], late = together((q_send[1], late))
     q_far = [send(q, "z", k + 1) for k, q in enumerate(q_send)]
     nears = [
         near_in(one, late[0]),
         [(early_2, WN2, 0), (late[1], WP - WN2, 0)],
         near_in(three, late[2]),
     ]
-    p_own = set_p(place, squares, projection, units + nears, parts_p, 0, F32)
+    p_own = set_p(place, squares, projection, units + nears, parts_p, 0, BF)
     merged = quotient(slice(0, WP), [p_own, p_far])
     return quotient(slice(WP, WIDE), [q_own, *q_far], merged)
 

time: 272 us -> 268 us (0.985)
  waiting for transfers between devices: 117 us -> 102 us
  starting transfers between devices: 45 us -> 55.1 us
  local copies, waits for them, and re-layouts: 12.7 us -> 15.8 us
    ppermute x25, starting transfers between devices: 27.6 us -> 37.3 us  [send(): return lax.ppermute(value, axis, shift(k) if axis in ('z', 'x') else SWAP)]
    ppermute x25, waiting for transfers between devices: 83.1 us -> 74.2 us  [send(): return lax.ppermute(value, axis, shift(k) if axis in ('z', 'x') else SWAP)]
    all_to_all x4, waiting for transfers between devices: 33.7 us -> 28.3 us  [over_x(): return lax.all_to_all(blocks, 'x', 0, 0, tiled=True)]
    pallas_call x1 -> x2, Pallas kernels: 14.6 us -> 18.4 us  [partial_outputs(): pl.pallas_call(partial_kernel, grid=(8,), in_specs=[pl.BlockSpec((TOK, UN...]
    convert_element_type x2, other arithmetic: 7.31 us -> 4.15 us  [pair(): both = (own.astype(F32) + send(other, 'core').astype(F32)).astype(BF)]
    unnamed x28 -> x44, local copies, waits for them, and re-layouts: 5.73 us -> 7.14 us
  transfers between devices with their start and end apart: 29 -> 29, of which waited for: 14 -> 14; matrix products, arithmetic and copies ran while one was open for 7% -> 6% of each run, Pallas kernels for 20% -> 22%
where the time goes in v6:
time: 268 us; the launch traced here: 266 us
  waiting for transfers between devices  102 us (38%)
  Pallas kernels  80.6 us (30%)
  starting transfers between devices  55.1 us (21%)
  local copies, waits for them, and re-layouts  15.8 us (6%)
  other arithmetic  12.2 us (5%)
    ppermute x25, waiting for transfers between devices, send(): return lax.ppermute(value, axis, shift(k) if axis in ('z', 'x') else SWAP)  74.2 us
    ppermute x25, starting transfers between devices, send(): return lax.ppermute(value, axis, shift(k) if axis in ('z', 'x') else SWAP)  37.3 us
    all_to_all x4, waiting for transfers between devices, over_x(): return lax.all_to_all(blocks, 'x', 0, 0, tiled=True)  28.3 us
    pallas_call x2, Pallas kernels, set_p(): pl.pallas_call(lambda *refs: set_p_kernel([len(group) for group in moved]...  20.2 us
    pallas_call x2, Pallas kernels, partial_outputs(): pl.pallas_call(partial_kernel, grid=(8,), in_specs=[pl.BlockSpec((TOK, UN...  18.4 us
    all_to_all x4, starting transfers between devices, over_x(): return lax.all_to_all(blocks, 'x', 0, 0, tiled=True)  17.8 us
    pallas_call x2, Pallas kernels, cut(): pl.pallas_call(kernel, grid_spec=pltpu.PrefetchScalarGridSpec(num_scalar_...  12.1 us
    pallas_call x2, Pallas kernels, quotient(): pl.pallas_call(lambda *refs: quotient_kernel(len(given), *refs), grid=(co...  9.02 us
  transfers between devices with their start and end apart: 29, of which 14 were waited for; matrix products, arithmetic and copies ran while one was open for 6% of the time, Pallas kernels for 22%

profile of v6, /device:TPU:1, one launch (start us, length us, event | category | flops | bytes accessed | tf_op | source)
XLA Modules:
  0.0 266.3 jit_solution(11255854571309388471)
XLA Ops:
  0.6 6.5 %shard_map.55 = (bf16[512,896]{1,0:T(8,128)(2,1)}, bf16[896,512]{1,0:T(8,128)(2,1)}) custom-call(s32[4]{0:T(128)} %pad_add_fusion.place_ref.refs_0_, s32[1,512]{1,0:T(1,128)} %rows_ref.1, bf16[1024,896]{1,0:T(8,128)(2,1)} %bitcast.40, bf16[1024,896]{1,0:T(8,128)(2,1)} %bitcast.41), custom_call_target="tpu_custom_call" | custom-call | flops 1 | bytes 1 | tf_op jit(solution)/shard_map/pallas_call | solution.py:52
  8.3 11.8 %shard_map.56 = (bf16[256,6144]{1,0:T(8,128)(2,1)S(1)}, bf16[256,6144]{1,0:T(8,128)(2,1)}) custom-call(bf16[512,896]{1,0:T(8,128)(2,1)S(1)} %copy-done.1, bf16[896,8192]{1,0:T(8,128)(2,1)} %bitcast.17, bf16[896,8192]{1,0:T(8,128)(2,1)} %bitcast.18, bf16[896,8192]{1,0:T(8,128)(2,1)} %bitcast.19), custom_call_target="tpu_custom_call" | custom-call | flops 1 | bytes 1 | tf_op jit(solution)/shard_map/pallas_call | solution.py:129
  21.5 7.8 %shard_map.58 = (bf16[896,1024]{1,0:T(8,128)(2,1)S(1)}, bf16[896,1920]{1,0:T(8,128)(2,1)}, bf16[896,1920]{1,0:T(8,128)(2,1)}) custom-call(s32[4]{0:T(128)S(1)} %copy-done.3, bf16[896,512]{1,0:T(8,128)(2,1)S(1)} %copy-done, bf16[896,8192]{1,0:T(8,128)(2,1)} %bitcast.20, bf16[896,8192]{1,0:T(8,128)(2,1)} %bitcast.21, bf16[896,8192]{1,0:T(8,128)(2,1)} %bitcast.22, ...), custom_call_target="tpu_custom_call" | custom-call | flops 1 | bytes 1 | tf_op jit(solution)/shard_map/pallas_call | solution.py:100
  36.1 4.8 %all-to-all-start = ((bf16[4,64,6144]{2,1,0:T(8,128)(2,1)}), bf16[4,64,6144]{2,1,0:T(8,128)(2,1)}, u32[]{:S(2)}, u32[]{:S(2)}) async-start(bf16[4,64,6144]{2,1,0:T(8,128)(2,1)} %bitcast.39), calls=%async_computation | async-start | bytes 6291456 | tf_op jit(solution)/shard_map/all_to_all | solution.py:342
  42.2 6.5 %shard_map.57 = (bf16[256,2048]{1,0:T(8,128)(2,1)S(1)}, bf16[256,2048]{1,0:T(8,128)(2,1)S(1)}) custom-call(bf16[512,896]{1,0:T(8,128)(2,1)S(1)} %copy-done.2, bf16[896,8192]{1,0:T(8,128)(2,1)} %bitcast.26), custom_call_target="tpu_custom_call" | custom-call | flops 1 | bytes 1 | tf_op jit(solution)/shard_map/pallas_call | solution.py:129
  53.1 25.2 %all-to-all-done = bf16[4,64,6144]{2,1,0:T(8,128)(2,1)} async-done(((bf16[4,64,6144]{2,1,0:T(8,128)(2,1)}), bf16[4,64,6144]{2,1,0:T(8,128)(2,1)}, u32[]{:S(2)}, u32[]{:S(2)}) %all-to-all-start) | async-done | bytes 3145760 | tf_op jit(solution)/shard_map/all_to_all | solution.py:342
  78.3 3.5 %reduce_sum.24.refs_1_ = bf16[64,6144]{1,0:T(8,128)(2,1)} reduce(bf16[4,64,6144]{2,1,0:T(8,128)(2,1)} %all-to-all-done, bf16[]{:T(256)} %constant.19.clone.1), dimensions={0}, to_apply=%region_0.0 | reduce | flops 1179648 | bytes 3932162 | tf_op jit(solution)/shard_map/reduce_sum | solution.py:345
  85.5 4.2 %all-to-all-start.1 = ((bf16[4,64,2048]{2,1,0:T(8,128)(2,1)}), bf16[4,64,2048]{2,1,0:T(8,128)(2,1)}, u32[]{:S(2)}, u32[]{:S(2)}) async-start(bf16[4,64,2048]{2,1,0:T(8,128)(2,1)} %bitcast.8), calls=%async_computation.1 | async-start | bytes 2097152 | tf_op jit(solution)/shard_map/all_to_all | solution.py:342
  89.7 4.4 %shard_map.60 = (bf16[896,128]{1,0:T(8,128)(2,1)S(1)}, bf16[896,640]{1,0:T(8,128)(2,1)S(1)}, bf16[896,128]{1,0:T(8,128)(2,1)S(1)}, bf16[896,128]{1,0:T(8,128)(2,1)S(1)}, bf16[896,768]{1,0:T(8,128)(2,1)S(1)}) custom-call(s32[4]{0:T(128)S(1)} %copy-done.3, bf16[896,8192]{1,0:T(8,128)(2,1)} %bitcast.27, bf16[896,8192]{1,0:T(8,128)(2,1)} %bitcast.28, ...), custom_call_target="tpu_custom_call" | custom-call | flops 1 | bytes 1 | tf_op jit(solution)/shard_map/pallas_call | solution.py:100
  96.2 6.1 %collective-permute-done.3.refs_2_ = bf16[64,6144]{1,0:T(8,128)(2,1)} collective-permute-done((bf16[64,6144]{1,0:T(8,128)(2,1)}, bf16[64,6144]{1,0:T(8,128)(2,1)}, u32[]{:S(2)}, u32[]{:S(2)}) %collective-permute-start.3) | collective-permute-done | bytes 786464 | tf_op jit(solution)/shard_map/ppermute | solution.py:323
  108.8 3.3 %collective-permute-start.7 = (bf16[64,1536]{1,0:T(8,128)(2,1)}, bf16[64,1536]{1,0:T(8,128)(2,1)S(1)}, u32[]{:S(2)}, u32[]{:S(2)}) collective-permute-start(bf16[64,1536]{1,0:T(8,128)(2,1)} %get-tuple-element.98), channel_id=1, source_target_pairs={{0,32},{16,48},{32,0},{48,16},{1,33},{17,49},{33,1},{49,17},{2,34}... | collective-permute-start | bytes 589832 | tf_op jit(solution)/shard_map/ppermute | solution.py:323
  116.2 4.5 %collective-permute-done.7 = bf16[64,1536]{1,0:T(8,128)(2,1)S(1)} collective-permute-done((bf16[64,1536]{1,0:T(8,128)(2,1)}, bf16[64,1536]{1,0:T(8,128)(2,1)S(1)}, u32[]{:S(2)}, u32[]{:S(2)}) %collective-permute-start.7) | collective-permute-done | bytes 196640 | tf_op jit(solution)/shard_map/ppermute | solution.py:323
  123.6 4.7 %all-to-all-start.2 = ((bf16[4,4,64,1536]{3,2,1,0:T(8,128)(2,1)}), bf16[4,4,64,1536]{3,2,1,0:T(8,128)(2,1)}, u32[]{:S(2)}, u32[]{:S(2)}) async-start(bf16[4,4,64,1536]{3,2,1,0:T(8,128)(2,1)} %broadcast_in_dim.4), calls=%async_computation.2 | async-start | bytes 6291456 | tf_op jit(solution)/shard_map/all_to_all | solution.py:342
  139.0 19.4 %collective-permute-done.13.refs_2_ = bf16[64,2048]{1,0:T(8,128)(2,1)S(1)} collective-permute-done((bf16[64,2048]{1,0:T(8,128)(2,1)}, bf16[64,2048]{1,0:T(8,128)(2,1)S(1)}, u32[]{:S(2)}, u32[]{:S(2)}) %collective-permute-start.13) | collective-permute-done | bytes 262176 | tf_op jit(solution)/shard_map/ppermute | solution.py:323
  163.1 4.1 %collective-permute-done.14 = bf16[64,1024]{1,0:T(8,128)(2,1)S(1)} collective-permute-done((bf16[64,1024]{1,0:T(8,128)(2,1)S(1)}, bf16[64,1024]{1,0:T(8,128)(2,1)S(1)}, u32[]{:S(2)}, u32[]{:S(2)}) %collective-permute-start.14) | collective-permute-done | bytes 131104 | tf_op jit(solution)/shard_map/ppermute | solution.py:323
  167.9 4.0 %collective-permute-done.10.refs_5_ = bf16[896,256]{1,0:T(8,128)(2,1)S(1)} collective-permute-done((bf16[896,256]{1,0:T(8,128)(2,1)}, bf16[896,256]{1,0:T(8,128)(2,1)S(1)}, u32[]{:S(2)}, u32[]{:S(2)}) %collective-permute-start.10) | collective-permute-done | bytes 458784 | tf_op jit(solution)/shard_map/ppermute | solution.py:323
  178.0 4.1 %all-to-all-start.3 = ((bf16[4,2,64,1024]{3,2,1,0:T(8,128)(2,1)}), bf16[4,2,64,1024]{3,2,1,0:T(8,128)(2,1)S(1)}, u32[]{:S(2)}, u32[]{:S(2)}) async-start(bf16[4,2,64,1024]{3,2,1,0:T(8,128)(2,1)} %broadcast_in_dim.5), calls=%async_computation.3 | async-start | bytes 2097152 | tf_op jit(solution)/shard_map/all_to_all | solution.py:342
  182.1 10.2 %shard_map.64 = bf16[2,896,768]{2,1,0:T(8,128)(2,1)} custom-call(s32[4]{0:T(128)} %pad_add_fusion.place_ref.refs_0_, bf16[896,512]{1,0:T(8,128)(2,1)} %get-tuple-element.107.squares_ref.own_units.refs_1_, bf16[896,8192]{1,0:T(8,128)(2,1)} %bitcast.31, bf16[896,1920]{1,0:T(8,128)(2,1)} %collective-permute-done.4.refs_3_.refs_4_.refs_9_, ...), custom_call_target="tpu_custom_call" | custom-call | flops 1 | bytes 1 | tf_op jit(solution)/shard_map/pallas_call | solution.py:219
  196.7 5.4 %collective-permute-done.15.refs_11_ = bf16[896,640]{1,0:T(8,128)(2,1)} collective-permute-done((bf16[896,640]{1,0:T(8,128)(2,1)S(1)}, bf16[896,640]{1,0:T(8,128)(2,1)}, u32[]{:S(2)}, u32[]{:S(2)}) %collective-permute-start.15) | collective-permute-done | bytes 1146912 | tf_op jit(solution)/shard_map/ppermute | solution.py:323
  208.3 8.3 %shard_map.62 = (bf16[2,896,256]{2,1,0:T(8,128)(2,1)}, bf16[2,896,256]{2,1,0:T(8,128)(2,1)}, bf16[2,896,256]{2,1,0:T(8,128)(2,1)}, bf16[2,896,256]{2,1,0:T(8,128)(2,1)}) custom-call(s32[4]{0:T(128)} %pad_add_fusion.place_ref.refs_0_, bf16[896,512]{1,0:T(8,128)(2,1)} %get-tuple-element.107.squares_ref.own_units.refs_1_, ...), custom_call_target="tpu_custom_call" | custom-call | flops 1 | bytes 1 | tf_op jit(solution)/shard_map/pallas_call | solution.py:263
  221.7 10.0 %shard_map.63.refs_0_ = bf16[2,896,768]{2,1,0:T(8,128)(2,1)} custom-call(s32[4]{0:T(128)} %pad_add_fusion.place_ref.refs_0_, bf16[896,512]{1,0:T(8,128)(2,1)} %get-tuple-element.107.squares_ref.own_units.refs_1_, bf16[896,8192]{1,0:T(8,128)(2,1)} %bitcast.36, bf16[896,1920]{1,0:T(8,128)(2,1)} %collective-permute-done.4.refs_3_.refs_4_.refs_9_, ...), custom_call_target="tpu_custom_call" | custom-call | flops 1 | bytes 1 | tf_op jit(solution)/shard_map/pallas_call | solution.py:219
  231.7 21.5 %collective-permute-done.24.refs_1_ = bf16[2,896,768]{2,1,0:T(8,128)(2,1)} collective-permute-done((bf16[2,896,768]{2,1,0:T(8,128)(2,1)}, bf16[2,896,768]{2,1,0:T(8,128)(2,1)}, u32[]{:S(2)}, u32[]{:S(2)}) %collective-permute-start.24) | collective-permute-done | bytes 2752544 | tf_op jit(solution)/shard_map/ppermute | solution.py:323
  253.3 4.9 %shard_map.65.refs_4_ = f32[896,1024]{1,0:T(8,128)} custom-call(bf16[2,896,768]{2,1,0:T(8,128)(2,1)} %shard_map.63.refs_0_, bf16[2,896,768]{2,1,0:T(8,128)(2,1)} %collective-permute-done.24.refs_1_), custom_call_target="tpu_custom_call" | custom-call | flops 1 | bytes 1 | tf_op jit(solution)/shard_map/pallas_call | solution.py:301
  262.2 4.1 %shard_map.66 = f32[896,1024]{1,0:T(8,128)} custom-call(bf16[2,896,256]{2,1,0:T(8,128)(2,1)} %get-tuple-element.121.refs_0_, bf16[2,896,256]{2,1,0:T(8,128)(2,1)} %copy-done.16, bf16[2,896,256]{2,1,0:T(8,128)(2,1)} %copy-done.15, bf16[2,896,256]{2,1,0:T(8,128)(2,1)} %copy-done.17, f32[896,1024]{1,0:T(8,128)} %shard_map.65.refs_4_), custom_call_target="tpu_custom_call", output_to_operand_aliasing={{}: (4, {})} | custom-call | flops 1 | bytes 1 | tf_op jit(solution)/shard_map/pallas_call | solution.py:301
  (102 shorter events, 76.9 us)
Async XLA Ops:
  20.1 13.2 %collective-permute-start = (bf16[256,6144]{1,0:T(8,128)(2,1)}, bf16[256,6144]{1,0:T(8,128)(2,1)S(1)}, u32[]{:S(2)}, u32[]{:S(2)}) collective-permute-start(bf16[256,6144]{1,0:T(8,128)(2,1)} %get-tuple-element.76), channel_id=1, source_target_pairs={{0,1},{1,0},{2,3},{3,2},{4,5},{5,4},{6,7},{7,6},{8,9},{9,8},{10,11... | collective-permute-start | bytes 9437192 | tf_op jit(solution)/shard_map/ppermute | solution.py:323
  29.3 79.0 %collective-permute-start.4 = (bf16[896,1920]{1,0:T(8,128)(2,1)}, bf16[896,1920]{1,0:T(8,128)(2,1)}, u32[]{:S(2)}, u32[]{:S(2)}) collective-permute-start(bf16[896,1920]{1,0:T(8,128)(2,1)} %get-tuple-element.88), channel_id=1, source_target_pairs={{0,16},{16,32},{32,48},{48,0},{1,17},{17,33},{33,49},{49,1},{2,18}... | collective-permute-start | bytes 10321928 | tf_op jit(solution)/shard_map/ppermute | solution.py:323
  31.1 77.2 %collective-permute-start.5 = (bf16[896,1920]{1,0:T(8,128)(2,1)}, bf16[896,1920]{1,0:T(8,128)(2,1)}, u32[]{:S(2)}, u32[]{:S(2)}) collective-permute-start(bf16[896,1920]{1,0:T(8,128)(2,1)} %get-tuple-element.89), channel_id=1, source_target_pairs={{0,48},{16,0},{32,16},{48,32},{1,49},{17,1},{33,17},{49,33},{2,50}... | collective-permute-start | bytes 10321928 | tf_op jit(solution)/shard_map/ppermute | solution.py:323
  36.1 42.2 %all-to-all-start = ((bf16[4,64,6144]{2,1,0:T(8,128)(2,1)}), bf16[4,64,6144]{2,1,0:T(8,128)(2,1)}, u32[]{:S(2)}, u32[]{:S(2)}) async-start(bf16[4,64,6144]{2,1,0:T(8,128)(2,1)} %bitcast.39), calls=%async_computation | async-start | bytes 6291456 | tf_op jit(solution)/shard_map/all_to_all | solution.py:342
  40.9 41.7 %collective-permute-start.2 = (bf16[896,1024]{1,0:T(8,128)(2,1)}, bf16[896,1024]{1,0:T(8,128)(2,1)}, u32[]{:S(2)}, u32[]{:S(2)}) collective-permute-start(bf16[896,1024]{1,0:T(8,128)(2,1)} %copy-done.4), channel_id=1, source_target_pairs={{0,64},{64,0},{1,65},{65,1},{2,66},{66,2},{3,67},{67,3},{4,68},{68... | collective-permute-start | bytes 5505032 | tf_op jit(solution)/shard_map/ppermute | solution.py:323
  82.6 19.7 %collective-permute-start.3 = (bf16[64,6144]{1,0:T(8,128)(2,1)}, bf16[64,6144]{1,0:T(8,128)(2,1)}, u32[]{:S(2)}, u32[]{:S(2)}) collective-permute-start(bf16[64,6144]{1,0:T(8,128)(2,1)} %reduce_sum.24.refs_1_), channel_id=1, source_target_pairs={{0,8},{8,0},{1,9},{9,1},{2,10},{10,2},{3,11},{11,3},{4,12},{12,4},... | collective-permute-start | bytes 2359304 | tf_op jit(solution)/shard_map/ppermute | solution.py:323
  85.5 22.8 %all-to-all-start.1 = ((bf16[4,64,2048]{2,1,0:T(8,128)(2,1)}), bf16[4,64,2048]{2,1,0:T(8,128)(2,1)}, u32[]{:S(2)}, u32[]{:S(2)}) async-start(bf16[4,64,2048]{2,1,0:T(8,128)(2,1)} %bitcast.8), calls=%async_computation.1 | async-start | bytes 2097152 | tf_op jit(solution)/shard_map/all_to_all | solution.py:342
  108.8 11.9 %collective-permute-start.7 = (bf16[64,1536]{1,0:T(8,128)(2,1)}, bf16[64,1536]{1,0:T(8,128)(2,1)S(1)}, u32[]{:S(2)}, u32[]{:S(2)}) collective-permute-start(bf16[64,1536]{1,0:T(8,128)(2,1)} %get-tuple-element.98), channel_id=1, source_target_pairs={{0,32},{16,48},{32,0},{48,16},{1,33},{17,49},{33,1},{49,17},{2,34}... | collective-permute-start | bytes 589832 | tf_op jit(solution)/shard_map/ppermute | solution.py:323
  123.6 49.2 %all-to-all-start.2 = ((bf16[4,4,64,1536]{3,2,1,0:T(8,128)(2,1)}), bf16[4,4,64,1536]{3,2,1,0:T(8,128)(2,1)}, u32[]{:S(2)}, u32[]{:S(2)}) async-start(bf16[4,4,64,1536]{3,2,1,0:T(8,128)(2,1)} %broadcast_in_dim.4), calls=%async_computation.2 | async-start | bytes 6291456 | tf_op jit(solution)/shard_map/all_to_all | solution.py:342
  128.3 44.5 %collective-permute-start.9 = (bf16[896,768]{1,0:T(8,128)(2,1)S(1)}, bf16[896,768]{1,0:T(8,128)(2,1)}, u32[]{:S(2)}, u32[]{:S(2)}) collective-permute-start(bf16[896,768]{1,0:T(8,128)(2,1)S(1)} %get-tuple-element.104), channel_id=1, source_target_pairs={{0,32},{16,48},{32,0},{48,16},{1,33},{17,49},{33,1},{49,17},{2,34}... | collective-permute-start | bytes 4128776 | tf_op jit(solution)/shard_map/ppermute | solution.py:323
  130.2 41.6 %collective-permute-start.12 = (bf16[896,512]{1,0:T(8,128)(2,1)S(1)}, bf16[896,512]{1,0:T(8,128)(2,1)}, u32[]{:S(2)}, u32[]{:S(2)}) collective-permute-start(bf16[896,512]{1,0:T(8,128)(2,1)S(1)} %copy-done), channel_id=1, source_target_pairs={{0,64},{64,0},{1,65},{65,1},{2,66},{66,2},{3,67},{67,3},{4,68},{68... | collective-permute-start | bytes 2752520 | tf_op jit(solution)/shard_map/ppermute | solution.py:323
  133.7 24.7 %collective-permute-start.13 = (bf16[64,2048]{1,0:T(8,128)(2,1)}, bf16[64,2048]{1,0:T(8,128)(2,1)S(1)}, u32[]{:S(2)}, u32[]{:S(2)}) collective-permute-start(bf16[64,2048]{1,0:T(8,128)(2,1)} %reduce_sum.25.refs_1_), channel_id=1, source_target_pairs={{0,8},{8,0},{1,9},{9,1},{2,10},{10,2},{3,11},{11,3},{4,12},{12,4},... | collective-permute-start | bytes 786440 | tf_op jit(solution)/shard_map/ppermute | solution.py:323
  136.3 35.5 %collective-permute-start.10 = (bf16[896,256]{1,0:T(8,128)(2,1)}, bf16[896,256]{1,0:T(8,128)(2,1)S(1)}, u32[]{:S(2)}, u32[]{:S(2)}) collective-permute-start(bf16[896,256]{1,0:T(8,128)(2,1)} %slice.12), channel_id=1, source_target_pairs={{0,16},{16,32},{32,48},{48,0},{1,17},{17,33},{33,49},{49,1},{2,18}... | collective-permute-start | bytes 1376264 | tf_op jit(solution)/shard_map/ppermute | solution.py:323
  138.0 33.8 %collective-permute-start.11 = (bf16[896,256]{1,0:T(8,128)(2,1)}, bf16[896,256]{1,0:T(8,128)(2,1)S(1)}, u32[]{:S(2)}, u32[]{:S(2)}) collective-permute-start(bf16[896,256]{1,0:T(8,128)(2,1)} %slice.13), channel_id=1, source_target_pairs={{0,48},{16,0},{32,16},{48,32},{1,49},{17,1},{33,17},{49,33},{2,50}... | collective-permute-start | bytes 1376264 | tf_op jit(solution)/shard_map/ppermute | solution.py:323
  172.8 9.3 %collective-permute-start.23 = (bf16[4,4,64,1536]{3,2,1,0:T(8,128)(2,1)}, bf16[4,4,64,1536]{3,2,1,0:T(8,128)(2,1)}, u32[]{:S(2)}, u32[]{:S(2)}) collective-permute-start(bf16[4,4,64,1536]{3,2,1,0:T(8,128)(2,1)} %all-to-all-done.2.refs_15_.refs_12_), channel_id=1, source_target_pairs={{0,1},{1,0},{2,3},{3,2},{4,5},{5,4},{6,7},{7,6},{8,9},{9,8},{10,11... | collective-permute-start | bytes 9437192 | tf_op jit(solution)/shard_map/ppermute | solution.py:323
  173.7 28.4 %collective-permute-start.15 = (bf16[896,640]{1,0:T(8,128)(2,1)S(1)}, bf16[896,640]{1,0:T(8,128)(2,1)}, u32[]{:S(2)}, u32[]{:S(2)}) collective-permute-start(bf16[896,640]{1,0:T(8,128)(2,1)S(1)} %get-tuple-element.116), channel_id=1, source_target_pairs={{0,32},{16,48},{32,0},{48,16},{1,33},{17,49},{33,1},{49,17},{2,34}... | collective-permute-start | bytes 3440648 | tf_op jit(solution)/shard_map/ppermute | solution.py:323
  178.0 18.8 %all-to-all-start.3 = ((bf16[4,2,64,1024]{3,2,1,0:T(8,128)(2,1)}), bf16[4,2,64,1024]{3,2,1,0:T(8,128)(2,1)S(1)}, u32[]{:S(2)}, u32[]{:S(2)}) async-start(bf16[4,2,64,1024]{3,2,1,0:T(8,128)(2,1)} %broadcast_in_dim.5), calls=%async_computation.3 | async-start | bytes 2097152 | tf_op jit(solution)/shard_map/all_to_all | solution.py:342
  192.3 61.0 %collective-permute-start.24 = (bf16[2,896,768]{2,1,0:T(8,128)(2,1)}, bf16[2,896,768]{2,1,0:T(8,128)(2,1)}, u32[]{:S(2)}, u32[]{:S(2)}) collective-permute-start(bf16[2,896,768]{2,1,0:T(8,128)(2,1)} %shard_map.64), channel_id=1, source_target_pairs={{0,64},{64,0},{1,65},{65,1},{2,66},{66,2},{3,67},{67,3},{4,68},{68... | collective-permute-start | bytes 8257544 | tf_op jit(solution)/shard_map/ppermute | solution.py:323
  203.0 13.6 %collective-permute-start.18 = (bf16[896,128]{1,0:T(8,128)(2,1)S(1)}, bf16[896,128]{1,0:T(8,128)(2,1)S(1)}, u32[]{:S(2)}, u32[]{:S(2)}) collective-permute-start(bf16[896,128]{1,0:T(8,128)(2,1)S(1)} %copy-done.10), channel_id=1, source_target_pairs={{0,16},{16,32},{32,48},{48,0},{1,17},{17,33},{33,49},{49,1},{2,18}... | collective-permute-start | bytes 688136 | tf_op jit(solution)/shard_map/ppermute | solution.py:323
  204.6 12.7 %collective-permute-start.19 = (bf16[896,128]{1,0:T(8,128)(2,1)S(1)}, bf16[896,128]{1,0:T(8,128)(2,1)S(1)}, u32[]{:S(2)}, u32[]{:S(2)}) collective-permute-start(bf16[896,128]{1,0:T(8,128)(2,1)S(1)} %copy-done.8), channel_id=1, source_target_pairs={{0,32},{16,48},{32,0},{48,16},{1,33},{17,49},{33,1},{49,17},{2,34}... | collective-permute-start | bytes 688136 | tf_op jit(solution)/shard_map/ppermute | solution.py:323
  206.5 10.7 %collective-permute-start.20 = (bf16[896,128]{1,0:T(8,128)(2,1)S(1)}, bf16[896,128]{1,0:T(8,128)(2,1)S(1)}, u32[]{:S(2)}, u32[]{:S(2)}) collective-permute-start(bf16[896,128]{1,0:T(8,128)(2,1)S(1)} %copy-done.6), channel_id=1, source_target_pairs={{0,48},{16,0},{32,16},{48,32},{1,49},{17,1},{33,17},{49,33},{2,50}... | collective-permute-start | bytes 688136 | tf_op jit(solution)/shard_map/ppermute | solution.py:323
  217.2 40.9 %collective-permute-start.21 = (bf16[2,896,256]{2,1,0:T(8,128)(2,1)}, bf16[2,896,256]{2,1,0:T(8,128)(2,1)S(1)}, u32[]{:S(2)}, u32[]{:S(2)}) collective-permute-start(bf16[2,896,256]{2,1,0:T(8,128)(2,1)} %get-tuple-element.127), channel_id=1, source_target_pairs={{0,32},{16,48},{32,0},{48,16},{1,33},{17,49},{33,1},{49,17},{2,34}... | collective-permute-start | bytes 2752520 | tf_op jit(solution)/shard_map/ppermute | solution.py:323
  219.0 42.0 %collective-permute-start.17 = (bf16[2,896,256]{2,1,0:T(8,128)(2,1)}, bf16[2,896,256]{2,1,0:T(8,128)(2,1)S(1)}, u32[]{:S(2)}, u32[]{:S(2)}) collective-permute-start(bf16[2,896,256]{2,1,0:T(8,128)(2,1)} %get-tuple-element.122), channel_id=1, source_target_pairs={{0,16},{16,32},{32,48},{48,0},{1,17},{17,33},{33,49},{49,1},{2,18}... | collective-permute-start | bytes 2752520 | tf_op jit(solution)/shard_map/ppermute | solution.py:323
  220.2 40.7 %collective-permute-start.22 = (bf16[2,896,256]{2,1,0:T(8,128)(2,1)}, bf16[2,896,256]{2,1,0:T(8,128)(2,1)S(1)}, u32[]{:S(2)}, u32[]{:S(2)}) collective-permute-start(bf16[2,896,256]{2,1,0:T(8,128)(2,1)} %get-tuple-element.128), channel_id=1, source_target_pairs={{0,48},{16,0},{32,16},{48,32},{1,49},{17,1},{33,17},{49,33},{2,50}... | collective-permute-start | bytes 2752520 | tf_op jit(solution)/shard_map/ppermute | solution.py:323
  (27 other events, 172.2 us)

commit v7 on v6

--- a/solution.py
+++ b/solution.py
@@ -187,11 +187,10 @@
 def sums(units, weights, squares, number):
     numerator = denominator = None
     for k in range(number):
-        fisher = jnp.dot(units[k], squares(k), preferred_element_type=F32) * (1.0 / TOK)
-        weighted = (fisher * weights(k).astype(F32)).astype(BF).astype(F32)
-        term = fisher.astype(BF).astype(F32)
+        fisher = jnp.dot(units[k], squares(k), preferred_element_type=F32)
+        weighted = fisher * weights(k).astype(F32)
         numerator = weighted if numerator is None else numerator + weighted
-        denominator = term if denominator is None else denominator + term
+        denominator = fisher if denominator is None else denominator + fisher
     return numerator, denominator
 
 
@@ -213,24 +212,24 @@
     out_ref[1] = denominator.astype(out_ref.dtype)
 
 
-def set_p(place, squares, projection, moved, parts, dy, dtype, first=0, count=4):
+def set_p(place, squares, projection, moved, parts, dy, dtype):
     tall = 224
     pieces = [piece for group in moved for piece in group]
     return pl.pallas_call(
         lambda *refs: set_p_kernel([len(group) for group in moved], *refs),
         grid_spec=pltpu.PrefetchScalarGridSpec(
             num_scalar_prefetch=1,
-            grid=(count,),
+            grid=(UNITS // tall,),
             in_specs=[
-                pl.BlockSpec((tall, TOK), lambda u, s: (u + first, 0)),
-                pl.BlockSpec((tall, WIDE), lambda u, s: (u + first, lax.rem(s[0] + dy, 2) * 4 + s[1])),
+                pl.BlockSpec((tall, TOK), lambda u, s: (u, 0)),
+                pl.BlockSpec((tall, WIDE), lambda u, s: (u, lax.rem(s[0] + dy, 2) * 4 + s[1])),
             ]
-            + [pl.BlockSpec((tall, width), lambda u, s, i=i: (u + first, i)) for _, width, i in pieces]
+            + [pl.BlockSpec((tall, width), lambda u, s, i=i: (u, i)) for _, width, i in pieces]
             + [pl.BlockSpec((4, 4, 64, WP), lambda u, s: (0, 0, 0, dy))] * 2,
             out_specs=pl.BlockSpec((2, tall, WP), lambda u, s: (0, u, 0)),
             scratch_shapes=[pltpu.VMEM((4, TOK, WP), BF)],
         ),
-        out_shape=shape(2, count * tall, WP, dtype=dtype),
+        out_shape=shape(2, UNITS, WP, dtype=dtype),
         compiler_params=pltpu.CompilerParams(vmem_limit_bytes=VMEM),
         cost_estimate=SMALL,
     )(place, squares, projection, *[array for array, _, _ in pieces], *parts)
@@ -290,23 +289,19 @@
             value = value + ref[i].astype(F32)
         return value
 
-    out_ref[...] = total(0) / (total(1) + 1e-06)
-
-
-def quotient(columns, terms, before=None, first=0, count=4):
-    tall = 224
+    out_ref[...] = total(0) / (total(1) + TOK * 1e-06)
+
+
+def quotient(columns, terms, before=None, tall=224):
     width = columns.stop - columns.start
     place = columns.start // width
     given = [] if before is None else [before]
     return pl.pallas_call(
         lambda *refs: quotient_kernel(len(given), *refs),
-        grid=(count,),
-        in_specs=[
-            pl.BlockSpec((2, tall, width), lambda u, start=first * (term.shape[1] == UNITS): (0, u + start, 0))
-            for term in terms
-        ]
+        grid=(UNITS // tall,),
+        in_specs=[pl.BlockSpec((2, tall, width), lambda u: (0, u, 0))] * len(terms)
         + [pl.BlockSpec(memory_space=pl.ANY)] * len(given),
-        out_specs=pl.BlockSpec((tall, width), lambda u: (u + first, place)),
+        out_specs=pl.BlockSpec((tall, width), lambda u: (u, place)),
         out_shape=shape(UNITS, WIDE, dtype=F32),
         input_output_aliases={len(terms): 0} if given else {},
         compiler_params=pltpu.CompilerParams(vmem_limit_bytes=VMEM),
@@ -344,8 +339,8 @@
     def total(blocks):
         return jnp.sum(blocks.astype(F32), axis=0).astype(BF)
 
-    def gathered(part):
-        return over_x(jnp.broadcast_to(part[None], (4,) + part.shape))
+    def four(part):
+        return jnp.broadcast_to(part[None], (4,) + part.shape)
 
     pair_p, hidden = together((pair(own_p, other_p), hidden))
     blocks_p = over_x(pair_p)
@@ -375,7 +370,7 @@
 
     u_2 = (send(u_2[0], "z", 1), send(u_2[1], "z", 3))
     far_2, u_side = send(far_2, "z", 2), send(squares_late, "y_lo")
-    row_p = gathered(mine_p)
+    row_p = over_x(four(mine_p))
     squares_q = error_squares(
         place, total_q, far_q, targets[0], WP, WIDE, shape(2, 64, 4 * WQ),
         pl.BlockSpec((1, 64, 4 * WQ), lambda j, s: (lax.rem(j + s[0], 2), 0, 0)), put_q,
@@ -398,7 +393,7 @@
     early_2 = send(early_2, "z", 2)
     parts_p = [row_p, send(row_p, "core")]
     p_far = send(set_p(place, squares, projection, units + fars, parts_p, 1, BF), "y_lo")
-    row_q, early_2, late = together((gathered(mine_q), early_2, late))
+    row_q, early_2, late = together((over_x(four(mine_q)), early_2, late))
     late = [send(piece, "z", k + 1) for k, piece in enumerate(late)]
     parts_q = [row_q, send(row_q, "core")]
     q_sums = set_q(place, squares, u_side, projection, side, parts_q)
@@ -412,7 +407,7 @@
     ]
     p_own = set_p(place, squares, projection, units + nears, parts_p, 0, BF)
     merged = quotient(slice(0, WP), [p_own, p_far])
-    return quotient(slice(WP, WIDE), [q_own, *q_far], merged)
+    return quotient(slice(WP, WIDE), [q_own, *q_far], merged, 448)
 
 
 def solution(mesh):

time: 268 us -> 267 us (level)
  transfers between devices with their start and end apart: 29 -> 29, of which waited for: 14 -> 14; matrix products, arithmetic and copies ran while one was open for 6% -> 7% of each run, Pallas kernels for 22% -> 22%
where the time goes in v7:
time: 267 us; the launch traced here: 265 us
  waiting for transfers between devices  103 us (39%)
  Pallas kernels  78.5 us (29%)
  starting transfers between devices  55.1 us (21%)
  local copies, waits for them, and re-layouts  15.8 us (6%)
  other arithmetic  12.2 us (5%)
    ppermute x25, waiting for transfers between devices, send(): return lax.ppermute(value, axis, shift(k) if axis in ('z', 'x') else SWAP)  74.9 us
    ppermute x25, starting transfers between devices, send(): return lax.ppermute(value, axis, shift(k) if axis in ('z', 'x') else SWAP)  37.3 us
    all_to_all x4, waiting for transfers between devices, over_x(): return lax.all_to_all(blocks, 'x', 0, 0, tiled=True)  28.5 us
    pallas_call x2, Pallas kernels, set_p(): pl.pallas_call(lambda *refs: set_p_kernel([len(group) for group in moved]...  19.7 us
    pallas_call x2, Pallas kernels, partial_outputs(): pl.pallas_call(partial_kernel, grid=(8,), in_specs=[pl.BlockSpec((TOK, UN...  18.4 us
    all_to_all x4, starting transfers between devices, over_x(): return lax.all_to_all(blocks, 'x', 0, 0, tiled=True)  17.8 us
    pallas_call x2, Pallas kernels, cut(): pl.pallas_call(kernel, grid_spec=pltpu.PrefetchScalarGridSpec(num_scalar_...  12.1 us
    pallas_call x2, Pallas kernels, quotient(): pl.pallas_call(lambda *refs: quotient_kernel(len(given), *refs), grid=(UN...  7.89 us
  transfers between devices with their start and end apart: 29, of which 14 were waited for; matrix products, arithmetic and copies ran while one was open for 7% of the time, Pallas kernels for 22%

profile of v7, /device:TPU:1, one launch (start us, length us, event | category | flops | bytes accessed | tf_op | source)
XLA Modules:
  0.0 265.2 jit_solution(15117798681533445651)
XLA Ops:
  0.6 6.5 %shard_map.55 = (bf16[512,896]{1,0:T(8,128)(2,1)}, bf16[896,512]{1,0:T(8,128)(2,1)}) custom-call(s32[4]{0:T(128)} %pad_add_fusion.place_ref.refs_0_, s32[1,512]{1,0:T(1,128)} %rows_ref.1, bf16[1024,896]{1,0:T(8,128)(2,1)} %bitcast.40, bf16[1024,896]{1,0:T(8,128)(2,1)} %bitcast.41), custom_call_target="tpu_custom_call" | custom-call | flops 1 | bytes 1 | tf_op jit(solution)/shard_map/pallas_call | solution.py:52
  8.3 11.8 %shard_map.56 = (bf16[256,6144]{1,0:T(8,128)(2,1)S(1)}, bf16[256,6144]{1,0:T(8,128)(2,1)}) custom-call(bf16[512,896]{1,0:T(8,128)(2,1)S(1)} %copy-done.1, bf16[896,8192]{1,0:T(8,128)(2,1)} %bitcast.17, bf16[896,8192]{1,0:T(8,128)(2,1)} %bitcast.18, bf16[896,8192]{1,0:T(8,128)(2,1)} %bitcast.19), custom_call_target="tpu_custom_call" | custom-call | flops 1 | bytes 1 | tf_op jit(solution)/shard_map/pallas_call | solution.py:129
  21.5 7.8 %shard_map.58 = (bf16[896,1024]{1,0:T(8,128)(2,1)S(1)}, bf16[896,1920]{1,0:T(8,128)(2,1)}, bf16[896,1920]{1,0:T(8,128)(2,1)}) custom-call(s32[4]{0:T(128)S(1)} %copy-done.3, bf16[896,512]{1,0:T(8,128)(2,1)S(1)} %copy-done, bf16[896,8192]{1,0:T(8,128)(2,1)} %bitcast.20, bf16[896,8192]{1,0:T(8,128)(2,1)} %bitcast.21, bf16[896,8192]{1,0:T(8,128)(2,1)} %bitcast.22, ...), custom_call_target="tpu_custom_call" | custom-call | flops 1 | bytes 1 | tf_op jit(solution)/shard_map/pallas_call | solution.py:100
  36.1 4.8 %all-to-all-start = ((bf16[4,64,6144]{2,1,0:T(8,128)(2,1)}), bf16[4,64,6144]{2,1,0:T(8,128)(2,1)}, u32[]{:S(2)}, u32[]{:S(2)}) async-start(bf16[4,64,6144]{2,1,0:T(8,128)(2,1)} %bitcast.39), calls=%async_computation | async-start | bytes 6291456 | tf_op jit(solution)/shard_map/all_to_all | solution.py:337
  42.2 6.5 %shard_map.57 = (bf16[256,2048]{1,0:T(8,128)(2,1)S(1)}, bf16[256,2048]{1,0:T(8,128)(2,1)S(1)}) custom-call(bf16[512,896]{1,0:T(8,128)(2,1)S(1)} %copy-done.2, bf16[896,8192]{1,0:T(8,128)(2,1)} %bitcast.26), custom_call_target="tpu_custom_call" | custom-call | flops 1 | bytes 1 | tf_op jit(solution)/shard_map/pallas_call | solution.py:129
  53.1 25.2 %all-to-all-done = bf16[4,64,6144]{2,1,0:T(8,128)(2,1)} async-done(((bf16[4,64,6144]{2,1,0:T(8,128)(2,1)}), bf16[4,64,6144]{2,1,0:T(8,128)(2,1)}, u32[]{:S(2)}, u32[]{:S(2)}) %all-to-all-start) | async-done | bytes 3145760 | tf_op jit(solution)/shard_map/all_to_all | solution.py:337
  78.3 3.5 %reduce_sum.24.refs_1_ = bf16[64,6144]{1,0:T(8,128)(2,1)} reduce(bf16[4,64,6144]{2,1,0:T(8,128)(2,1)} %all-to-all-done, bf16[]{:T(256)} %constant.19.clone.1), dimensions={0}, to_apply=%region_0.0 | reduce | flops 1179648 | bytes 3932162 | tf_op jit(solution)/shard_map/reduce_sum | solution.py:340
  85.5 4.2 %all-to-all-start.1 = ((bf16[4,64,2048]{2,1,0:T(8,128)(2,1)}), bf16[4,64,2048]{2,1,0:T(8,128)(2,1)}, u32[]{:S(2)}, u32[]{:S(2)}) async-start(bf16[4,64,2048]{2,1,0:T(8,128)(2,1)} %bitcast.8), calls=%async_computation.1 | async-start | bytes 2097152 | tf_op jit(solution)/shard_map/all_to_all | solution.py:337
  89.7 4.4 %shard_map.60 = (bf16[896,128]{1,0:T(8,128)(2,1)S(1)}, bf16[896,640]{1,0:T(8,128)(2,1)S(1)}, bf16[896,128]{1,0:T(8,128)(2,1)S(1)}, bf16[896,128]{1,0:T(8,128)(2,1)S(1)}, bf16[896,768]{1,0:T(8,128)(2,1)S(1)}) custom-call(s32[4]{0:T(128)S(1)} %copy-done.3, bf16[896,8192]{1,0:T(8,128)(2,1)} %bitcast.27, bf16[896,8192]{1,0:T(8,128)(2,1)} %bitcast.28, ...), custom_call_target="tpu_custom_call" | custom-call | flops 1 | bytes 1 | tf_op jit(solution)/shard_map/pallas_call | solution.py:100
  96.2 6.1 %collective-permute-done.3.refs_2_ = bf16[64,6144]{1,0:T(8,128)(2,1)} collective-permute-done((bf16[64,6144]{1,0:T(8,128)(2,1)}, bf16[64,6144]{1,0:T(8,128)(2,1)}, u32[]{:S(2)}, u32[]{:S(2)}) %collective-permute-start.3) | collective-permute-done | bytes 786464 | tf_op jit(solution)/shard_map/ppermute | solution.py:318
  108.8 3.3 %collective-permute-start.7 = (bf16[64,1536]{1,0:T(8,128)(2,1)}, bf16[64,1536]{1,0:T(8,128)(2,1)S(1)}, u32[]{:S(2)}, u32[]{:S(2)}) collective-permute-start(bf16[64,1536]{1,0:T(8,128)(2,1)} %get-tuple-element.98), channel_id=1, source_target_pairs={{0,32},{16,48},{32,0},{48,16},{1,33},{17,49},{33,1},{49,17},{2,34}... | collective-permute-start | bytes 589832 | tf_op jit(solution)/shard_map/ppermute | solution.py:318
  116.2 4.5 %collective-permute-done.7 = bf16[64,1536]{1,0:T(8,128)(2,1)S(1)} collective-permute-done((bf16[64,1536]{1,0:T(8,128)(2,1)}, bf16[64,1536]{1,0:T(8,128)(2,1)S(1)}, u32[]{:S(2)}, u32[]{:S(2)}) %collective-permute-start.7) | collective-permute-done | bytes 196640 | tf_op jit(solution)/shard_map/ppermute | solution.py:318
  123.6 4.7 %all-to-all-start.2 = ((bf16[4,4,64,1536]{3,2,1,0:T(8,128)(2,1)}), bf16[4,4,64,1536]{3,2,1,0:T(8,128)(2,1)}, u32[]{:S(2)}, u32[]{:S(2)}) async-start(bf16[4,4,64,1536]{3,2,1,0:T(8,128)(2,1)} %broadcast_in_dim.4), calls=%async_computation.2 | async-start | bytes 6291456 | tf_op jit(solution)/shard_map/all_to_all | solution.py:337
  139.0 19.4 %collective-permute-done.13.refs_2_ = bf16[64,2048]{1,0:T(8,128)(2,1)S(1)} collective-permute-done((bf16[64,2048]{1,0:T(8,128)(2,1)}, bf16[64,2048]{1,0:T(8,128)(2,1)S(1)}, u32[]{:S(2)}, u32[]{:S(2)}) %collective-permute-start.13) | collective-permute-done | bytes 262176 | tf_op jit(solution)/shard_map/ppermute | solution.py:318
  163.1 4.1 %collective-permute-done.14 = bf16[64,1024]{1,0:T(8,128)(2,1)S(1)} collective-permute-done((bf16[64,1024]{1,0:T(8,128)(2,1)S(1)}, bf16[64,1024]{1,0:T(8,128)(2,1)S(1)}, u32[]{:S(2)}, u32[]{:S(2)}) %collective-permute-start.14) | collective-permute-done | bytes 131104 | tf_op jit(solution)/shard_map/ppermute | solution.py:318
  167.9 4.0 %collective-permute-done.10.refs_5_ = bf16[896,256]{1,0:T(8,128)(2,1)S(1)} collective-permute-done((bf16[896,256]{1,0:T(8,128)(2,1)}, bf16[896,256]{1,0:T(8,128)(2,1)S(1)}, u32[]{:S(2)}, u32[]{:S(2)}) %collective-permute-start.10) | collective-permute-done | bytes 458784 | tf_op jit(solution)/shard_map/ppermute | solution.py:318
  178.0 4.1 %all-to-all-start.3 = ((bf16[4,2,64,1024]{3,2,1,0:T(8,128)(2,1)}), bf16[4,2,64,1024]{3,2,1,0:T(8,128)(2,1)S(1)}, u32[]{:S(2)}, u32[]{:S(2)}) async-start(bf16[4,2,64,1024]{3,2,1,0:T(8,128)(2,1)} %broadcast_in_dim.5), calls=%async_computation.3 | async-start | bytes 2097152 | tf_op jit(solution)/shard_map/all_to_all | solution.py:337
  182.1 9.9 %shard_map.64 = bf16[2,896,768]{2,1,0:T(8,128)(2,1)} custom-call(s32[4]{0:T(128)} %pad_add_fusion.place_ref.refs_0_, bf16[896,512]{1,0:T(8,128)(2,1)} %get-tuple-element.107.squares_ref.own_units.refs_1_, bf16[896,8192]{1,0:T(8,128)(2,1)} %bitcast.31, bf16[896,1920]{1,0:T(8,128)(2,1)} %collective-permute-done.4.refs_3_.refs_4_.refs_9_, ...), custom_call_target="tpu_custom_call" | custom-call | flops 1 | bytes 1 | tf_op jit(solution)/shard_map/pallas_call | solution.py:218
  193.4 3.3 %all-to-all-done.3.refs_0_ = bf16[4,2,64,1024]{3,2,1,0:T(8,128)(2,1)S(1)} async-done(((bf16[4,2,64,1024]{3,2,1,0:T(8,128)(2,1)}), bf16[4,2,64,1024]{3,2,1,0:T(8,128)(2,1)S(1)}, u32[]{:S(2)}, u32[]{:S(2)}) %all-to-all-start.3) | async-done | bytes 1048608 | tf_op jit(solution)/shard_map/all_to_all | solution.py:337
  196.7 5.4 %collective-permute-done.15.refs_11_ = bf16[896,640]{1,0:T(8,128)(2,1)} collective-permute-done((bf16[896,640]{1,0:T(8,128)(2,1)S(1)}, bf16[896,640]{1,0:T(8,128)(2,1)}, u32[]{:S(2)}, u32[]{:S(2)}) %collective-permute-start.15) | collective-permute-done | bytes 1146912 | tf_op jit(solution)/shard_map/ppermute | solution.py:318
  208.3 7.8 %shard_map.62 = (bf16[2,896,256]{2,1,0:T(8,128)(2,1)}, bf16[2,896,256]{2,1,0:T(8,128)(2,1)}, bf16[2,896,256]{2,1,0:T(8,128)(2,1)}, bf16[2,896,256]{2,1,0:T(8,128)(2,1)}) custom-call(s32[4]{0:T(128)} %pad_add_fusion.place_ref.refs_0_, bf16[896,512]{1,0:T(8,128)(2,1)} %get-tuple-element.107.squares_ref.own_units.refs_1_, ...), custom_call_target="tpu_custom_call" | custom-call | flops 1 | bytes 1 | tf_op jit(solution)/shard_map/pallas_call | solution.py:262
  221.7 9.8 %shard_map.63.refs_0_ = bf16[2,896,768]{2,1,0:T(8,128)(2,1)} custom-call(s32[4]{0:T(128)} %pad_add_fusion.place_ref.refs_0_, bf16[896,512]{1,0:T(8,128)(2,1)} %get-tuple-element.107.squares_ref.own_units.refs_1_, bf16[896,8192]{1,0:T(8,128)(2,1)} %bitcast.36, bf16[896,1920]{1,0:T(8,128)(2,1)} %collective-permute-done.4.refs_3_.refs_4_.refs_9_, ...), custom_call_target="tpu_custom_call" | custom-call | flops 1 | bytes 1 | tf_op jit(solution)/shard_map/pallas_call | solution.py:218
  231.5 21.5 %collective-permute-done.24.refs_1_ = bf16[2,896,768]{2,1,0:T(8,128)(2,1)} collective-permute-done((bf16[2,896,768]{2,1,0:T(8,128)(2,1)}, bf16[2,896,768]{2,1,0:T(8,128)(2,1)}, u32[]{:S(2)}, u32[]{:S(2)}) %collective-permute-start.24) | collective-permute-done | bytes 2752544 | tf_op jit(solution)/shard_map/ppermute | solution.py:318
  253.0 4.9 %shard_map.65.refs_4_ = f32[896,1024]{1,0:T(8,128)} custom-call(bf16[2,896,768]{2,1,0:T(8,128)(2,1)} %shard_map.63.refs_0_, bf16[2,896,768]{2,1,0:T(8,128)(2,1)} %collective-permute-done.24.refs_1_), custom_call_target="tpu_custom_call" | custom-call | flops 1 | bytes 1 | tf_op jit(solution)/shard_map/pallas_call | solution.py:299
  (102 shorter events, 77.6 us)
Async XLA Ops:
  20.1 13.2 %collective-permute-start = (bf16[256,6144]{1,0:T(8,128)(2,1)}, bf16[256,6144]{1,0:T(8,128)(2,1)S(1)}, u32[]{:S(2)}, u32[]{:S(2)}) collective-permute-start(bf16[256,6144]{1,0:T(8,128)(2,1)} %get-tuple-element.76), channel_id=1, source_target_pairs={{0,1},{1,0},{2,3},{3,2},{4,5},{5,4},{6,7},{7,6},{8,9},{9,8},{10,11... | collective-permute-start | bytes 9437192 | tf_op jit(solution)/shard_map/ppermute | solution.py:318
  29.3 79.0 %collective-permute-start.4 = (bf16[896,1920]{1,0:T(8,128)(2,1)}, bf16[896,1920]{1,0:T(8,128)(2,1)}, u32[]{:S(2)}, u32[]{:S(2)}) collective-permute-start(bf16[896,1920]{1,0:T(8,128)(2,1)} %get-tuple-element.88), channel_id=1, source_target_pairs={{0,16},{16,32},{32,48},{48,0},{1,17},{17,33},{33,49},{49,1},{2,18}... | collective-permute-start | bytes 10321928 | tf_op jit(solution)/shard_map/ppermute | solution.py:318
  31.1 77.2 %collective-permute-start.5 = (bf16[896,1920]{1,0:T(8,128)(2,1)}, bf16[896,1920]{1,0:T(8,128)(2,1)}, u32[]{:S(2)}, u32[]{:S(2)}) collective-permute-start(bf16[896,1920]{1,0:T(8,128)(2,1)} %get-tuple-element.89), channel_id=1, source_target_pairs={{0,48},{16,0},{32,16},{48,32},{1,49},{17,1},{33,17},{49,33},{2,50}... | collective-permute-start | bytes 10321928 | tf_op jit(solution)/shard_map/ppermute | solution.py:318
  36.1 42.2 %all-to-all-start = ((bf16[4,64,6144]{2,1,0:T(8,128)(2,1)}), bf16[4,64,6144]{2,1,0:T(8,128)(2,1)}, u32[]{:S(2)}, u32[]{:S(2)}) async-start(bf16[4,64,6144]{2,1,0:T(8,128)(2,1)} %bitcast.39), calls=%async_computation | async-start | bytes 6291456 | tf_op jit(solution)/shard_map/all_to_all | solution.py:337
  40.9 41.7 %collective-permute-start.2 = (bf16[896,1024]{1,0:T(8,128)(2,1)}, bf16[896,1024]{1,0:T(8,128)(2,1)}, u32[]{:S(2)}, u32[]{:S(2)}) collective-permute-start(bf16[896,1024]{1,0:T(8,128)(2,1)} %copy-done.4), channel_id=1, source_target_pairs={{0,64},{64,0},{1,65},{65,1},{2,66},{66,2},{3,67},{67,3},{4,68},{68... | collective-permute-start | bytes 5505032 | tf_op jit(solution)/shard_map/ppermute | solution.py:318
  82.6 19.7 %collective-permute-start.3 = (bf16[64,6144]{1,0:T(8,128)(2,1)}, bf16[64,6144]{1,0:T(8,128)(2,1)}, u32[]{:S(2)}, u32[]{:S(2)}) collective-permute-start(bf16[64,6144]{1,0:T(8,128)(2,1)} %reduce_sum.24.refs_1_), channel_id=1, source_target_pairs={{0,8},{8,0},{1,9},{9,1},{2,10},{10,2},{3,11},{11,3},{4,12},{12,4},... | collective-permute-start | bytes 2359304 | tf_op jit(solution)/shard_map/ppermute | solution.py:318
  85.5 22.8 %all-to-all-start.1 = ((bf16[4,64,2048]{2,1,0:T(8,128)(2,1)}), bf16[4,64,2048]{2,1,0:T(8,128)(2,1)}, u32[]{:S(2)}, u32[]{:S(2)}) async-start(bf16[4,64,2048]{2,1,0:T(8,128)(2,1)} %bitcast.8), calls=%async_computation.1 | async-start | bytes 2097152 | tf_op jit(solution)/shard_map/all_to_all | solution.py:337
  108.8 11.9 %collective-permute-start.7 = (bf16[64,1536]{1,0:T(8,128)(2,1)}, bf16[64,1536]{1,0:T(8,128)(2,1)S(1)}, u32[]{:S(2)}, u32[]{:S(2)}) collective-permute-start(bf16[64,1536]{1,0:T(8,128)(2,1)} %get-tuple-element.98), channel_id=1, source_target_pairs={{0,32},{16,48},{32,0},{48,16},{1,33},{17,49},{33,1},{49,17},{2,34}... | collective-permute-start | bytes 589832 | tf_op jit(solution)/shard_map/ppermute | solution.py:318
  123.6 49.2 %all-to-all-start.2 = ((bf16[4,4,64,1536]{3,2,1,0:T(8,128)(2,1)}), bf16[4,4,64,1536]{3,2,1,0:T(8,128)(2,1)}, u32[]{:S(2)}, u32[]{:S(2)}) async-start(bf16[4,4,64,1536]{3,2,1,0:T(8,128)(2,1)} %broadcast_in_dim.4), calls=%async_computation.2 | async-start | bytes 6291456 | tf_op jit(solution)/shard_map/all_to_all | solution.py:337
  128.3 44.5 %collective-permute-start.9 = (bf16[896,768]{1,0:T(8,128)(2,1)S(1)}, bf16[896,768]{1,0:T(8,128)(2,1)}, u32[]{:S(2)}, u32[]{:S(2)}) collective-permute-start(bf16[896,768]{1,0:T(8,128)(2,1)S(1)} %get-tuple-element.104), channel_id=1, source_target_pairs={{0,32},{16,48},{32,0},{48,16},{1,33},{17,49},{33,1},{49,17},{2,34}... | collective-permute-start | bytes 4128776 | tf_op jit(solution)/shard_map/ppermute | solution.py:318
  130.2 41.6 %collective-permute-start.12 = (bf16[896,512]{1,0:T(8,128)(2,1)S(1)}, bf16[896,512]{1,0:T(8,128)(2,1)}, u32[]{:S(2)}, u32[]{:S(2)}) collective-permute-start(bf16[896,512]{1,0:T(8,128)(2,1)S(1)} %copy-done), channel_id=1, source_target_pairs={{0,64},{64,0},{1,65},{65,1},{2,66},{66,2},{3,67},{67,3},{4,68},{68... | collective-permute-start | bytes 2752520 | tf_op jit(solution)/shard_map/ppermute | solution.py:318
  133.7 24.7 %collective-permute-start.13 = (bf16[64,2048]{1,0:T(8,128)(2,1)}, bf16[64,2048]{1,0:T(8,128)(2,1)S(1)}, u32[]{:S(2)}, u32[]{:S(2)}) collective-permute-start(bf16[64,2048]{1,0:T(8,128)(2,1)} %reduce_sum.25.refs_1_), channel_id=1, source_target_pairs={{0,8},{8,0},{1,9},{9,1},{2,10},{10,2},{3,11},{11,3},{4,12},{12,4},... | collective-permute-start | bytes 786440 | tf_op jit(solution)/shard_map/ppermute | solution.py:318
  136.3 35.5 %collective-permute-start.10 = (bf16[896,256]{1,0:T(8,128)(2,1)}, bf16[896,256]{1,0:T(8,128)(2,1)S(1)}, u32[]{:S(2)}, u32[]{:S(2)}) collective-permute-start(bf16[896,256]{1,0:T(8,128)(2,1)} %slice.12), channel_id=1, source_target_pairs={{0,16},{16,32},{32,48},{48,0},{1,17},{17,33},{33,49},{49,1},{2,18}... | collective-permute-start | bytes 1376264 | tf_op jit(solution)/shard_map/ppermute | solution.py:318
  138.0 33.8 %collective-permute-start.11 = (bf16[896,256]{1,0:T(8,128)(2,1)}, bf16[896,256]{1,0:T(8,128)(2,1)S(1)}, u32[]{:S(2)}, u32[]{:S(2)}) collective-permute-start(bf16[896,256]{1,0:T(8,128)(2,1)} %slice.13), channel_id=1, source_target_pairs={{0,48},{16,0},{32,16},{48,32},{1,49},{17,1},{33,17},{49,33},{2,50}... | collective-permute-start | bytes 1376264 | tf_op jit(solution)/shard_map/ppermute | solution.py:318
  172.8 9.3 %collective-permute-start.23 = (bf16[4,4,64,1536]{3,2,1,0:T(8,128)(2,1)}, bf16[4,4,64,1536]{3,2,1,0:T(8,128)(2,1)}, u32[]{:S(2)}, u32[]{:S(2)}) collective-permute-start(bf16[4,4,64,1536]{3,2,1,0:T(8,128)(2,1)} %all-to-all-done.2.refs_15_.refs_12_), channel_id=1, source_target_pairs={{0,1},{1,0},{2,3},{3,2},{4,5},{5,4},{6,7},{7,6},{8,9},{9,8},{10,11... | collective-permute-start | bytes 9437192 | tf_op jit(solution)/shard_map/ppermute | solution.py:318
  173.7 28.4 %collective-permute-start.15 = (bf16[896,640]{1,0:T(8,128)(2,1)S(1)}, bf16[896,640]{1,0:T(8,128)(2,1)}, u32[]{:S(2)}, u32[]{:S(2)}) collective-permute-start(bf16[896,640]{1,0:T(8,128)(2,1)S(1)} %get-tuple-element.116), channel_id=1, source_target_pairs={{0,32},{16,48},{32,0},{48,16},{1,33},{17,49},{33,1},{49,17},{2,34}... | collective-permute-start | bytes 3440648 | tf_op jit(solution)/shard_map/ppermute | solution.py:318
  178.0 18.8 %all-to-all-start.3 = ((bf16[4,2,64,1024]{3,2,1,0:T(8,128)(2,1)}), bf16[4,2,64,1024]{3,2,1,0:T(8,128)(2,1)S(1)}, u32[]{:S(2)}, u32[]{:S(2)}) async-start(bf16[4,2,64,1024]{3,2,1,0:T(8,128)(2,1)} %broadcast_in_dim.5), calls=%async_computation.3 | async-start | bytes 2097152 | tf_op jit(solution)/shard_map/all_to_all | solution.py:337
  192.0 61.0 %collective-permute-start.24 = (bf16[2,896,768]{2,1,0:T(8,128)(2,1)}, bf16[2,896,768]{2,1,0:T(8,128)(2,1)}, u32[]{:S(2)}, u32[]{:S(2)}) collective-permute-start(bf16[2,896,768]{2,1,0:T(8,128)(2,1)} %shard_map.64), channel_id=1, source_target_pairs={{0,64},{64,0},{1,65},{65,1},{2,66},{66,2},{3,67},{67,3},{4,68},{68... | collective-permute-start | bytes 8257544 | tf_op jit(solution)/shard_map/ppermute | solution.py:318
  203.0 13.1 %collective-permute-start.18 = (bf16[896,128]{1,0:T(8,128)(2,1)S(1)}, bf16[896,128]{1,0:T(8,128)(2,1)S(1)}, u32[]{:S(2)}, u32[]{:S(2)}) collective-permute-start(bf16[896,128]{1,0:T(8,128)(2,1)S(1)} %copy-done.10), channel_id=1, source_target_pairs={{0,16},{16,32},{32,48},{48,0},{1,17},{17,33},{33,49},{49,1},{2,18}... | collective-permute-start | bytes 688136 | tf_op jit(solution)/shard_map/ppermute | solution.py:318
  204.6 12.7 %collective-permute-start.19 = (bf16[896,128]{1,0:T(8,128)(2,1)S(1)}, bf16[896,128]{1,0:T(8,128)(2,1)S(1)}, u32[]{:S(2)}, u32[]{:S(2)}) collective-permute-start(bf16[896,128]{1,0:T(8,128)(2,1)S(1)} %copy-done.8), channel_id=1, source_target_pairs={{0,32},{16,48},{32,0},{48,16},{1,33},{17,49},{33,1},{49,17},{2,34}... | collective-permute-start | bytes 688136 | tf_op jit(solution)/shard_map/ppermute | solution.py:318
  206.5 10.7 %collective-permute-start.20 = (bf16[896,128]{1,0:T(8,128)(2,1)S(1)}, bf16[896,128]{1,0:T(8,128)(2,1)S(1)}, u32[]{:S(2)}, u32[]{:S(2)}) collective-permute-start(bf16[896,128]{1,0:T(8,128)(2,1)S(1)} %copy-done.6), channel_id=1, source_target_pairs={{0,48},{16,0},{32,16},{48,32},{1,49},{17,1},{33,17},{49,33},{2,50}... | collective-permute-start | bytes 688136 | tf_op jit(solution)/shard_map/ppermute | solution.py:318
  217.2 40.7 %collective-permute-start.21 = (bf16[2,896,256]{2,1,0:T(8,128)(2,1)}, bf16[2,896,256]{2,1,0:T(8,128)(2,1)S(1)}, u32[]{:S(2)}, u32[]{:S(2)}) collective-permute-start(bf16[2,896,256]{2,1,0:T(8,128)(2,1)} %get-tuple-element.127), channel_id=1, source_target_pairs={{0,32},{16,48},{32,0},{48,16},{1,33},{17,49},{33,1},{49,17},{2,34}... | collective-permute-start | bytes 2752520 | tf_op jit(solution)/shard_map/ppermute | solution.py:318
  219.0 42.0 %collective-permute-start.17 = (bf16[2,896,256]{2,1,0:T(8,128)(2,1)}, bf16[2,896,256]{2,1,0:T(8,128)(2,1)S(1)}, u32[]{:S(2)}, u32[]{:S(2)}) collective-permute-start(bf16[2,896,256]{2,1,0:T(8,128)(2,1)} %get-tuple-element.122), channel_id=1, source_target_pairs={{0,16},{16,32},{32,48},{48,0},{1,17},{17,33},{33,49},{49,1},{2,18}... | collective-permute-start | bytes 2752520 | tf_op jit(solution)/shard_map/ppermute | solution.py:318
  220.2 40.7 %collective-permute-start.22 = (bf16[2,896,256]{2,1,0:T(8,128)(2,1)}, bf16[2,896,256]{2,1,0:T(8,128)(2,1)S(1)}, u32[]{:S(2)}, u32[]{:S(2)}) collective-permute-start(bf16[2,896,256]{2,1,0:T(8,128)(2,1)} %get-tuple-element.128), channel_id=1, source_target_pairs={{0,48},{16,0},{32,16},{48,32},{1,49},{17,1},{33,17},{49,33},{2,50}... | collective-permute-start | bytes 2752520 | tf_op jit(solution)/shard_map/ppermute | solution.py:318
  (27 other events, 172.9 us)

commit v8 on v7

--- a/solution.py
+++ b/solution.py
@@ -213,7 +213,7 @@
 
 
 def set_p(place, squares, projection, moved, parts, dy, dtype):
-    tall = 224
+    tall = 128
     pieces = [piece for group in moved for piece in group]
     return pl.pallas_call(
         lambda *refs: set_p_kernel([len(group) for group in moved], *refs),
@@ -254,7 +254,7 @@
 
 
 def set_q(place, units, far_units, projection, far, parts):
-    tall = 224
+    tall = 128
 
     def own(dz):
         return pl.BlockSpec((tall, WQ), lambda u, s: (u, (s[0] * 4 + lax.rem(s[1] + dz, 4)) * (WIDE // WQ) + WP // WQ))

time: 267 us -> 268 us (level)
  Pallas kernels: 78.5 us -> 83.1 us
  waiting for transfers between devices: 103 us -> 100 us
    pallas_call x2, Pallas kernels: 19.7 us -> 22.7 us  [set_p(): pl.pallas_call(lambda *refs: set_p_kernel([len(group) for group in moved]...]
  transfers between devices with their start and end apart: 29 -> 29, of which waited for: 14 -> 13; matrix products, arithmetic and copies ran while one was open for 7% -> 6% of each run, Pallas kernels for 22% -> 23%
where the time goes in v8:
time: 268 us; the launch traced here: 266 us
  waiting for transfers between devices  100 us (37%)
  Pallas kernels  83.1 us (31%)
  starting transfers between devices  54.5 us (20%)
  local copies, waits for them, and re-layouts  15.8 us (6%)
  other arithmetic  12.2 us (5%)
    ppermute x25, waiting for transfers between devices, send(): return lax.ppermute(value, axis, shift(k) if axis in ('z', 'x') else SWAP)  72.9 us
    ppermute x25, starting transfers between devices, send(): return lax.ppermute(value, axis, shift(k) if axis in ('z', 'x') else SWAP)  36.7 us
    all_to_all x4, waiting for transfers between devices, over_x(): return lax.all_to_all(blocks, 'x', 0, 0, tiled=True)  27.1 us
    pallas_call x2, Pallas kernels, set_p(): pl.pallas_call(lambda *refs: set_p_kernel([len(group) for group in moved]...  22.7 us
    pallas_call x2, Pallas kernels, partial_outputs(): pl.pallas_call(partial_kernel, grid=(8,), in_specs=[pl.BlockSpec((TOK, UN...  18.4 us
    all_to_all x4, starting transfers between devices, over_x(): return lax.all_to_all(blocks, 'x', 0, 0, tiled=True)  17.8 us
    pallas_call x2, Pallas kernels, cut(): pl.pallas_call(kernel, grid_spec=pltpu.PrefetchScalarGridSpec(num_scalar_...  12.1 us
    pallas_call x1, Pallas kernels, set_q(): pl.pallas_call(set_q_kernel, grid_spec=pltpu.PrefetchScalarGridSpec(num_s...  9.48 us
  transfers between devices with their start and end apart: 29, of which 13 were waited for; matrix products, arithmetic and copies ran while one was open for 6% of the time, Pallas kernels for 23%

profile of v8, /device:TPU:1, one launch (start us, length us, event | category | flops | bytes accessed | tf_op | source)
XLA Modules:
  0.0 265.8 jit_solution(4366827242127326278)
XLA Ops:
  0.6 6.5 %shard_map.55 = (bf16[512,896]{1,0:T(8,128)(2,1)}, bf16[896,512]{1,0:T(8,128)(2,1)}) custom-call(s32[4]{0:T(128)} %pad_add_fusion.place_ref.refs_0_, s32[1,512]{1,0:T(1,128)} %rows_ref.1, bf16[1024,896]{1,0:T(8,128)(2,1)} %bitcast.40, bf16[1024,896]{1,0:T(8,128)(2,1)} %bitcast.41), custom_call_target="tpu_custom_call" | custom-call | flops 1 | bytes 1 | tf_op jit(solution)/shard_map/pallas_call | solution.py:52
  8.3 11.8 %shard_map.56 = (bf16[256,6144]{1,0:T(8,128)(2,1)S(1)}, bf16[256,6144]{1,0:T(8,128)(2,1)}) custom-call(bf16[512,896]{1,0:T(8,128)(2,1)S(1)} %copy-done.1, bf16[896,8192]{1,0:T(8,128)(2,1)} %bitcast.17, bf16[896,8192]{1,0:T(8,128)(2,1)} %bitcast.18, bf16[896,8192]{1,0:T(8,128)(2,1)} %bitcast.19), custom_call_target="tpu_custom_call" | custom-call | flops 1 | bytes 1 | tf_op jit(solution)/shard_map/pallas_call | solution.py:129
  21.5 7.8 %shard_map.58 = (bf16[896,1024]{1,0:T(8,128)(2,1)S(1)}, bf16[896,1920]{1,0:T(8,128)(2,1)}, bf16[896,1920]{1,0:T(8,128)(2,1)}) custom-call(s32[4]{0:T(128)S(1)} %copy-done.3, bf16[896,512]{1,0:T(8,128)(2,1)S(1)} %copy-done, bf16[896,8192]{1,0:T(8,128)(2,1)} %bitcast.20, bf16[896,8192]{1,0:T(8,128)(2,1)} %bitcast.21, bf16[896,8192]{1,0:T(8,128)(2,1)} %bitcast.22, ...), custom_call_target="tpu_custom_call" | custom-call | flops 1 | bytes 1 | tf_op jit(solution)/shard_map/pallas_call | solution.py:100
  36.1 4.8 %all-to-all-start = ((bf16[4,64,6144]{2,1,0:T(8,128)(2,1)}), bf16[4,64,6144]{2,1,0:T(8,128)(2,1)}, u32[]{:S(2)}, u32[]{:S(2)}) async-start(bf16[4,64,6144]{2,1,0:T(8,128)(2,1)} %bitcast.39), calls=%async_computation | async-start | bytes 6291456 | tf_op jit(solution)/shard_map/all_to_all | solution.py:337
  42.2 6.5 %shard_map.57 = (bf16[256,2048]{1,0:T(8,128)(2,1)S(1)}, bf16[256,2048]{1,0:T(8,128)(2,1)S(1)}) custom-call(bf16[512,896]{1,0:T(8,128)(2,1)S(1)} %copy-done.2, bf16[896,8192]{1,0:T(8,128)(2,1)} %bitcast.26), custom_call_target="tpu_custom_call" | custom-call | flops 1 | bytes 1 | tf_op jit(solution)/shard_map/pallas_call | solution.py:129
  53.1 25.2 %all-to-all-done = bf16[4,64,6144]{2,1,0:T(8,128)(2,1)} async-done(((bf16[4,64,6144]{2,1,0:T(8,128)(2,1)}), bf16[4,64,6144]{2,1,0:T(8,128)(2,1)}, u32[]{:S(2)}, u32[]{:S(2)}) %all-to-all-start) | async-done | bytes 3145760 | tf_op jit(solution)/shard_map/all_to_all | solution.py:337
  78.3 3.5 %reduce_sum.24.refs_1_ = bf16[64,6144]{1,0:T(8,128)(2,1)} reduce(bf16[4,64,6144]{2,1,0:T(8,128)(2,1)} %all-to-all-done, bf16[]{:T(256)} %constant.19.clone.1), dimensions={0}, to_apply=%region_0.0 | reduce | flops 1179648 | bytes 3932162 | tf_op jit(solution)/shard_map/reduce_sum | solution.py:340
  85.5 4.2 %all-to-all-start.1 = ((bf16[4,64,2048]{2,1,0:T(8,128)(2,1)}), bf16[4,64,2048]{2,1,0:T(8,128)(2,1)}, u32[]{:S(2)}, u32[]{:S(2)}) async-start(bf16[4,64,2048]{2,1,0:T(8,128)(2,1)} %bitcast.8), calls=%async_computation.1 | async-start | bytes 2097152 | tf_op jit(solution)/shard_map/all_to_all | solution.py:337
  89.7 4.4 %shard_map.60 = (bf16[896,128]{1,0:T(8,128)(2,1)S(1)}, bf16[896,640]{1,0:T(8,128)(2,1)S(1)}, bf16[896,128]{1,0:T(8,128)(2,1)S(1)}, bf16[896,128]{1,0:T(8,128)(2,1)S(1)}, bf16[896,768]{1,0:T(8,128)(2,1)S(1)}) custom-call(s32[4]{0:T(128)S(1)} %copy-done.3, bf16[896,8192]{1,0:T(8,128)(2,1)} %bitcast.27, bf16[896,8192]{1,0:T(8,128)(2,1)} %bitcast.28, ...), custom_call_target="tpu_custom_call" | custom-call | flops 1 | bytes 1 | tf_op jit(solution)/shard_map/pallas_call | solution.py:100
  96.2 6.1 %collective-permute-done.3.refs_2_ = bf16[64,6144]{1,0:T(8,128)(2,1)} collective-permute-done((bf16[64,6144]{1,0:T(8,128)(2,1)}, bf16[64,6144]{1,0:T(8,128)(2,1)}, u32[]{:S(2)}, u32[]{:S(2)}) %collective-permute-start.3) | collective-permute-done | bytes 786464 | tf_op jit(solution)/shard_map/ppermute | solution.py:318
  102.3 3.3 %shard_map.59 = (bf16[64,1536]{1,0:T(8,128)(2,1)}, bf16[64,1536]{1,0:T(8,128)(2,1)}, bf16[64,1536]{1,0:T(8,128)(2,1)}, bf16[64,1536]{1,0:T(8,128)(2,1)}) custom-call(s32[4]{0:T(128)} %pad_add_fusion.place_ref.refs_0_, bf16[64,6144]{1,0:T(8,128)(2,1)} %reduce_sum.24.refs_1_, bf16[64,6144]{1,0:T(8,128)(2,1)} %collective-permute-done.3.refs_2_, ...), custom_call_target="tpu_custom_call" | custom-call | flops 1 | bytes 1 | tf_op jit(solution)/shard_map/pallas_call | solution.py:161
  108.8 3.3 %collective-permute-start.7 = (bf16[64,1536]{1,0:T(8,128)(2,1)}, bf16[64,1536]{1,0:T(8,128)(2,1)S(1)}, u32[]{:S(2)}, u32[]{:S(2)}) collective-permute-start(bf16[64,1536]{1,0:T(8,128)(2,1)} %get-tuple-element.98), channel_id=1, source_target_pairs={{0,32},{16,48},{32,0},{48,16},{1,33},{17,49},{33,1},{49,17},{2,34}... | collective-permute-start | bytes 589832 | tf_op jit(solution)/shard_map/ppermute | solution.py:318
  116.2 4.5 %collective-permute-done.7 = bf16[64,1536]{1,0:T(8,128)(2,1)S(1)} collective-permute-done((bf16[64,1536]{1,0:T(8,128)(2,1)}, bf16[64,1536]{1,0:T(8,128)(2,1)S(1)}, u32[]{:S(2)}, u32[]{:S(2)}) %collective-permute-start.7) | collective-permute-done | bytes 196640 | tf_op jit(solution)/shard_map/ppermute | solution.py:318
  123.6 4.7 %all-to-all-start.2 = ((bf16[4,4,64,1536]{3,2,1,0:T(8,128)(2,1)}), bf16[4,4,64,1536]{3,2,1,0:T(8,128)(2,1)}, u32[]{:S(2)}, u32[]{:S(2)}) async-start(bf16[4,4,64,1536]{3,2,1,0:T(8,128)(2,1)} %broadcast_in_dim.4), calls=%async_computation.2 | async-start | bytes 6291456 | tf_op jit(solution)/shard_map/all_to_all | solution.py:337
  139.0 19.4 %collective-permute-done.13.refs_2_ = bf16[64,2048]{1,0:T(8,128)(2,1)S(1)} collective-permute-done((bf16[64,2048]{1,0:T(8,128)(2,1)}, bf16[64,2048]{1,0:T(8,128)(2,1)S(1)}, u32[]{:S(2)}, u32[]{:S(2)}) %collective-permute-start.13) | collective-permute-done | bytes 262176 | tf_op jit(solution)/shard_map/ppermute | solution.py:318
  163.1 4.1 %collective-permute-done.14 = bf16[64,1024]{1,0:T(8,128)(2,1)S(1)} collective-permute-done((bf16[64,1024]{1,0:T(8,128)(2,1)S(1)}, bf16[64,1024]{1,0:T(8,128)(2,1)S(1)}, u32[]{:S(2)}, u32[]{:S(2)}) %collective-permute-start.14) | collective-permute-done | bytes 131104 | tf_op jit(solution)/shard_map/ppermute | solution.py:318
  167.9 4.0 %collective-permute-done.10.refs_5_ = bf16[896,256]{1,0:T(8,128)(2,1)S(1)} collective-permute-done((bf16[896,256]{1,0:T(8,128)(2,1)}, bf16[896,256]{1,0:T(8,128)(2,1)S(1)}, u32[]{:S(2)}, u32[]{:S(2)}) %collective-permute-start.10) | collective-permute-done | bytes 458784 | tf_op jit(solution)/shard_map/ppermute | solution.py:318
  178.0 4.1 %all-to-all-start.3 = ((bf16[4,2,64,1024]{3,2,1,0:T(8,128)(2,1)}), bf16[4,2,64,1024]{3,2,1,0:T(8,128)(2,1)S(1)}, u32[]{:S(2)}, u32[]{:S(2)}) async-start(bf16[4,2,64,1024]{3,2,1,0:T(8,128)(2,1)} %broadcast_in_dim.5), calls=%async_computation.3 | async-start | bytes 2097152 | tf_op jit(solution)/shard_map/all_to_all | solution.py:337
  182.1 11.4 %shard_map.64 = bf16[2,896,768]{2,1,0:T(8,128)(2,1)} custom-call(s32[4]{0:T(128)} %pad_add_fusion.place_ref.refs_0_, bf16[896,512]{1,0:T(8,128)(2,1)} %get-tuple-element.107.squares_ref.own_units.refs_1_, bf16[896,8192]{1,0:T(8,128)(2,1)} %bitcast.31, bf16[896,1920]{1,0:T(8,128)(2,1)} %collective-permute-done.4.refs_3_.refs_4_.refs_9_, ...), custom_call_target="tpu_custom_call" | custom-call | flops 1 | bytes 1 | tf_op jit(solution)/shard_map/pallas_call | solution.py:218
  196.7 5.4 %collective-permute-done.15.refs_11_ = bf16[896,640]{1,0:T(8,128)(2,1)} collective-permute-done((bf16[896,640]{1,0:T(8,128)(2,1)S(1)}, bf16[896,640]{1,0:T(8,128)(2,1)}, u32[]{:S(2)}, u32[]{:S(2)}) %collective-permute-start.15) | collective-permute-done | bytes 1146912 | tf_op jit(solution)/shard_map/ppermute | solution.py:318
  208.3 9.5 %shard_map.62 = (bf16[2,896,256]{2,1,0:T(8,128)(2,1)}, bf16[2,896,256]{2,1,0:T(8,128)(2,1)}, bf16[2,896,256]{2,1,0:T(8,128)(2,1)}, bf16[2,896,256]{2,1,0:T(8,128)(2,1)}) custom-call(s32[4]{0:T(128)} %pad_add_fusion.place_ref.refs_0_, bf16[896,512]{1,0:T(8,128)(2,1)} %get-tuple-element.107.squares_ref.own_units.refs_1_, ...), custom_call_target="tpu_custom_call" | custom-call | flops 1 | bytes 1 | tf_op jit(solution)/shard_map/pallas_call | solution.py:262
  221.7 11.3 %shard_map.63.refs_0_ = bf16[2,896,768]{2,1,0:T(8,128)(2,1)} custom-call(s32[4]{0:T(128)} %pad_add_fusion.place_ref.refs_0_, bf16[896,512]{1,0:T(8,128)(2,1)} %get-tuple-element.107.squares_ref.own_units.refs_1_, bf16[896,8192]{1,0:T(8,128)(2,1)} %bitcast.36, bf16[896,1920]{1,0:T(8,128)(2,1)} %collective-permute-done.4.refs_3_.refs_4_.refs_9_, ...), custom_call_target="tpu_custom_call" | custom-call | flops 1 | bytes 1 | tf_op jit(solution)/shard_map/pallas_call | solution.py:218
  232.9 21.6 %collective-permute-done.24.refs_1_ = bf16[2,896,768]{2,1,0:T(8,128)(2,1)} collective-permute-done((bf16[2,896,768]{2,1,0:T(8,128)(2,1)}, bf16[2,896,768]{2,1,0:T(8,128)(2,1)}, u32[]{:S(2)}, u32[]{:S(2)}) %collective-permute-start.24) | collective-permute-done | bytes 2752544 | tf_op jit(solution)/shard_map/ppermute | solution.py:318
  254.5 4.9 %shard_map.65.refs_4_ = f32[896,1024]{1,0:T(8,128)} custom-call(bf16[2,896,768]{2,1,0:T(8,128)(2,1)} %shard_map.63.refs_0_, bf16[2,896,768]{2,1,0:T(8,128)(2,1)} %collective-permute-done.24.refs_1_), custom_call_target="tpu_custom_call" | custom-call | flops 1 | bytes 1 | tf_op jit(solution)/shard_map/pallas_call | solution.py:299
  (102 shorter events, 73.6 us)
Async XLA Ops:
  20.1 13.2 %collective-permute-start = (bf16[256,6144]{1,0:T(8,128)(2,1)}, bf16[256,6144]{1,0:T(8,128)(2,1)S(1)}, u32[]{:S(2)}, u32[]{:S(2)}) collective-permute-start(bf16[256,6144]{1,0:T(8,128)(2,1)} %get-tuple-element.76), channel_id=1, source_target_pairs={{0,1},{1,0},{2,3},{3,2},{4,5},{5,4},{6,7},{7,6},{8,9},{9,8},{10,11... | collective-permute-start | bytes 9437192 | tf_op jit(solution)/shard_map/ppermute | solution.py:318
  29.3 79.0 %collective-permute-start.4 = (bf16[896,1920]{1,0:T(8,128)(2,1)}, bf16[896,1920]{1,0:T(8,128)(2,1)}, u32[]{:S(2)}, u32[]{:S(2)}) collective-permute-start(bf16[896,1920]{1,0:T(8,128)(2,1)} %get-tuple-element.88), channel_id=1, source_target_pairs={{0,16},{16,32},{32,48},{48,0},{1,17},{17,33},{33,49},{49,1},{2,18}... | collective-permute-start | bytes 10321928 | tf_op jit(solution)/shard_map/ppermute | solution.py:318
  31.1 77.2 %collective-permute-start.5 = (bf16[896,1920]{1,0:T(8,128)(2,1)}, bf16[896,1920]{1,0:T(8,128)(2,1)}, u32[]{:S(2)}, u32[]{:S(2)}) collective-permute-start(bf16[896,1920]{1,0:T(8,128)(2,1)} %get-tuple-element.89), channel_id=1, source_target_pairs={{0,48},{16,0},{32,16},{48,32},{1,49},{17,1},{33,17},{49,33},{2,50}... | collective-permute-start | bytes 10321928 | tf_op jit(solution)/shard_map/ppermute | solution.py:318
  36.1 42.2 %all-to-all-start = ((bf16[4,64,6144]{2,1,0:T(8,128)(2,1)}), bf16[4,64,6144]{2,1,0:T(8,128)(2,1)}, u32[]{:S(2)}, u32[]{:S(2)}) async-start(bf16[4,64,6144]{2,1,0:T(8,128)(2,1)} %bitcast.39), calls=%async_computation | async-start | bytes 6291456 | tf_op jit(solution)/shard_map/all_to_all | solution.py:337
  40.9 41.7 %collective-permute-start.2 = (bf16[896,1024]{1,0:T(8,128)(2,1)}, bf16[896,1024]{1,0:T(8,128)(2,1)}, u32[]{:S(2)}, u32[]{:S(2)}) collective-permute-start(bf16[896,1024]{1,0:T(8,128)(2,1)} %copy-done.4), channel_id=1, source_target_pairs={{0,64},{64,0},{1,65},{65,1},{2,66},{66,2},{3,67},{67,3},{4,68},{68... | collective-permute-start | bytes 5505032 | tf_op jit(solution)/shard_map/ppermute | solution.py:318
  82.6 19.7 %collective-permute-start.3 = (bf16[64,6144]{1,0:T(8,128)(2,1)}, bf16[64,6144]{1,0:T(8,128)(2,1)}, u32[]{:S(2)}, u32[]{:S(2)}) collective-permute-start(bf16[64,6144]{1,0:T(8,128)(2,1)} %reduce_sum.24.refs_1_), channel_id=1, source_target_pairs={{0,8},{8,0},{1,9},{9,1},{2,10},{10,2},{3,11},{11,3},{4,12},{12,4},... | collective-permute-start | bytes 2359304 | tf_op jit(solution)/shard_map/ppermute | solution.py:318
  85.5 22.8 %all-to-all-start.1 = ((bf16[4,64,2048]{2,1,0:T(8,128)(2,1)}), bf16[4,64,2048]{2,1,0:T(8,128)(2,1)}, u32[]{:S(2)}, u32[]{:S(2)}) async-start(bf16[4,64,2048]{2,1,0:T(8,128)(2,1)} %bitcast.8), calls=%async_computation.1 | async-start | bytes 2097152 | tf_op jit(solution)/shard_map/all_to_all | solution.py:337
  108.8 11.9 %collective-permute-start.7 = (bf16[64,1536]{1,0:T(8,128)(2,1)}, bf16[64,1536]{1,0:T(8,128)(2,1)S(1)}, u32[]{:S(2)}, u32[]{:S(2)}) collective-permute-start(bf16[64,1536]{1,0:T(8,128)(2,1)} %get-tuple-element.98), channel_id=1, source_target_pairs={{0,32},{16,48},{32,0},{48,16},{1,33},{17,49},{33,1},{49,17},{2,34}... | collective-permute-start | bytes 589832 | tf_op jit(solution)/shard_map/ppermute | solution.py:318
  123.6 49.2 %all-to-all-start.2 = ((bf16[4,4,64,1536]{3,2,1,0:T(8,128)(2,1)}), bf16[4,4,64,1536]{3,2,1,0:T(8,128)(2,1)}, u32[]{:S(2)}, u32[]{:S(2)}) async-start(bf16[4,4,64,1536]{3,2,1,0:T(8,128)(2,1)} %broadcast_in_dim.4), calls=%async_computation.2 | async-start | bytes 6291456 | tf_op jit(solution)/shard_map/all_to_all | solution.py:337
  128.3 44.5 %collective-permute-start.9 = (bf16[896,768]{1,0:T(8,128)(2,1)S(1)}, bf16[896,768]{1,0:T(8,128)(2,1)}, u32[]{:S(2)}, u32[]{:S(2)}) collective-permute-start(bf16[896,768]{1,0:T(8,128)(2,1)S(1)} %get-tuple-element.104), channel_id=1, source_target_pairs={{0,32},{16,48},{32,0},{48,16},{1,33},{17,49},{33,1},{49,17},{2,34}... | collective-permute-start | bytes 4128776 | tf_op jit(solution)/shard_map/ppermute | solution.py:318
  130.2 41.6 %collective-permute-start.12 = (bf16[896,512]{1,0:T(8,128)(2,1)S(1)}, bf16[896,512]{1,0:T(8,128)(2,1)}, u32[]{:S(2)}, u32[]{:S(2)}) collective-permute-start(bf16[896,512]{1,0:T(8,128)(2,1)S(1)} %copy-done), channel_id=1, source_target_pairs={{0,64},{64,0},{1,65},{65,1},{2,66},{66,2},{3,67},{67,3},{4,68},{68... | collective-permute-start | bytes 2752520 | tf_op jit(solution)/shard_map/ppermute | solution.py:318
  133.7 24.7 %collective-permute-start.13 = (bf16[64,2048]{1,0:T(8,128)(2,1)}, bf16[64,2048]{1,0:T(8,128)(2,1)S(1)}, u32[]{:S(2)}, u32[]{:S(2)}) collective-permute-start(bf16[64,2048]{1,0:T(8,128)(2,1)} %reduce_sum.25.refs_1_), channel_id=1, source_target_pairs={{0,8},{8,0},{1,9},{9,1},{2,10},{10,2},{3,11},{11,3},{4,12},{12,4},... | collective-permute-start | bytes 786440 | tf_op jit(solution)/shard_map/ppermute | solution.py:318
  136.3 35.5 %collective-permute-start.10 = (bf16[896,256]{1,0:T(8,128)(2,1)}, bf16[896,256]{1,0:T(8,128)(2,1)S(1)}, u32[]{:S(2)}, u32[]{:S(2)}) collective-permute-start(bf16[896,256]{1,0:T(8,128)(2,1)} %slice.12), channel_id=1, source_target_pairs={{0,16},{16,32},{32,48},{48,0},{1,17},{17,33},{33,49},{49,1},{2,18}... | collective-permute-start | bytes 1376264 | tf_op jit(solution)/shard_map/ppermute | solution.py:318
  138.0 33.8 %collective-permute-start.11 = (bf16[896,256]{1,0:T(8,128)(2,1)}, bf16[896,256]{1,0:T(8,128)(2,1)S(1)}, u32[]{:S(2)}, u32[]{:S(2)}) collective-permute-start(bf16[896,256]{1,0:T(8,128)(2,1)} %slice.13), channel_id=1, source_target_pairs={{0,48},{16,0},{32,16},{48,32},{1,49},{17,1},{33,17},{49,33},{2,50}... | collective-permute-start | bytes 1376264 | tf_op jit(solution)/shard_map/ppermute | solution.py:318
  172.8 9.3 %collective-permute-start.23 = (bf16[4,4,64,1536]{3,2,1,0:T(8,128)(2,1)}, bf16[4,4,64,1536]{3,2,1,0:T(8,128)(2,1)}, u32[]{:S(2)}, u32[]{:S(2)}) collective-permute-start(bf16[4,4,64,1536]{3,2,1,0:T(8,128)(2,1)} %all-to-all-done.2.refs_15_.refs_12_), channel_id=1, source_target_pairs={{0,1},{1,0},{2,3},{3,2},{4,5},{5,4},{6,7},{7,6},{8,9},{9,8},{10,11... | collective-permute-start | bytes 9437192 | tf_op jit(solution)/shard_map/ppermute | solution.py:318
  173.7 28.4 %collective-permute-start.15 = (bf16[896,640]{1,0:T(8,128)(2,1)S(1)}, bf16[896,640]{1,0:T(8,128)(2,1)}, u32[]{:S(2)}, u32[]{:S(2)}) collective-permute-start(bf16[896,640]{1,0:T(8,128)(2,1)S(1)} %get-tuple-element.116), channel_id=1, source_target_pairs={{0,32},{16,48},{32,0},{48,16},{1,33},{17,49},{33,1},{49,17},{2,34}... | collective-permute-start | bytes 3440648 | tf_op jit(solution)/shard_map/ppermute | solution.py:318
  178.0 18.8 %all-to-all-start.3 = ((bf16[4,2,64,1024]{3,2,1,0:T(8,128)(2,1)}), bf16[4,2,64,1024]{3,2,1,0:T(8,128)(2,1)S(1)}, u32[]{:S(2)}, u32[]{:S(2)}) async-start(bf16[4,2,64,1024]{3,2,1,0:T(8,128)(2,1)} %broadcast_in_dim.5), calls=%async_computation.3 | async-start | bytes 2097152 | tf_op jit(solution)/shard_map/all_to_all | solution.py:337
  193.5 61.0 %collective-permute-start.24 = (bf16[2,896,768]{2,1,0:T(8,128)(2,1)}, bf16[2,896,768]{2,1,0:T(8,128)(2,1)}, u32[]{:S(2)}, u32[]{:S(2)}) collective-permute-start(bf16[2,896,768]{2,1,0:T(8,128)(2,1)} %shard_map.64), channel_id=1, source_target_pairs={{0,64},{64,0},{1,65},{65,1},{2,66},{66,2},{3,67},{67,3},{4,68},{68... | collective-permute-start | bytes 8257544 | tf_op jit(solution)/shard_map/ppermute | solution.py:318
  203.0 14.8 %collective-permute-start.18 = (bf16[896,128]{1,0:T(8,128)(2,1)S(1)}, bf16[896,128]{1,0:T(8,128)(2,1)S(1)}, u32[]{:S(2)}, u32[]{:S(2)}) collective-permute-start(bf16[896,128]{1,0:T(8,128)(2,1)S(1)} %copy-done.10), channel_id=1, source_target_pairs={{0,16},{16,32},{32,48},{48,0},{1,17},{17,33},{33,49},{49,1},{2,18}... | collective-permute-start | bytes 688136 | tf_op jit(solution)/shard_map/ppermute | solution.py:318
  204.6 13.2 %collective-permute-start.19 = (bf16[896,128]{1,0:T(8,128)(2,1)S(1)}, bf16[896,128]{1,0:T(8,128)(2,1)S(1)}, u32[]{:S(2)}, u32[]{:S(2)}) collective-permute-start(bf16[896,128]{1,0:T(8,128)(2,1)S(1)} %copy-done.8), channel_id=1, source_target_pairs={{0,32},{16,48},{32,0},{48,16},{1,33},{17,49},{33,1},{49,17},{2,34}... | collective-permute-start | bytes 688136 | tf_op jit(solution)/shard_map/ppermute | solution.py:318
  206.5 11.3 %collective-permute-start.20 = (bf16[896,128]{1,0:T(8,128)(2,1)S(1)}, bf16[896,128]{1,0:T(8,128)(2,1)S(1)}, u32[]{:S(2)}, u32[]{:S(2)}) collective-permute-start(bf16[896,128]{1,0:T(8,128)(2,1)S(1)} %copy-done.6), channel_id=1, source_target_pairs={{0,48},{16,0},{32,16},{48,32},{1,49},{17,1},{33,17},{49,33},{2,50}... | collective-permute-start | bytes 688136 | tf_op jit(solution)/shard_map/ppermute | solution.py:318
  217.8 41.5 %collective-permute-start.21 = (bf16[2,896,256]{2,1,0:T(8,128)(2,1)}, bf16[2,896,256]{2,1,0:T(8,128)(2,1)S(1)}, u32[]{:S(2)}, u32[]{:S(2)}) collective-permute-start(bf16[2,896,256]{2,1,0:T(8,128)(2,1)} %get-tuple-element.127), channel_id=1, source_target_pairs={{0,32},{16,48},{32,0},{48,16},{1,33},{17,49},{33,1},{49,17},{2,34}... | collective-permute-start | bytes 2752520 | tf_op jit(solution)/shard_map/ppermute | solution.py:318
  219.0 42.6 %collective-permute-start.17 = (bf16[2,896,256]{2,1,0:T(8,128)(2,1)}, bf16[2,896,256]{2,1,0:T(8,128)(2,1)S(1)}, u32[]{:S(2)}, u32[]{:S(2)}) collective-permute-start(bf16[2,896,256]{2,1,0:T(8,128)(2,1)} %get-tuple-element.122), channel_id=1, source_target_pairs={{0,16},{16,32},{32,48},{48,0},{1,17},{17,33},{33,49},{49,1},{2,18}... | collective-permute-start | bytes 2752520 | tf_op jit(solution)/shard_map/ppermute | solution.py:318
  220.2 41.4 %collective-permute-start.22 = (bf16[2,896,256]{2,1,0:T(8,128)(2,1)}, bf16[2,896,256]{2,1,0:T(8,128)(2,1)S(1)}, u32[]{:S(2)}, u32[]{:S(2)}) collective-permute-start(bf16[2,896,256]{2,1,0:T(8,128)(2,1)} %get-tuple-element.128), channel_id=1, source_target_pairs={{0,48},{16,0},{32,16},{48,32},{1,49},{17,1},{33,17},{49,33},{2,50}... | collective-permute-start | bytes 2752520 | tf_op jit(solution)/shard_map/ppermute | solution.py:318
  (27 other events, 169.2 us)
